TPU v7x, 256 devices: a whole 4x4x8 slice. The times are simulated.
256 devices in a mesh: seq: 64 (over x, z, y_lo), dp: 4 (over y_hi, core).
Axes of the slice: x: 4, y: 4 (y_hi: 2, y_lo: 2; y = y_hi * 2 + y_lo), z: 8, core: 2. Of those that a mesh axis runs over, the one named last changes fastest.
Arguments:
- tokens: bfloat16 [4, 8192, 1536], P('dp', 'seq'), may hold values from -16 to 16
- upstream: bfloat16 [4, 8192, 1536], P('dp', 'seq'), may hold values from -6 to 6
- w_query: bfloat16 [1536, 512], replicated, may hold values from -10 to 10, as said below
- w_keyval: bfloat16 [1536, 256], replicated, may hold values from -1 to 1, as said below
- w_out: bfloat16 [512, 1536], replicated, may hold values from -0.25 to 0.25
Outputs:
- attended: bfloat16 [4, 8192, 1536], P('dp', 'seq')
- grad_tokens: bfloat16 [4, 8192, 1536], P('dp', 'seq')
- grad_query: float32 [1536, 512], P('seq')
- grad_keyval: float32 [1536, 256], P('seq')
- grad_out: float32 [512, 1536], P('seq')
Inputs may be any that keep to these rules, and one draw needn't show every extreme that they name: `w_query`: entries of order 1536 ** -0.5 times a modest factor. `w_keyval`: entries of order 1536 ** -0.5.
All inputs are finite; a program needn't handle non-finite values.
Results may differ from a plain program's by a relative error of at most 0.035.
The roundings to bfloat16 on the way count: a program that leaves them out, or rounds other values in their place, can miss the bound.
Values may be sent and summed in bfloat16 or wider, within the bound.
No kernel may reach another device: no remote copies, remote signals or barrier semaphores. Data moves between devices by JAX's collectives and lax.ppermute only.
A program may use at most 128 MiB of HBM per device.

v0:
```python
import jax
import jax.numpy as jnp
from jax import lax
from jax.sharding import PartitionSpec as P

HEADS = 4
HEAD_DIM = 128


def head_rows(matrix):
    count = matrix.shape[0]
    return matrix.reshape(count, HEADS, -1).transpose(1, 0, 2).reshape(HEADS * count, -1)


def token_rows(matrix):
    count = matrix.shape[0] // HEADS
    return matrix.reshape(HEADS, count, -1).transpose(1, 0, 2).reshape(count, -1)


def softmax_grads(qrows, drows, lse_rows, delta_rows, keys, values):
    scale = 1.0 / HEAD_DIM**0.5
    score = jnp.einsum("rd,kd->rk", qrows, keys, preferred_element_type=jnp.float32) * scale
    prob = jnp.exp(score - lse_rows[:, None])
    dprob = jnp.einsum("rd,kd->rk", drows, values, preferred_element_type=jnp.float32)
    dscore = (prob * (dprob - delta_rows[:, None]) * scale).astype(jnp.bfloat16)
    return (prob.astype(jnp.bfloat16), dscore)


def gather_keys(keyval):
    return lax.all_gather(keyval, "seq", axis=0, tiled=True)


def body(tokens, upstream, w_query, w_keyval, w_out):
    scale = 1.0 / HEAD_DIM**0.5
    local = tokens[0]
    cotangent = upstream[0]
    count = local.shape[0]
    query = jnp.dot(local, w_query, preferred_element_type=jnp.float32).astype(jnp.bfloat16)
    keyval = jnp.dot(local, w_keyval, preferred_element_type=jnp.float32).astype(jnp.bfloat16)
    qheads = head_rows(query)
    width = HEADS * count
    top = jnp.full((width,), -jnp.inf, jnp.float32)
    total = jnp.zeros((width,), jnp.float32)
    keys = lax.all_gather(keyval, "seq", axis=0, tiled=True)[:, :HEAD_DIM]
    score = jnp.einsum("rd,kd->rk", qheads, keys, preferred_element_type=jnp.float32) * scale
    new_top = jnp.max(score, axis=1)
    total = total * jnp.exp(top - new_top) + jnp.sum(jnp.exp(score - new_top[:, None]), axis=1)
    top, total = (new_top, total)
    kv_all = gather_keys(keyval)
    total_len = kv_all.shape[0]
    block = min(512, total_len)
    kv_blocks = kv_all.reshape(total_len // block, block, 2 * HEAD_DIM)
    logsum = top + jnp.log(total)

    def value_block(accum, kv_block):
        keys = kv_block[:, :HEAD_DIM]
        values = kv_block[:, HEAD_DIM:]
        score = jnp.einsum("rd,kd->rk", qheads, keys, preferred_element_type=jnp.float32) * scale
        prob = jnp.exp(score - logsum[:, None]).astype(jnp.bfloat16)
        return (accum + jnp.dot(prob, values, preferred_element_type=jnp.float32), None)

    accum, unused = lax.scan(value_block, jnp.zeros((width, HEAD_DIM), jnp.float32), kv_blocks)
    mixed_heads = accum.astype(jnp.bfloat16)
    mixed = token_rows(mixed_heads)
    attended = (
        local.astype(jnp.float32) + jnp.dot(mixed, w_out, preferred_element_type=jnp.float32)
    ).astype(jnp.bfloat16)
    dmixed = jnp.dot(cotangent, w_out.T, preferred_element_type=jnp.float32).astype(jnp.bfloat16)
    dheads = head_rows(dmixed)
    delta = jnp.sum(dheads.astype(jnp.float32) * mixed_heads.astype(jnp.float32), axis=1)

    def key_block(dq_acc, kv_block):
        keys = kv_block[:, :HEAD_DIM]
        values = kv_block[:, HEAD_DIM:]
        prob, dscore = softmax_grads(qheads, dheads, logsum, delta, keys, values)
        dq_acc = dq_acc + jnp.dot(dscore, keys, preferred_element_type=jnp.float32)
        dkey = jnp.einsum("rk,rd->kd", dscore, qheads, preferred_element_type=jnp.float32)
        dvalue = jnp.einsum("rk,rd->kd", prob, dheads, preferred_element_type=jnp.float32)
        return (dq_acc, jnp.concatenate([dkey, dvalue], axis=1))

    dq_heads, terms = lax.scan(key_block, jnp.zeros((width, HEAD_DIM), jnp.float32), kv_blocks)
    terms = terms.reshape(total_len, 2 * HEAD_DIM)
    dkeyval = lax.psum_scatter(terms, "seq", scatter_dimension=0, tiled=True).astype(jnp.bfloat16)
    dquery = token_rows(dq_heads.astype(jnp.bfloat16))
    grad_tokens = (
        jnp.dot(dquery, w_query.T, preferred_element_type=jnp.float32)
        + jnp.dot(dkeyval, w_keyval.T, preferred_element_type=jnp.float32)
    ).astype(jnp.bfloat16)
    term_q = jnp.einsum("nd,ne->de", local, dquery, preferred_element_type=jnp.float32)
    term_kv = jnp.einsum("nd,ne->de", local, dkeyval, preferred_element_type=jnp.float32)
    term_o = jnp.einsum("ne,nd->ed", mixed, cotangent, preferred_element_type=jnp.float32)
    shares = (
        lax.psum_scatter(term_q, "seq", scatter_dimension=0, tiled=True),
        lax.psum_scatter(term_kv, "seq", scatter_dimension=0, tiled=True),
        lax.psum_scatter(term_o, "seq", scatter_dimension=0, tiled=True),
    )
    grad_q, grad_kv, grad_o = (
        lax.psum(shares[0].astype(jnp.bfloat16), "dp").astype(jnp.float32),
        lax.psum(shares[1].astype(jnp.bfloat16), "dp").astype(jnp.float32),
        lax.psum(shares[2].astype(jnp.bfloat16), "dp").astype(jnp.float32),
    )
    return (attended[None], grad_tokens[None], grad_q, grad_kv, grad_o)


def solution(mesh):
    return jax.shard_map(
        body,
        mesh=mesh,
        in_specs=(P("dp", "seq", None), P("dp", "seq", None), P(), P(), P()),
        out_specs=(
            P("dp", "seq", None),
            P("dp", "seq", None),
            P("seq", None),
            P("seq", None),
            P("seq", None),
        ),
        check_vma=False,
    )
```

profile of v0, /device:TPU:1, one launch (start us, length us, event | category | flops | bytes accessed | tf_op | source)
XLA Modules:
  0.0 1776.3 jit_solution(13551815745535869873)
XLA Ops:
  7.3 2.3 convolution_convert_fusion.2
  9.7 2.3 convolution_convert_fusion
  17.1 257.1 %all-gather.2.cloned.1.call-done = bf16[8192,256]{1,0:T(8,128)(2,1)} async-done(((bf16[128,256]{1,0:T(8,128)(2,1)}), bf16[8192,256]{1,0:T(8,128)(2,1)}) %all-gather.2.cloned.1.call-update) | async-done | bytes 4194320 | tf_op jit(solution)/shard_map/all_gather | solution.py:30
  274.3 9.7 multiply_reduce_fusion
  283.9 8.7 exponential_reduce_fusion
  292.6 26.2 %while.24 = (s32[]{:T(128)}, f32[512,128]{1,0:T(8,128)S(1)}, bf16[16,512,256]{2,1,0:T(8,128)(2,1)}, bf16[512,128]{1,0:T(8,128)(2,1)S(1)}, f32[512]{0:T(512)S(1)}, /*index=5*/s32[]{:T(128)}, s32[]{:T(128)}) while((s32[]{:T(128)}, f32[512,128]{1,0:T(8,128)S(1)}, bf16[16,512,256]{2,1,0:T(8,128)(2,1)}, bf16[512,128]{1,0:T(8,128)(2,1)S(1)}, ...), condition=%wide.region_3.4_spmd.clone, body=%wide.region_2.3_spmd.clone.sunk | while | flops 135135232 | bytes 1443939 | solution.py:62
  320.4 112.9 %while.25 = (s32[]{:T(128)}, f32[512,128]{1,0:T(8,128)}, f32[16,512,256]{2,1,0:T(8,128)}, bf16[16,512,256]{2,1,0:T(8,128)(2,1)}, bf16[512,128]{1,0:T(8,128)(2,1)...) while((s32[]{:T(128)}, f32[512,128]{1,0:T(8,128)}, ...), condition=%wide.region_6.7_spmd.clone, body=%wide.region_5.6_spmd.clone.sunk | while | flops 337641472 | bytes 10358911 | solution.py:81
  343.3 2.0 convolution_add_fusion.4
  350.4 2.0 convolution_add_fusion.4
  371.7 2.0 convolution_add_fusion.4
  378.8 2.0 convolution_add_fusion.4
  400.2 2.0 convolution_add_fusion.4
  414.4 2.0 convolution_add_fusion.4
  421.6 2.0 convolution_add_fusion.4
  434.4 2.2 convolution_bitcast_fusion
  436.7 3.5 copy.33
  441.3 2.2 fusion.27
  443.6 315.0 %reduce-scatter.9.cloned.1.call-done = f32[128,256]{1,0:T(8,128)} async-done(((f32[8192,256]{1,0:T(8,128)}), f32[128,256]{1,0:T(8,128)}) %reduce-scatter.9.cloned.1.call-update) | async-done | bytes 131088 | tf_op jit(solution)/shard_map/reduce_scatter | solution.py:83
  761.5 2.2 fusion.24
  763.7 311.3 %reduce-scatter.13.cloned.1.call-done = f32[24,512]{1,0:T(8,128)} async-done(((f32[1536,512]{1,0:T(8,128)}), f32[24,512]{1,0:T(8,128)}) %reduce-scatter.13.cloned.1.call-update) | async-done | bytes 49168
  1075.9 314.3 %reduce-scatter.11.cloned.1.call-done = f32[8,1536]{1,0:T(8,128)} async-done(((f32[512,1536]{1,0:T(8,128)}), f32[8,1536]{1,0:T(8,128)}) %reduce-scatter.11.cloned.1.call-update) | async-done | bytes 49168 | tf_op jit(solution)/shard_map/reduce_scatter | solution.py:95
  1392.6 2.3 fusion.23
  1394.9 304.9 %reduce-scatter.15.cloned.1.call-done = f32[24,256]{1,0:T(8,128)} async-done(((f32[1536,256]{1,0:T(8,128)}), f32[24,256]{1,0:T(8,128)}) %reduce-scatter.15.cloned.1.call-update) | async-done | bytes 24592
  1700.7 67.0 %all-reduce = (bf16[24,512]{0,1:T(8,128)(2,1)S(1)}, bf16[24,256]{0,1:T(8,128)(2,1)S(1)}, bf16[8,1536]{1,0:T(8,128)(2,1)S(1)}) all-reduce(bf16[24,512]{0,1:T(8,128)(2,1)S(1)} %copy.34, bf16[24,256]{0,1:T(8,128)(2,1)S(1)} %copy.36, bf16[8,1536]{1,0:T(8,128)(2,1)S(1)} %convert_element_type.77), channel_id=1, replica_groups=mesh['seq'=64,'dp'=4] {'dp'}, use_global_device_ids=true, to_apply=%region_9.10 | all-reduce | flops 30720 | bytes 122880 | tf_op jit(solution)/shard_map/psum | solution.py:98
  (223 shorter events, 141.9 us)
Async XLA Ops:
  7.2 2.5 copy-start
  7.2 7.9 copy-start.1
  7.2 7.9 copy-start.4
  7.2 267.1 %all-gather.2.cloned.1.call-start = ((), (), s32[]{:S(2)}) async-start(), calls=%async_computation.4 | async-start | bytes 4259840 | tf_op jit(solution)/shard_map/all_gather | solution.py:30
  9.6 749.0 %reduce-scatter.9.cloned.1.call-start = ((), (), s32[]{:S(2)}) async-start(), calls=%async_computation.5 | async-start | bytes 8519680 | tf_op jit(solution)/shard_map/reduce_scatter | solution.py:83
  283.9 8.7 copy-start.10
  433.3 0.9 copy-start.3
  433.3 1.1 copy-start.2
  433.3 641.7 %reduce-scatter.13.cloned.1.call-start = ((), (), s32[]{:S(2)}) async-start(), calls=%async_computation.7 | async-start | bytes 3194880
  434.4 2.3 copy-start.7
  440.2 0.9 copy-start.9
  440.2 1.1 copy-start.6
  440.2 950.0 %reduce-scatter.11.cloned.1.call-start = ((), (), s32[]{:S(2)}) async-start(), calls=%async_computation.6 | async-start | bytes 3194880 | tf_op jit(solution)/shard_map/reduce_scatter | solution.py:95
  441.2 2.3 copy-start.8
  443.5 1256.4 %reduce-scatter.15.cloned.1.call-start = ((), (), s32[]{:S(2)}) async-start(), calls=%async_computation.8 | async-start | bytes 1597440
  761.5 631.1 %copy-start.5 = (bf16[1536,512]{1,0:T(8,128)(2,1)S(1)}, bf16[1536,512]{1,0:T(8,128)(2,1)}, u32[]{:S(2)}) copy-start(bf16[1536,512]{1,0:T(8,128)(2,1)} %param.11) | copy-start | bytes 4718596
Sparse Core Ops, SparseCore 0:
  9.8 264.3 all-gather.1
  433.4 325.0 reduce-scatter.8
  761.1 313.8 reduce-scatter.12
  1077.5 312.6 reduce-scatter.10
  1392.5 307.2 reduce-scatter.14
where the time goes:
time: 1780 us
  waiting for transfers between devices  1500 us (84%)
  matrix products  117 us (7%)
  blocking collectives  67 us (4%)
  local copies, waits for them, and re-layouts  62 us (3%)
    unnamed x7, waiting for transfers between devices  616 us
    reduce_scatter x1, waiting for transfers between devices, body(): lax.psum_scatter(terms, 'seq', scatter_dimension=0, tiled=True)  315 us
    reduce_scatter x1, waiting for transfers between devices, body(): lax.psum_scatter(term_o, 'seq', scatter_dimension=0, tiled=True)  314 us
    all_gather x1, waiting for transfers between devices, gather_keys(): return lax.all_gather(keyval, 'seq', axis=0, tiled=True)  257 us
    psum x1, blocking collectives, body(): lax.psum(shares[0].astype(jnp.bfloat16), 'dp').astype(jnp.float32)  67 us
  transfers between devices with their start and end apart: 5, of which 5 were waited for; matrix products, arithmetic and copies ran while one was open for 1% of the time, Pallas kernels for 0%

commit v1 on v0

v1 whole, which is shorter than its diff:
```python
import math

import jax
import jax.numpy as jnp
from jax import lax
from jax.experimental import pallas as pl
from jax.experimental.pallas import tpu as pltpu
from jax.sharding import Mesh, PartitionSpec as P

HEADS = 4
HEAD_DIM = 128
POS = 128
ROWS = HEADS * POS
GROUP = 8
KEYS = 8 * POS
FORWARD_CHUNK = 512
BACKWARD_CHUNK = 128
SCALE = 1.0 / HEAD_DIM**0.5
LOG2E = math.log2(math.e)
AXES = ("x", "z", "yl", "yh", "core")
SEQ = ("x", "z", "yl")
DP = ("yh", "core")
NT = (((1,), (1,)), ((), ()))
TN = (((0,), (0,)), ((), ()))
F32 = jnp.float32
BF16 = jnp.bfloat16
VMEM_LIMIT = 56 * 1024 * 1024


def dot(a, b, dims=(((1,), (0,)), ((), ()))):
    return lax.dot_general(a, b, dims, preferred_element_type=F32)


def send(array, axis, size, step):
    return lax.ppermute(array, axis, [(i, (i + step) % size) for i in range(size)])


def rows_of(block):
    return jnp.concatenate(
        [block[:, h * HEAD_DIM : (h + 1) * HEAD_DIM] for h in range(HEADS)], axis=0
    )


def forward_kernel(qd, *refs):
    mixed, stats_ref, kv, vt, score = refs[8:]
    for i in range(8):
        kv[i * POS : (i + 1) * POS, :] = refs[i][...]
    vt[...] = kv[:, HEAD_DIM:].T

    def block(p, carry):
        both = qd[p]
        q4 = rows_of(both[:, :ROWS])
        d4 = rows_of(both[:, ROWS:])
        top = jnp.full((1, ROWS), -jnp.inf, F32)
        for c in range(KEYS // FORWARD_CHUNK):
            part = slice(c * FORWARD_CHUNK, (c + 1) * FORWARD_CHUNK)
            s = dot(kv[part, :HEAD_DIM], q4, NT)
            score[part, :] = s
            top = jnp.maximum(top, jnp.max(s, axis=0, keepdims=True))
        base = top * (SCALE * LOG2E)
        total = jnp.zeros((1, ROWS), F32)
        weighted = jnp.zeros((1, ROWS), F32)
        acc = jnp.zeros((HEAD_DIM, ROWS), F32)
        for c in range(KEYS // FORWARD_CHUNK):
            part = slice(c * FORWARD_CHUNK, (c + 1) * FORWARD_CHUNK)
            e = jnp.exp2(score[part, :] * (SCALE * LOG2E) - base)
            dp = dot(kv[part, HEAD_DIM:], d4, NT)
            total = total + jnp.sum(e, axis=0, keepdims=True)
            weighted = weighted + jnp.sum(e * dp, axis=0, keepdims=True)
            acc = acc + dot(vt[:, part], e.astype(BF16))
        inverse = 1.0 / total
        mixed[p] = (acc * inverse).astype(BF16)
        stats_ref[pl.ds(p, 1), :] = top * SCALE + jnp.log(total)
        stats_ref[pl.ds(8 + p, 1), :] = weighted * inverse
        return carry

    lax.fori_loop(0, GROUP, block, 0)


def combine(logs, bars):
    top = jnp.max(logs, axis=0)
    weights = jnp.exp(logs - top)
    total = jnp.sum(weights, axis=0)
    weights = weights / total
    return top + jnp.log(total), jnp.sum(weights * bars, axis=0), weights


def backward_kernel(qd, stats_ref, *refs):
    dq, dkv_out = refs[8], refs[9:17]
    kv, kt, stat, dkv = refs[17:]
    for i in range(8):
        kv[i * POS : (i + 1) * POS, :] = refs[i][...]
    kt[...] = kv[:, :HEAD_DIM].T
    logsum, delta, unused = combine(stats_ref[:, :8, :], stats_ref[:, 8:, :])
    stat[:8, :] = logsum * LOG2E
    stat[8:, :] = delta
    dkv[...] = jnp.zeros_like(dkv)

    def block(p, carry):
        both = qd[p]
        q4 = rows_of(both[:, :ROWS])
        d4 = rows_of(both[:, ROWS:])
        base = stat[pl.ds(p, 1), :]
        delta = stat[pl.ds(8 + p, 1), :]
        acc = jnp.zeros((HEAD_DIM, ROWS), F32)
        for c in range(KEYS // BACKWARD_CHUNK):
            part = slice(c * BACKWARD_CHUNK, (c + 1) * BACKWARD_CHUNK)
            s = dot(kv[part, :HEAD_DIM], q4, NT)
            prob = jnp.exp2(s * (SCALE * LOG2E) - base)
            dp = dot(kv[part, HEAD_DIM:], d4, NT)
            ds = (prob * (dp - delta)).astype(BF16)
            dkv[part, HEAD_DIM:] += dot(prob.astype(BF16), d4)
            dkv[part, :HEAD_DIM] += dot(ds, q4)
            acc = acc + dot(kt[:, part], ds)
        dq[p] = (acc * SCALE).astype(BF16)
        return carry

    lax.fori_loop(0, GROUP, block, 0)
    for i in range(8):
        part = slice(i * POS, (i + 1) * POS)
        dkv_out[i][:, :HEAD_DIM] = (dkv[part, :HEAD_DIM] * SCALE).astype(BF16)
        dkv_out[i][:, HEAD_DIM:] = dkv[part, HEAD_DIM:].astype(BF16)


def output_kernel(place, parts, stats_ref, tokens_ref, upstream_ref, w_out_ref, *outs):
    attended_ref, keep_ref, give_ref = outs
    mine = place[1]
    unused, unused, weights = combine(
        stats_ref[:, pl.ds(mine, 1), :], stats_ref[:, pl.ds(8 + mine, 1), :]
    )
    mixed_t = jnp.sum(weights * parts[...].astype(F32), axis=0)
    heads_t = [mixed_t[:, h * POS : (h + 1) * POS] for h in range(HEADS)]
    mixed = jnp.concatenate([m.T for m in heads_t], axis=1).astype(BF16)
    mixed_rows = jnp.concatenate(heads_t, axis=0).astype(BF16)
    attended_ref[...] = (
        tokens_ref[...].astype(F32) + dot(mixed, w_out_ref[...])
    ).astype(BF16)
    half = upstream_ref.shape[1] // 2
    first = place[0] == 0
    low, high = upstream_ref[:, :half], upstream_ref[:, half:]
    keep_ref[...] = dot(mixed_rows, jnp.where(first, low, high)).astype(BF16)
    give_ref[...] = dot(mixed_rows, jnp.where(first, high, low)).astype(BF16)


def input_kernel(place, dq_ref, *refs):
    dkv_refs = refs[:8]
    tokens_ref, w_query_ref, w_keyval_ref, grad_ref, keep_ref, give_ref = refs[8:]
    dq_t = jnp.sum(dq_ref[...].astype(F32), axis=0)
    dquery = jnp.concatenate(
        [dq_t[:, h * POS : (h + 1) * POS].T for h in range(HEADS)], axis=1
    ).astype(BF16)
    dkeyval = sum(ref[...].astype(F32) for ref in dkv_refs).astype(BF16)
    grad_ref[...] = (
        dot(dquery, w_query_ref[...], NT) + dot(dkeyval, w_keyval_ref[...], NT)
    ).astype(BF16)
    first = place[0] == 0
    q_low, q_high = dquery[:, :256], dquery[:, 256:]
    kv_low, kv_high = dkeyval[:, :128], dkeyval[:, 128:]
    low = jnp.concatenate([q_low, kv_low], axis=1)
    high = jnp.concatenate([q_high, kv_high], axis=1)
    keep_ref[...] = dot(tokens_ref[...], jnp.where(first, low, high), TN).astype(BF16)
    give_ref[...] = dot(tokens_ref[...], jnp.where(first, high, low), TN).astype(BF16)


VM = pl.BlockSpec(memory_space=pltpu.VMEM)
SM = pl.BlockSpec(memory_space=pltpu.SMEM)


def call(kernel, ins, outs, in_specs, out_specs, scratch, flops):
    return pl.pallas_call(
        kernel,
        out_shape=outs,
        in_specs=in_specs,
        out_specs=out_specs,
        scratch_shapes=scratch,
        compiler_params=pltpu.CompilerParams(vmem_limit_bytes=VMEM_LIMIT),
        cost_estimate=pl.CostEstimate(flops=flops, bytes_accessed=6_000_000, transcendentals=0),
    )(*ins)


def shape(*dims, dtype=BF16):
    return jax.ShapeDtypeStruct(dims, dtype)


def swap(blocks, axes):
    return lax.all_to_all(blocks, axes, 0, 0)


def share(array, axes, count):
    return swap(jnp.broadcast_to(array[None], (count,) + array.shape), axes)


def added(blocks):
    return jnp.sum(blocks.astype(F32), axis=0)


def plus(a, b):
    return (a.astype(F32) + b.astype(F32)).astype(BF16)


def body(tokens, upstream, w_query, w_keyval, w_out):
    local = tokens[0]
    cotangent = upstream[0]
    core = lax.axis_index("core")
    group = lax.axis_index("x") * 2 + lax.axis_index("yl")
    place = jnp.stack([core, group]).astype(jnp.int32)
    query = jnp.dot(local, w_query, preferred_element_type=F32).astype(BF16)
    dmixed = jnp.dot(cotangent, w_out.T, preferred_element_type=F32).astype(BF16)
    qd = jnp.concatenate([query, dmixed], axis=1)
    qds = share(qd, ("x", "yl"), 8)
    qd, early = lax.optimization_barrier((qd, local))
    keyval = jnp.dot(early, w_keyval, preferred_element_type=F32).astype(BF16)
    kvs = [keyval] + [send(keyval, "z", 8, d) for d in range(1, 8)]

    mixed_parts, stats = call(
        forward_kernel,
        [qds, *kvs],
        [shape(8, HEAD_DIM, ROWS), shape(16, ROWS, dtype=F32)],
        [VM] * 9,
        [VM] * 2,
        [
            pltpu.VMEM((KEYS, 2 * HEAD_DIM), BF16),
            pltpu.VMEM((HEAD_DIM, KEYS), BF16),
            pltpu.VMEM((KEYS, ROWS), F32),
        ],
        10_000_000_000,
    )
    all_stats = share(stats, ("x", "yl"), 8)
    mixed_parts, all_stats = lax.optimization_barrier((mixed_parts, all_stats))
    mine = swap(mixed_parts, ("x", "yl"))
    dq_parts, *dkv_parts = call(
        backward_kernel,
        [qds, all_stats, *kvs],
        [shape(8, HEAD_DIM, ROWS)] + [shape(POS, 2 * HEAD_DIM)] * 8,
        [VM] * 10,
        [VM] * 9,
        [
            pltpu.VMEM((KEYS, 2 * HEAD_DIM), BF16),
            pltpu.VMEM((HEAD_DIM, KEYS), BF16),
            pltpu.VMEM((16, ROWS), F32),
            pltpu.VMEM((KEYS, 2 * HEAD_DIM), F32),
        ],
        16_000_000_000,
    )
    dq_parts, mine = lax.optimization_barrier((dq_parts, mine))
    dqs = swap(dq_parts, ("x", "yl"))
    dkvs = [dkv_parts[0]] + [send(dkv_parts[d], "z", 8, -d) for d in range(1, 8)]
    attended, keep_o, give_o = call(
        output_kernel,
        [place, mine, all_stats, local, cotangent, w_out],
        [shape(*local.shape), shape(512, 768), shape(512, 768)],
        [SM] + [VM] * 5,
        [VM] * 3,
        [],
        600_000_000,
    )
    give_o, dqs = lax.optimization_barrier((give_o, dqs))
    got_o = send(give_o, "core", 2, 1)
    term_o = keep_o.astype(F32) + got_o.astype(F32)
    term_o = lax.psum_scatter(term_o, "x", scatter_dimension=0, tiled=True)
    term_o = term_o.reshape(16, 8, 2, 384).transpose(0, 2, 1, 3).reshape(16, 16, 384)

    grad_tokens, keep_i, give_i = call(
        input_kernel,
        [place, dqs, *dkvs, local, w_query, w_keyval],
        [shape(*local.shape), shape(1536, 384), shape(1536, 384)],
        [SM] + [VM] * 12,
        [VM] * 3,
        [],
        900_000_000,
    )
    term_i = plus(keep_i, send(give_i, "core", 2, 1))
    term_i = added(swap(term_i.reshape(4, 384, 384), "x"))
    ends = jnp.concatenate([term_i.reshape(16, 24, 384), term_o], axis=1).astype(BF16)
    ends = added(swap(ends, ("z", "yl")))
    ends = ends + send(ends, "yh", 2, 1)
    other = send(ends, "core", 2, 1)
    low, high = jnp.where(core == 0, ends, other), jnp.where(core == 0, other, ends)
    grad_o = jnp.stack([low[24:], high[24:]]).reshape(2, 2, 8, 384)
    grad_o = grad_o.transpose(2, 0, 1, 3).reshape(8, 1536)
    return (
        attended[None],
        grad_tokens[None],
        jnp.concatenate([low[:24, :256], high[:24, :256]], axis=1),
        jnp.concatenate([low[:24, 256:], high[:24, 256:]], axis=1),
        grad_o,
    )


def solution(mesh):
    torus = Mesh(mesh.devices.reshape(4, 8, 2, 2, 2), AXES)
    return jax.shard_map(
        body,
        mesh=torus,
        in_specs=(P(DP, SEQ, None), P(DP, SEQ, None), P(), P(), P()),
        out_specs=(
            P(DP, SEQ, None),
            P(DP, SEQ, None),
            P(SEQ, None),
            P(SEQ, None),
            P(SEQ, None),
        ),
        check_vma=False,
    )
```

time: 1780 us -> 217 us (0.12)
  waiting for transfers between devices: 1500 us -> 38.2 us
  matrix products: 117 us -> 2.96 us
  local copies, waits for them, and re-layouts: 62 us -> 3.86 us
  starting transfers between devices: 0.21 us -> 58.3 us
  Pallas kernels: 0 us -> 43 us
  blocking collectives: 67 us -> 47.5 us
    reduce_scatter x2 -> x1, waiting for transfers between devices: 629 us -> 0.02 us  [body(): term_o = lax.psum_scatter(term_o, 'x', scatter_dimension=0, tiled=True)]
    unnamed x7 -> x1, waiting for transfers between devices: 616 us -> 0.02 us
    all_gather x1 -> x0, waiting for transfers between devices: 257 us -> none  [gather_keys(): return lax.all_gather(keyval, 'seq', axis=0, tiled=True)]
    dot_general x106 -> x3, matrix products: 117 us -> 2.96 us  [the longest x1 2.04 us: body(): query = jnp.dot(local, w_query, preferred_element_type=F32).astype(BF16)]
    psum x1 -> x0, blocking collectives: 67 us -> none  [body(): lax.psum(shares[0].astype(jnp.bfloat16), 'dp').astype(jnp.float32)]
    all_to_all x0 -> x3, blocking collectives: none -> 47.5 us  [swap(): return lax.all_to_all(blocks, axes, 0, 0)]
    ppermute x0 -> x18, starting transfers between devices: none -> 43.7 us  [send(): lax.ppermute(array, axis, [(i, (i + step) % size) for i in range(size)])]
    pallas_call x0 -> x4, Pallas kernels: none -> 43 us  [call(): pl.pallas_call(kernel, out_shape=outs, in_specs=in_specs, out_specs=out_s...]
  transfers between devices with their start and end apart: 5 -> 22, of which waited for: 5 -> 12; matrix products, arithmetic and copies ran while one was open for 1% -> 1% of each run, Pallas kernels for 0% -> 14%
where the time goes in v1:
time: 217 us; the launch traced here: 216 us
  starting transfers between devices  58.3 us (27%)
  blocking collectives  47.5 us (22%)
  Pallas kernels  43 us (20%)
  waiting for transfers between devices  38.2 us (18%)
  between operations  14.4 us (7%)
  other arithmetic  7.98 us (4%)
  local copies, waits for them, and re-layouts  3.86 us (2%)
  matrix products  2.96 us (1%)
    all_to_all x3, blocking collectives, swap(): return lax.all_to_all(blocks, axes, 0, 0)  47.5 us
    ppermute x18, starting transfers between devices, send(): lax.ppermute(array, axis, [(i, (i + step) % size) for i in range(size)])  43.7 us
    pallas_call x4, Pallas kernels, call(): pl.pallas_call(kernel, out_shape=outs, in_specs=in_specs, out_specs=out_s...  43 us
    ppermute x18, waiting for transfers between devices, send(): lax.ppermute(array, axis, [(i, (i + step) % size) for i in range(size)])  25.1 us
    all_to_all x3, starting transfers between devices, swap(): return lax.all_to_all(blocks, axes, 0, 0)  14.6 us
    all_to_all x3, waiting for transfers between devices, swap(): return lax.all_to_all(blocks, axes, 0, 0)  13 us
  transfers between devices with their start and end apart: 22, of which 12 were waited for; matrix products, arithmetic and copies ran while one was open for 1% of the time, Pallas kernels for 14%

profile of v1, /device:TPU:1, one launch (start us, length us, event | category | flops | bytes accessed | tf_op | source)
XLA Modules:
  0.0 216.1 jit_solution(15725399018933325856)
XLA Ops:
  11.5 6.0 %all-to-all-start = ((bf16[8,128,1024]{2,1,0:T(8,128)(2,1)}), bf16[8,128,1024]{2,1,0:T(8,128)(2,1)}, u32[]{:S(2)}, u32[]{:S(2)}) async-start(bf16[8,128,1024]{2,1,0:T(8,128)(2,1)} %broadcast_in_dim.8), calls=%async_computation | async-start | bytes 4194304 | tf_op jit(solution)/shard_map/all_to_all | solution.py:186
  17.8 5.7 %collective-permute-start.6 = (bf16[128,256]{1,0:T(8,128)(2,1)S(1)}, bf16[128,256]{1,0:T(8,128)(2,1)S(1)}, u32[]{:S(2)}, u32[]{:S(2)}) collective-permute-start(bf16[128,256]{1,0:T(8,128)(2,1)S(1)} %convolution_convert_fusion.2.refs_0_), channel_id=1, source_target_pairs={{0,56},{8,0},{16,8},{24,16},{32,24},{40,32},{48,40},{56,48},{1,57}... | collective-permute-start | bytes 196616 | tf_op jit(solution)/shard_map/ppermute | solution.py:35
  25.1 4.5 %collective-permute-start.3 = (bf16[128,256]{1,0:T(8,128)(2,1)S(1)}, bf16[128,256]{1,0:T(8,128)(2,1)S(1)}, u32[]{:S(2)}, u32[]{:S(2)}) collective-permute-start(bf16[128,256]{1,0:T(8,128)(2,1)S(1)} %convolution_convert_fusion.2.refs_0_), channel_id=1, source_target_pairs={{0,32},{8,40},{16,48},{24,56},{32,0},{40,8},{48,16},{56,24},{1,33}... | collective-permute-start | bytes 196616 | tf_op jit(solution)/shard_map/ppermute | solution.py:35
  33.2 3.1 %collective-permute-done.2.refs_3_ = bf16[128,256]{1,0:T(8,128)(2,1)S(1)} collective-permute-done((bf16[128,256]{1,0:T(8,128)(2,1)S(1)}, bf16[128,256]{1,0:T(8,128)(2,1)S(1)}, u32[]{:S(2)}, u32[]{:S(2)}) %collective-permute-start.2) | collective-permute-done | bytes 65568 | tf_op jit(solution)/shard_map/ppermute | solution.py:35
  36.3 5.3 %collective-permute-done.1.refs_2_ = bf16[128,256]{1,0:T(8,128)(2,1)S(1)} collective-permute-done((bf16[128,256]{1,0:T(8,128)(2,1)S(1)}, bf16[128,256]{1,0:T(8,128)(2,1)S(1)}, u32[]{:S(2)}, u32[]{:S(2)}) %collective-permute-start.1) | collective-permute-done | bytes 65568 | tf_op jit(solution)/shard_map/ppermute | solution.py:35
  41.8 5.4 %all-to-all-done.qd = bf16[8,128,1024]{2,1,0:T(8,128)(2,1)} async-done(((bf16[8,128,1024]{2,1,0:T(8,128)(2,1)}), bf16[8,128,1024]{2,1,0:T(8,128)(2,1)}, u32[]{:S(2)}, u32[]{:S(2)}) %all-to-all-start) | async-done | bytes 2097184 | tf_op jit(solution)/shard_map/all_to_all | solution.py:186
  47.2 13.1 %shard_map.92 = (bf16[8,128,512]{2,1,0:T(8,128)(2,1)}, f32[16,512]{1,0:T(8,128)}) custom-call(bf16[8,128,1024]{2,1,0:T(8,128)(2,1)} %all-to-all-done.qd, bf16[128,256]{1,0:T(8,128)(2,1)} %copy-done.13, bf16[128,256]{1,0:T(8,128)(2,1)} %copy-done.27, bf16[128,256]{1,0:T(8,128)(2,1)} %copy-done.26, bf16[128,256]{1,0:T(8,128)(2,1)} %copy-done.25, ...), custom_call_target="tpu_custom_call" | custom-call | flops 10000000000 | bytes 6000000 | tf_op jit(solution)/shard_map/pallas_call | solution.py:170
  61.1 9.0 %all_to_all.30.stats_ref = f32[8,16,512]{2,1,0:T(8,128)} all-to-all(f32[8,16,512]{2,1,0:T(8,128)S(1)} %broadcast_in_dim.9), channel_id=1, replica_groups=mesh['x'=4,'z'=8,'yl'=2,'yh'=2,'core'=2] {'x','yl'}, dimensions={0} | all-to-all | bytes 524288 | tf_op jit(solution)/shard_map/all_to_all | solution.py:186
  70.1 3.6 %all-to-all-start.2 = ((bf16[8,128,512]{2,1,0:T(8,128)(2,1)}), bf16[8,128,512]{2,1,0:T(8,128)(2,1)S(1)}, u32[]{:S(2)}, u32[]{:S(2)}) async-start(bf16[8,128,512]{2,1,0:T(8,128)(2,1)} %get-tuple-element.34), calls=%async_computation.2 | async-start | bytes 2097152 | tf_op jit(solution)/shard_map/all_to_all | solution.py:186
  73.6 20.7 %shard_map.93 = (bf16[8,128,512]{2,1,0:T(8,128)(2,1)}, bf16[128,256]{1,0:T(8,128)(2,1)}, bf16[128,256]{1,0:T(8,128)(2,1)}, bf16[128,256]{1,0:T(8,128)(2,1)}, bf1...) custom-call(bf16[8,128,1024]{2,1,0:T(8,128)(2,1)} %all-to-all-done.q, ...), custom_call_target="tpu_custom_call" | custom-call | flops 16000000000 | bytes 6000000 | tf_op jit(solution)/shard_map/pallas_call | solution.py:170
  94.3 5.1 %all-to-all-start.3 = ((bf16[8,128,512]{2,1,0:T(8,128)(2,1)}), bf16[8,128,512]{2,1,0:T(8,128)(2,1)S(1)}, u32[]{:S(2)}, u32[]{:S(2)}) async-start(bf16[8,128,512]{2,1,0:T(8,128)(2,1)} %get-tuple-element.38), calls=%async_computation.3 | async-start | bytes 2097152 | tf_op jit(solution)/shard_map/all_to_all | solution.py:186
  100.1 4.1 %shard_map.94 = (bf16[128,1536]{1,0:T(8,128)(2,1)}, bf16[512,768]{1,0:T(8,128)(2,1)}, bf16[512,768]{1,0:T(8,128)(2,1)}) custom-call(s32[2]{0:T(128)} %pad_add_fusion.place, bf16[8,128,512]{2,1,0:T(8,128)(2,1)} %copy-done.3, f32[8,16,512]{2,1,0:T(8,128)} %all_to_all.30.stats_ref, bf16[128,1536]{1,0:T(8,128)(2,1)} %bitcast.28, bf16[128,1536]{1,0:T(8,128)(2,1)} %bitcast.32, ...), custom_call_target="tpu_custom_call" | custom-call | flops 600000000 | bytes 6000000 | tf_op jit(solution)/shard_map/pallas_call | solution.py:170
  104.1 7.6 %all-to-all-done.3.dq_ref = bf16[8,128,512]{2,1,0:T(8,128)(2,1)S(1)} async-done(((bf16[8,128,512]{2,1,0:T(8,128)(2,1)}), bf16[8,128,512]{2,1,0:T(8,128)(2,1)S(1)}, u32[]{:S(2)}, u32[]{:S(2)}) %all-to-all-start.3) | async-done | bytes 1048608 | tf_op jit(solution)/shard_map/all_to_all | solution.py:186
  111.8 4.2 %collective-permute-start.15 = (bf16[512,768]{1,0:T(8,128)(2,1)}, bf16[512,768]{1,0:T(8,128)(2,1)S(1)}, u32[]{:S(2)}, u32[]{:S(2)}) collective-permute-start(bf16[512,768]{1,0:T(8,128)(2,1)} %get-tuple-element.52), channel_id=1, source_target_pairs={{0,1},{1,0},{2,3},{3,2},{4,5},{5,4},{6,7},{7,6},{8,9},{9,8},{10,11... | collective-permute-start | bytes 2359304 | tf_op jit(solution)/shard_map/ppermute | solution.py:35
  121.4 6.5 %collective-permute-start.7 = (bf16[128,256]{1,0:T(8,128)(2,1)S(1)}, bf16[128,256]{1,0:T(8,128)(2,1)S(1)}, u32[]{:S(2)}, u32[]{:S(2)}) collective-permute-start(bf16[128,256]{1,0:T(8,128)(2,1)S(1)} %copy-done.20), channel_id=1, source_target_pairs={{0,56},{8,0},{16,8},{24,16},{32,24},{40,32},{48,40},{56,48},{1,57}... | collective-permute-start | bytes 196616 | tf_op jit(solution)/shard_map/ppermute | solution.py:35
  129.5 4.5 %collective-permute-start.10 = (bf16[128,256]{1,0:T(8,128)(2,1)S(1)}, bf16[128,256]{1,0:T(8,128)(2,1)S(1)}, u32[]{:S(2)}, u32[]{:S(2)}) collective-permute-start(bf16[128,256]{1,0:T(8,128)(2,1)S(1)} %copy-done.17), channel_id=1, source_target_pairs={{0,32},{8,40},{16,48},{24,56},{32,0},{40,8},{48,16},{56,24},{1,33}... | collective-permute-start | bytes 196616 | tf_op jit(solution)/shard_map/ppermute | solution.py:35
  137.6 2.5 %collective-permute-done.11.refs_5_ = bf16[128,256]{1,0:T(8,128)(2,1)S(1)} collective-permute-done((bf16[128,256]{1,0:T(8,128)(2,1)S(1)}, bf16[128,256]{1,0:T(8,128)(2,1)S(1)}, u32[]{:S(2)}, u32[]{:S(2)}) %collective-permute-start.11) | collective-permute-done | bytes 65568 | tf_op jit(solution)/shard_map/ppermute | solution.py:35
  140.1 4.8 %collective-permute-done.12.refs_6_ = bf16[128,256]{1,0:T(8,128)(2,1)S(1)} collective-permute-done((bf16[128,256]{1,0:T(8,128)(2,1)S(1)}, bf16[128,256]{1,0:T(8,128)(2,1)S(1)}, u32[]{:S(2)}, u32[]{:S(2)}) %collective-permute-start.12) | collective-permute-done | bytes 65568 | tf_op jit(solution)/shard_map/ppermute | solution.py:35
  147.1 5.1 %shard_map.95 = (bf16[128,1536]{1,0:T(8,128)(2,1)}, bf16[1536,384]{1,0:T(8,128)(2,1)}, bf16[1536,384]{1,0:T(8,128)(2,1)}) custom-call(s32[2]{0:T(128)} %pad_add_fusion.place, bf16[8,128,512]{2,1,0:T(8,128)(2,1)} %copy-done.2, bf16[128,256]{1,0:T(8,128)(2,1)} %get-tuple-element.40.refs_0_, bf16[128,256]{1,0:T(8,128)(2,1)} %copy-done.6, ...), custom_call_target="tpu_custom_call" | custom-call | flops 900000000 | bytes 6000000 | tf_op jit(solution)/shard_map/pallas_call | solution.py:170
  153.3 2.7 %collective-permute-done.14 = bf16[1536,384]{1,0:T(8,128)(2,1)S(1)} collective-permute-done((bf16[1536,384]{1,0:T(8,128)(2,1)}, bf16[1536,384]{1,0:T(8,128)(2,1)S(1)}, u32[]{:S(2)}, u32[]{:S(2)}) %collective-permute-start.14) | collective-permute-done | bytes 1179680 | tf_op jit(solution)/shard_map/ppermute | solution.py:35
  157.6 18.7 %all_to_all.31 = bf16[4,384,384]{2,1,0:T(8,128)(2,1)S(1)} all-to-all(bf16[4,384,384]{2,1,0:T(8,128)(2,1)S(1)} %bitcast.31), channel_id=1, replica_groups=mesh['x'=4,'z'=8,'yl'=2,'yh'=2,'core'=2] {'x'}, dimensions={0} | all-to-all | bytes 2359296 | tf_op jit(solution)/shard_map/all_to_all | solution.py:186
  177.6 19.8 %all_to_all.32 = bf16[16,40,384]{2,1,0:T(8,128)(2,1)S(1)} all-to-all(bf16[16,40,384]{2,1,0:T(8,128)(2,1)S(1)} %pad_maximum_fusion), channel_id=1, replica_groups=mesh['x'=4,'z'=8,'yl'=2,'yh'=2,'core'=2] {'z','yl'}, dimensions={0} | all-to-all | bytes 983040 | tf_op jit(solution)/shard_map/all_to_all | solution.py:186
  197.5 2.7 %collective-permute-start.16 = (f32[40,384]{1,0:T(8,128)S(1)}, f32[40,384]{1,0:T(8,128)S(1)}, u32[]{:S(2)}, u32[]{:S(2)}) collective-permute-start(f32[40,384]{1,0:T(8,128)S(1)} %convert_reduce_fusion), channel_id=1, source_target_pairs={{0,2},{2,0},{1,3},{3,1},{4,6},{6,4},{5,7},{7,5},{8,10},{10,8},{9,1... | collective-permute-start | bytes 184328 | tf_op jit(solution)/shard_map/ppermute | solution.py:35
  202.2 4.2 %collective-permute-start.17 = (f32[40,384]{1,0:T(8,128)S(1)}, f32[40,384]{1,0:T(8,128)S(1)}, u32[]{:S(2)}, u32[]{:S(2)}) collective-permute-start(f32[40,384]{1,0:T(8,128)S(1)} %add.17), channel_id=1, source_target_pairs={{0,1},{1,0},{2,3},{3,2},{4,5},{5,4},{6,7},{7,6},{8,9},{9,8},{10,11... | collective-permute-start | bytes 184328 | tf_op jit(solution)/shard_map/ppermute | solution.py:35
  (107 shorter events, 33.0 us)
Async XLA Ops:
  11.5 35.6 %all-to-all-start = ((bf16[8,128,1024]{2,1,0:T(8,128)(2,1)}), bf16[8,128,1024]{2,1,0:T(8,128)(2,1)}, u32[]{:S(2)}, u32[]{:S(2)}) async-start(bf16[8,128,1024]{2,1,0:T(8,128)(2,1)} %broadcast_in_dim.8), calls=%async_computation | async-start | bytes 4194304 | tf_op jit(solution)/shard_map/all_to_all | solution.py:186
  17.8 29.4 %copy-start.13 = (bf16[128,256]{1,0:T(8,128)(2,1)}, bf16[128,256]{1,0:T(8,128)(2,1)S(1)}, u32[]{:S(2)}) copy-start(bf16[128,256]{1,0:T(8,128)(2,1)S(1)} %convolution_convert_fusion.2.refs_0_) | copy-start | bytes 196612
  17.8 11.8 %collective-permute-start.6 = (bf16[128,256]{1,0:T(8,128)(2,1)S(1)}, bf16[128,256]{1,0:T(8,128)(2,1)S(1)}, u32[]{:S(2)}, u32[]{:S(2)}) collective-permute-start(bf16[128,256]{1,0:T(8,128)(2,1)S(1)} %convolution_convert_fusion.2.refs_0_), channel_id=1, source_target_pairs={{0,56},{8,0},{16,8},{24,16},{32,24},{40,32},{48,40},{56,48},{1,57}... | collective-permute-start | bytes 196616 | tf_op jit(solution)/shard_map/ppermute | solution.py:35
  23.5 8.3 %collective-permute-start.5 = (bf16[128,256]{1,0:T(8,128)(2,1)S(1)}, bf16[128,256]{1,0:T(8,128)(2,1)S(1)}, u32[]{:S(2)}, u32[]{:S(2)}) collective-permute-start(bf16[128,256]{1,0:T(8,128)(2,1)S(1)} %convolution_convert_fusion.2.refs_0_), channel_id=1, source_target_pairs={{0,48},{8,56},{16,0},{24,8},{32,16},{40,24},{48,32},{56,40},{1,49}... | collective-permute-start | bytes 196616 | tf_op jit(solution)/shard_map/ppermute | solution.py:35
  24.6 8.5 %collective-permute-start.4 = (bf16[128,256]{1,0:T(8,128)(2,1)S(1)}, bf16[128,256]{1,0:T(8,128)(2,1)S(1)}, u32[]{:S(2)}, u32[]{:S(2)}) collective-permute-start(bf16[128,256]{1,0:T(8,128)(2,1)S(1)} %convolution_convert_fusion.2.refs_0_), channel_id=1, source_target_pairs={{0,40},{8,48},{16,56},{24,0},{32,8},{40,16},{48,24},{56,32},{1,41}... | collective-permute-start | bytes 196616 | tf_op jit(solution)/shard_map/ppermute | solution.py:35
  25.1 8.0 %collective-permute-start.3 = (bf16[128,256]{1,0:T(8,128)(2,1)S(1)}, bf16[128,256]{1,0:T(8,128)(2,1)S(1)}, u32[]{:S(2)}, u32[]{:S(2)}) collective-permute-start(bf16[128,256]{1,0:T(8,128)(2,1)S(1)} %convolution_convert_fusion.2.refs_0_), channel_id=1, source_target_pairs={{0,32},{8,40},{16,48},{24,56},{32,0},{40,8},{48,16},{56,24},{1,33}... | collective-permute-start | bytes 196616 | tf_op jit(solution)/shard_map/ppermute | solution.py:35
  29.6 6.7 %collective-permute-start.2 = (bf16[128,256]{1,0:T(8,128)(2,1)S(1)}, bf16[128,256]{1,0:T(8,128)(2,1)S(1)}, u32[]{:S(2)}, u32[]{:S(2)}) collective-permute-start(bf16[128,256]{1,0:T(8,128)(2,1)S(1)} %convolution_convert_fusion.2.refs_0_), channel_id=1, source_target_pairs={{0,24},{8,32},{16,40},{24,48},{32,56},{40,0},{48,8},{56,16},{1,25}... | collective-permute-start | bytes 196616 | tf_op jit(solution)/shard_map/ppermute | solution.py:35
  29.6 17.6 %copy-start.21 = (bf16[128,256]{1,0:T(8,128)(2,1)}, bf16[128,256]{1,0:T(8,128)(2,1)S(1)}, u32[]{:S(2)}) copy-start(bf16[128,256]{1,0:T(8,128)(2,1)S(1)} %collective-permute-done.6.refs_7_) | copy-start | bytes 196612
  29.6 12.0 %collective-permute-start.1 = (bf16[128,256]{1,0:T(8,128)(2,1)S(1)}, bf16[128,256]{1,0:T(8,128)(2,1)S(1)}, u32[]{:S(2)}, u32[]{:S(2)}) collective-permute-start(bf16[128,256]{1,0:T(8,128)(2,1)S(1)} %convolution_convert_fusion.2.refs_0_), channel_id=1, source_target_pairs={{0,16},{8,24},{16,32},{24,40},{32,48},{40,56},{48,0},{56,8},{1,17}... | collective-permute-start | bytes 196616 | tf_op jit(solution)/shard_map/ppermute | solution.py:35
  31.8 10.0 %collective-permute-start = (bf16[128,256]{1,0:T(8,128)(2,1)S(1)}, bf16[128,256]{1,0:T(8,128)(2,1)S(1)}, u32[]{:S(2)}, u32[]{:S(2)}) collective-permute-start(bf16[128,256]{1,0:T(8,128)(2,1)S(1)} %convolution_convert_fusion.2.refs_0_), channel_id=1, source_target_pairs={{0,8},{8,16},{16,24},{24,32},{32,40},{40,48},{48,56},{56,0},{1,9},... | collective-permute-start | bytes 196616 | tf_op jit(solution)/shard_map/ppermute | solution.py:35
  70.1 24.3 %all-to-all-start.2 = ((bf16[8,128,512]{2,1,0:T(8,128)(2,1)}), bf16[8,128,512]{2,1,0:T(8,128)(2,1)S(1)}, u32[]{:S(2)}, u32[]{:S(2)}) async-start(bf16[8,128,512]{2,1,0:T(8,128)(2,1)} %get-tuple-element.34), calls=%async_computation.2 | async-start | bytes 2097152 | tf_op jit(solution)/shard_map/all_to_all | solution.py:186
  94.3 17.4 %all-to-all-start.3 = ((bf16[8,128,512]{2,1,0:T(8,128)(2,1)}), bf16[8,128,512]{2,1,0:T(8,128)(2,1)S(1)}, u32[]{:S(2)}, u32[]{:S(2)}) async-start(bf16[8,128,512]{2,1,0:T(8,128)(2,1)} %get-tuple-element.38), calls=%async_computation.3 | async-start | bytes 2097152 | tf_op jit(solution)/shard_map/all_to_all | solution.py:186
  99.4 77.1 %reduce-scatter.2.cloned.1.call-start = ((), (), s32[]{:S(2)}) async-start(), calls=%async_computation.7 | async-start | bytes 1966080 | tf_op jit(solution)/shard_map/reduce_scatter | solution.py:260
  111.8 6.3 %collective-permute-start.15 = (bf16[512,768]{1,0:T(8,128)(2,1)}, bf16[512,768]{1,0:T(8,128)(2,1)S(1)}, u32[]{:S(2)}, u32[]{:S(2)}) collective-permute-start(bf16[512,768]{1,0:T(8,128)(2,1)} %get-tuple-element.52), channel_id=1, source_target_pairs={{0,1},{1,0},{2,3},{3,2},{4,5},{5,4},{6,7},{7,6},{8,9},{9,8},{10,11... | collective-permute-start | bytes 2359304 | tf_op jit(solution)/shard_map/ppermute | solution.py:35
  121.4 12.6 %collective-permute-start.7 = (bf16[128,256]{1,0:T(8,128)(2,1)S(1)}, bf16[128,256]{1,0:T(8,128)(2,1)S(1)}, u32[]{:S(2)}, u32[]{:S(2)}) collective-permute-start(bf16[128,256]{1,0:T(8,128)(2,1)S(1)} %copy-done.20), channel_id=1, source_target_pairs={{0,56},{8,0},{16,8},{24,16},{32,24},{40,32},{48,40},{56,48},{1,57}... | collective-permute-start | bytes 196616 | tf_op jit(solution)/shard_map/ppermute | solution.py:35
  127.9 8.2 %collective-permute-start.8 = (bf16[128,256]{1,0:T(8,128)(2,1)S(1)}, bf16[128,256]{1,0:T(8,128)(2,1)S(1)}, u32[]{:S(2)}, u32[]{:S(2)}) collective-permute-start(bf16[128,256]{1,0:T(8,128)(2,1)S(1)} %copy-done.19), channel_id=1, source_target_pairs={{0,48},{8,56},{16,0},{24,8},{32,16},{40,24},{48,32},{56,40},{1,49}... | collective-permute-start | bytes 196616 | tf_op jit(solution)/shard_map/ppermute | solution.py:35
  129.0 8.6 %collective-permute-start.9 = (bf16[128,256]{1,0:T(8,128)(2,1)S(1)}, bf16[128,256]{1,0:T(8,128)(2,1)S(1)}, u32[]{:S(2)}, u32[]{:S(2)}) collective-permute-start(bf16[128,256]{1,0:T(8,128)(2,1)S(1)} %copy-done.18), channel_id=1, source_target_pairs={{0,40},{8,48},{16,56},{24,0},{32,8},{40,16},{48,24},{56,32},{1,41}... | collective-permute-start | bytes 196616 | tf_op jit(solution)/shard_map/ppermute | solution.py:35
  129.5 8.1 %collective-permute-start.10 = (bf16[128,256]{1,0:T(8,128)(2,1)S(1)}, bf16[128,256]{1,0:T(8,128)(2,1)S(1)}, u32[]{:S(2)}, u32[]{:S(2)}) collective-permute-start(bf16[128,256]{1,0:T(8,128)(2,1)S(1)} %copy-done.17), channel_id=1, source_target_pairs={{0,32},{8,40},{16,48},{24,56},{32,0},{40,8},{48,16},{56,24},{1,33}... | collective-permute-start | bytes 196616 | tf_op jit(solution)/shard_map/ppermute | solution.py:35
  134.0 6.1 %collective-permute-start.11 = (bf16[128,256]{1,0:T(8,128)(2,1)S(1)}, bf16[128,256]{1,0:T(8,128)(2,1)S(1)}, u32[]{:S(2)}, u32[]{:S(2)}) collective-permute-start(bf16[128,256]{1,0:T(8,128)(2,1)S(1)} %copy-done.16), channel_id=1, source_target_pairs={{0,24},{8,32},{16,40},{24,48},{32,56},{40,0},{48,8},{56,16},{1,25}... | collective-permute-start | bytes 196616 | tf_op jit(solution)/shard_map/ppermute | solution.py:35
  134.0 10.9 %collective-permute-start.12 = (bf16[128,256]{1,0:T(8,128)(2,1)S(1)}, bf16[128,256]{1,0:T(8,128)(2,1)S(1)}, u32[]{:S(2)}, u32[]{:S(2)}) collective-permute-start(bf16[128,256]{1,0:T(8,128)(2,1)S(1)} %copy-done.15), channel_id=1, source_target_pairs={{0,16},{8,24},{16,32},{24,40},{32,48},{40,56},{48,0},{56,8},{1,17}... | collective-permute-start | bytes 196616 | tf_op jit(solution)/shard_map/ppermute | solution.py:35
  136.1 10.4 %collective-permute-start.13 = (bf16[128,256]{1,0:T(8,128)(2,1)S(1)}, bf16[128,256]{1,0:T(8,128)(2,1)S(1)}, u32[]{:S(2)}, u32[]{:S(2)}) collective-permute-start(bf16[128,256]{1,0:T(8,128)(2,1)S(1)} %copy-done.14), channel_id=1, source_target_pairs={{0,8},{8,16},{16,24},{24,32},{32,40},{40,48},{48,56},{56,0},{1,9},... | collective-permute-start | bytes 196616 | tf_op jit(solution)/shard_map/ppermute | solution.py:35
  152.2 3.7 %collective-permute-start.14 = (bf16[1536,384]{1,0:T(8,128)(2,1)}, bf16[1536,384]{1,0:T(8,128)(2,1)S(1)}, u32[]{:S(2)}, u32[]{:S(2)}) collective-permute-start(bf16[1536,384]{1,0:T(8,128)(2,1)} %get-tuple-element.50), channel_id=1, source_target_pairs={{0,1},{1,0},{2,3},{3,2},{4,5},{5,4},{6,7},{7,6},{8,9},{9,8},{10,11... | collective-permute-start | bytes 3538952 | tf_op jit(solution)/shard_map/ppermute | solution.py:35
  197.5 4.7 %collective-permute-start.16 = (f32[40,384]{1,0:T(8,128)S(1)}, f32[40,384]{1,0:T(8,128)S(1)}, u32[]{:S(2)}, u32[]{:S(2)}) collective-permute-start(f32[40,384]{1,0:T(8,128)S(1)} %convert_reduce_fusion), channel_id=1, source_target_pairs={{0,2},{2,0},{1,3},{3,1},{4,6},{6,4},{5,7},{7,5},{8,10},{10,8},{9,1... | collective-permute-start | bytes 184328 | tf_op jit(solution)/shard_map/ppermute | solution.py:35
  202.2 5.1 %collective-permute-start.17 = (f32[40,384]{1,0:T(8,128)S(1)}, f32[40,384]{1,0:T(8,128)S(1)}, u32[]{:S(2)}, u32[]{:S(2)}) collective-permute-start(f32[40,384]{1,0:T(8,128)S(1)} %add.17), channel_id=1, source_target_pairs={{0,1},{1,0},{2,3},{3,2},{4,5},{5,4},{6,7},{7,6},{8,9},{9,8},{10,11... | collective-permute-start | bytes 184328 | tf_op jit(solution)/shard_map/ppermute | solution.py:35
  (26 other events, 213.3 us)
Sparse Core Ops, SparseCore 0:
  120.7 28.3 reduce-scatter.1

commit v2 on v1

--- a/solution.py
+++ b/solution.py
@@ -13,8 +13,8 @@
 ROWS = HEADS * POS
 GROUP = 8
 KEYS = 8 * POS
-FORWARD_CHUNK = 512
-BACKWARD_CHUNK = 128
+CHUNK = 512
+TILE = 32
 SCALE = 1.0 / HEAD_DIM**0.5
 LOG2E = math.log2(math.e)
 AXES = ("x", "z", "yl", "yh", "core")
@@ -41,40 +41,46 @@
     )
 
 
-def forward_kernel(qd, *refs):
-    mixed, stats_ref, kv, vt, score = refs[8:]
-    for i in range(8):
-        kv[i * POS : (i + 1) * POS, :] = refs[i][...]
+def tiles(count):
+    return [slice(t * TILE, (t + 1) * TILE) for t in range(count // TILE)]
+
+
+def fold(values, op):
+    return op(values.reshape(-1, 8, values.shape[1]), axis=0)
+
+
+def forward_kernel(qd, kv, mixed, stats_ref, vt, *scratch):
     vt[...] = kv[:, HEAD_DIM:].T
 
-    def block(p, carry):
-        both = qd[p]
-        q4 = rows_of(both[:, :ROWS])
-        d4 = rows_of(both[:, ROWS:])
-        top = jnp.full((1, ROWS), -jnp.inf, F32)
-        for c in range(KEYS // FORWARD_CHUNK):
-            part = slice(c * FORWARD_CHUNK, (c + 1) * FORWARD_CHUNK)
-            s = dot(kv[part, :HEAD_DIM], q4, NT)
-            score[part, :] = s
-            top = jnp.maximum(top, jnp.max(s, axis=0, keepdims=True))
+    def scores(p, score):
+        score[...] = dot(kv[:, :HEAD_DIM], rows_of(qd[p, :, :ROWS]), NT)
+
+    def softmax(p, score, weight):
+        top = jnp.full((8, ROWS), -jnp.inf, F32)
+        for part in tiles(KEYS):
+            top = jnp.maximum(top, fold(score[part, :], jnp.max))
+        top = jnp.max(top, axis=0, keepdims=True)
         base = top * (SCALE * LOG2E)
-        total = jnp.zeros((1, ROWS), F32)
-        weighted = jnp.zeros((1, ROWS), F32)
-        acc = jnp.zeros((HEAD_DIM, ROWS), F32)
-        for c in range(KEYS // FORWARD_CHUNK):
-            part = slice(c * FORWARD_CHUNK, (c + 1) * FORWARD_CHUNK)
+        total = jnp.zeros((8, ROWS), F32)
+        for part in tiles(KEYS):
             e = jnp.exp2(score[part, :] * (SCALE * LOG2E) - base)
-            dp = dot(kv[part, HEAD_DIM:], d4, NT)
-            total = total + jnp.sum(e, axis=0, keepdims=True)
-            weighted = weighted + jnp.sum(e * dp, axis=0, keepdims=True)
-            acc = acc + dot(vt[:, part], e.astype(BF16))
-        inverse = 1.0 / total
-        mixed[p] = (acc * inverse).astype(BF16)
+            total = total + fold(e, jnp.sum)
+            weight[part, :] = e.astype(BF16)
+        total = jnp.sum(total, axis=0, keepdims=True)
+        acc = dot(vt[...], weight[...]) * (1.0 / total)
+        mixed[p] = acc.astype(BF16)
         stats_ref[pl.ds(p, 1), :] = top * SCALE + jnp.log(total)
-        stats_ref[pl.ds(8 + p, 1), :] = weighted * inverse
+        d4 = rows_of(qd[p, :, ROWS:])
+        stats_ref[pl.ds(8 + p, 1), :] = jnp.sum(acc * d4.T.astype(F32), axis=0, keepdims=True)
+
+    def block(i, carry):
+        for n in range(2):
+            scores(2 * i + n, scratch[n])
+        for n in range(2):
+            softmax(2 * i + n, scratch[n], scratch[2 + n])
         return carry
 
-    lax.fori_loop(0, GROUP, block, 0)
+    lax.fori_loop(0, GROUP // 2, block, 0)
 
 
 def combine(logs, bars):
@@ -85,11 +91,7 @@
     return top + jnp.log(total), jnp.sum(weights * bars, axis=0), weights
 
 
-def backward_kernel(qd, stats_ref, *refs):
-    dq, dkv_out = refs[8], refs[9:17]
-    kv, kt, stat, dkv = refs[17:]
-    for i in range(8):
-        kv[i * POS : (i + 1) * POS, :] = refs[i][...]
+def backward_kernel(qd, stats_ref, kv, dq, dkv_out, kt, stat, dkv, *scratch):
     kt[...] = kv[:, :HEAD_DIM].T
     logsum, delta, unused = combine(stats_ref[:, :8, :], stats_ref[:, 8:, :])
     stat[:8, :] = logsum * LOG2E
@@ -103,23 +105,28 @@
         base = stat[pl.ds(p, 1), :]
         delta = stat[pl.ds(8 + p, 1), :]
         acc = jnp.zeros((HEAD_DIM, ROWS), F32)
-        for c in range(KEYS // BACKWARD_CHUNK):
-            part = slice(c * BACKWARD_CHUNK, (c + 1) * BACKWARD_CHUNK)
-            s = dot(kv[part, :HEAD_DIM], q4, NT)
-            prob = jnp.exp2(s * (SCALE * LOG2E) - base)
-            dp = dot(kv[part, HEAD_DIM:], d4, NT)
-            ds = (prob * (dp - delta)).astype(BF16)
-            dkv[part, HEAD_DIM:] += dot(prob.astype(BF16), d4)
-            dkv[part, :HEAD_DIM] += dot(ds, q4)
-            acc = acc + dot(kt[:, part], ds)
+        count = KEYS // CHUNK
+        for c in range(count):
+            part = slice(c * CHUNK, (c + 1) * CHUNK)
+            score, dprob = scratch[4 * c : 4 * c + 2]
+            score[...] = dot(kv[part, :HEAD_DIM], q4, NT)
+            dprob[...] = dot(kv[part, HEAD_DIM:], d4, NT)
+        for c in range(count):
+            part = slice(c * CHUNK, (c + 1) * CHUNK)
+            score, dprob, weight, dscore = scratch[4 * c : 4 * c + 4]
+            for tile in tiles(CHUNK):
+                prob = jnp.exp2(score[tile, :] * (SCALE * LOG2E) - base)
+                weight[tile, :] = prob.astype(BF16)
+                dscore[tile, :] = (prob * (dprob[tile, :] - delta)).astype(BF16)
+            dkv[part, HEAD_DIM:] += dot(weight[...], d4)
+            dkv[part, :HEAD_DIM] += dot(dscore[...], q4)
+            acc = acc + dot(kt[:, part], dscore[...])
         dq[p] = (acc * SCALE).astype(BF16)
         return carry
 
     lax.fori_loop(0, GROUP, block, 0)
-    for i in range(8):
-        part = slice(i * POS, (i + 1) * POS)
-        dkv_out[i][:, :HEAD_DIM] = (dkv[part, :HEAD_DIM] * SCALE).astype(BF16)
-        dkv_out[i][:, HEAD_DIM:] = dkv[part, HEAD_DIM:].astype(BF16)
+    dkv_out[:, :HEAD_DIM] = (dkv[:, :HEAD_DIM] * SCALE).astype(BF16)
+    dkv_out[:, HEAD_DIM:] = dkv[:, HEAD_DIM:].astype(BF16)
 
 
 def output_kernel(place, parts, stats_ref, tokens_ref, upstream_ref, w_out_ref, *outs):
@@ -142,14 +149,13 @@
     give_ref[...] = dot(mixed_rows, jnp.where(first, high, low)).astype(BF16)
 
 
-def input_kernel(place, dq_ref, *refs):
-    dkv_refs = refs[:8]
-    tokens_ref, w_query_ref, w_keyval_ref, grad_ref, keep_ref, give_ref = refs[8:]
+def input_kernel(place, dq_ref, dkv_ref, tokens_ref, w_query_ref, w_keyval_ref, *outs):
+    grad_ref, keep_ref, give_ref = outs
     dq_t = jnp.sum(dq_ref[...].astype(F32), axis=0)
     dquery = jnp.concatenate(
         [dq_t[:, h * POS : (h + 1) * POS].T for h in range(HEADS)], axis=1
     ).astype(BF16)
-    dkeyval = sum(ref[...].astype(F32) for ref in dkv_refs).astype(BF16)
+    dkeyval = jnp.sum(dkv_ref[...].astype(F32), axis=0).astype(BF16)
     grad_ref[...] = (
         dot(dquery, w_query_ref[...], NT) + dot(dkeyval, w_keyval_ref[...], NT)
     ).astype(BF16)
@@ -210,41 +216,42 @@
     qds = share(qd, ("x", "yl"), 8)
     qd, early = lax.optimization_barrier((qd, local))
     keyval = jnp.dot(early, w_keyval, preferred_element_type=F32).astype(BF16)
-    kvs = [keyval] + [send(keyval, "z", 8, d) for d in range(1, 8)]
+    kvs = lax.all_gather(keyval, "z", axis=0, tiled=True)
 
     mixed_parts, stats = call(
         forward_kernel,
-        [qds, *kvs],
+        [qds, kvs],
         [shape(8, HEAD_DIM, ROWS), shape(16, ROWS, dtype=F32)],
-        [VM] * 9,
+        [VM] * 2,
         [VM] * 2,
         [
-            pltpu.VMEM((KEYS, 2 * HEAD_DIM), BF16),
             pltpu.VMEM((HEAD_DIM, KEYS), BF16),
             pltpu.VMEM((KEYS, ROWS), F32),
+            pltpu.VMEM((KEYS, ROWS), F32),
+            pltpu.VMEM((KEYS, ROWS), BF16),
+            pltpu.VMEM((KEYS, ROWS), BF16),
         ],
         10_000_000_000,
     )
     all_stats = share(stats, ("x", "yl"), 8)
     mixed_parts, all_stats = lax.optimization_barrier((mixed_parts, all_stats))
     mine = swap(mixed_parts, ("x", "yl"))
-    dq_parts, *dkv_parts = call(
+    dq_parts, dkv_parts = call(
         backward_kernel,
-        [qds, all_stats, *kvs],
-        [shape(8, HEAD_DIM, ROWS)] + [shape(POS, 2 * HEAD_DIM)] * 8,
-        [VM] * 10,
-        [VM] * 9,
+        [qds, all_stats, kvs],
+        [shape(8, HEAD_DIM, ROWS), shape(KEYS, 2 * HEAD_DIM)],
+        [VM] * 3,
+        [VM] * 2,
         [
-            pltpu.VMEM((KEYS, 2 * HEAD_DIM), BF16),
             pltpu.VMEM((HEAD_DIM, KEYS), BF16),
             pltpu.VMEM((16, ROWS), F32),
             pltpu.VMEM((KEYS, 2 * HEAD_DIM), F32),
-        ],
+        ]
+        + [pltpu.VMEM((CHUNK, ROWS), t) for t in (F32, F32, BF16, BF16)] * (KEYS // CHUNK),
         16_000_000_000,
     )
-    dq_parts, mine = lax.optimization_barrier((dq_parts, mine))
-    dqs = swap(dq_parts, ("x", "yl"))
-    dkvs = [dkv_parts[0]] + [send(dkv_parts[d], "z", 8, -d) for d in range(1, 8)]
+    dq_parts, dkv_parts, mine = lax.optimization_barrier((dq_parts, dkv_parts, mine))
+    dkv = swap(dkv_parts.reshape(8, POS, 2 * HEAD_DIM), "z")
     attended, keep_o, give_o = call(
         output_kernel,
         [place, mine, all_stats, local, cotangent, w_out],
@@ -254,30 +261,42 @@
         [],
         600_000_000,
     )
-    give_o, dqs = lax.optimization_barrier((give_o, dqs))
-    got_o = send(give_o, "core", 2, 1)
-    term_o = keep_o.astype(F32) + got_o.astype(F32)
-    term_o = lax.psum_scatter(term_o, "x", scatter_dimension=0, tiled=True)
-    term_o = term_o.reshape(16, 8, 2, 384).transpose(0, 2, 1, 3).reshape(16, 16, 384)
+    give_o, dkv, dq_parts = lax.optimization_barrier((give_o, dkv, dq_parts))
+    term_o = keep_o.astype(F32) + send(give_o, "core", 2, 1).astype(F32)
+    dqs = swap(dq_parts, ("x", "yl"))
+    unused, dqs = lax.optimization_barrier((term_o, dqs))
+    term_o = term_o.reshape(32, 2, 8, 2, 384).transpose(3, 1, 0, 2, 4).reshape(1024, 384)
+    term_o = lax.psum_scatter(term_o, ("yh", "yl"), scatter_dimension=0, tiled=True)
 
     grad_tokens, keep_i, give_i = call(
         input_kernel,
-        [place, dqs, *dkvs, local, w_query, w_keyval],
+        [place, dqs, dkv, local, w_query, w_keyval],
         [shape(*local.shape), shape(1536, 384), shape(1536, 384)],
-        [SM] + [VM] * 12,
+        [SM] + [VM] * 5,
         [VM] * 3,
         [],
         900_000_000,
     )
-    term_i = plus(keep_i, send(give_i, "core", 2, 1))
-    term_i = added(swap(term_i.reshape(4, 384, 384), "x"))
-    ends = jnp.concatenate([term_i.reshape(16, 24, 384), term_o], axis=1).astype(BF16)
+    term_i = plus(keep_i, send(give_i, "core", 2, 1)).reshape(4, 384, 384)
+    terms = jnp.concatenate([term_i, term_o.astype(BF16).reshape(4, 64, 384)], axis=1)
+    terms = added(swap(terms, "x"))
+    term_i = terms[:384].reshape(8, 2, 24, 384)
+    here = (jnp.arange(2) == lax.axis_index("yl"))[None, :, None, None]
+    term_o = jnp.where(here, terms[384:].reshape(8, 1, 8, 384), 0.0)
+    ends = jnp.concatenate([term_i, term_o], axis=2).astype(BF16).reshape(16, 32, 384)
     ends = added(swap(ends, ("z", "yl")))
-    ends = ends + send(ends, "yh", 2, 1)
+    got = send(ends, "yh", 2, 1)
+    yh = lax.axis_index("yh")
+    ends = jnp.concatenate(
+        [
+            ends[:24] + got[:24],
+            jnp.where(yh == 0, ends[24:], got[24:]),
+            jnp.where(yh == 0, got[24:], ends[24:]),
+        ]
+    )
     other = send(ends, "core", 2, 1)
     low, high = jnp.where(core == 0, ends, other), jnp.where(core == 0, other, ends)
-    grad_o = jnp.stack([low[24:], high[24:]]).reshape(2, 2, 8, 384)
-    grad_o = grad_o.transpose(2, 0, 1, 3).reshape(8, 1536)
+    grad_o = jnp.concatenate([low[24:32], low[32:], high[24:32], high[32:]], axis=1)
     return (
         attended[None],
         grad_tokens[None],

time: 217 us -> 210 us (0.968)
  blocking collectives: 47.5 us -> 70.2 us
  starting transfers between devices: 58.3 us -> 36.9 us
  Pallas kernels: 43 us -> 33.5 us
    ppermute x18 -> x4, starting transfers between devices: 43.7 us -> 14.2 us  [send(): lax.ppermute(array, axis, [(i, (i + step) % size) for i in range(size)])]
    all_gather x0 -> x1, blocking collectives: none -> 26.4 us  [body(): kvs = lax.all_gather(keyval, 'z', axis=0, tiled=True)]
    ppermute x18 -> x4, waiting for transfers between devices: 25.1 us -> 7.29 us  [send(): lax.ppermute(array, axis, [(i, (i + step) % size) for i in range(size)])]
    all_to_all x3 -> x4, waiting for transfers between devices: 13 us -> 30.1 us  [swap(): return lax.all_to_all(blocks, axes, 0, 0)]
    pallas_call x4, Pallas kernels: 43 us -> 33.5 us  [call(): pl.pallas_call(kernel, out_shape=outs, in_specs=in_specs, out_specs=out_s...]
    all_to_all x3 -> x4, starting transfers between devices: 14.6 us -> 22.7 us  [swap(): return lax.all_to_all(blocks, axes, 0, 0)]
    all_to_all x3, blocking collectives: 47.5 us -> 43.8 us  [swap(): return lax.all_to_all(blocks, axes, 0, 0)]
  transfers between devices with their start and end apart: 22 -> 9, of which waited for: 12 -> 8; matrix products, arithmetic and copies ran while one was open for 1% -> 1% of each run, Pallas kernels for 14% -> 11%
where the time goes in v2:
time: 210 us; the launch traced here: 209 us
  blocking collectives  70.2 us (33%)
  waiting for transfers between devices  38.3 us (18%)
  starting transfers between devices  36.9 us (18%)
  Pallas kernels  33.5 us (16%)
  between operations  14.2 us (7%)
  other arithmetic  8.02 us (4%)
  local copies, waits for them, and re-layouts  5.01 us (2%)
  matrix products  2.95 us (1%)
    all_to_all x3, blocking collectives, swap(): return lax.all_to_all(blocks, axes, 0, 0)  43.8 us
    pallas_call x4, Pallas kernels, call(): pl.pallas_call(kernel, out_shape=outs, in_specs=in_specs, out_specs=out_s...  33.5 us
    all_to_all x4, waiting for transfers between devices, swap(): return lax.all_to_all(blocks, axes, 0, 0)  30.1 us
    all_gather x1, blocking collectives, body(): kvs = lax.all_gather(keyval, 'z', axis=0, tiled=True)  26.4 us
    all_to_all x4, starting transfers between devices, swap(): return lax.all_to_all(blocks, axes, 0, 0)  22.7 us
    ppermute x4, starting transfers between devices, send(): lax.ppermute(array, axis, [(i, (i + step) % size) for i in range(size)])  14.2 us
    ppermute x4, waiting for transfers between devices, send(): lax.ppermute(array, axis, [(i, (i + step) % size) for i in range(size)])  7.29 us
  transfers between devices with their start and end apart: 9, of which 8 were waited for; matrix products, arithmetic and copies ran while one was open for 1% of the time, Pallas kernels for 11%

profile of v2, /device:TPU:1, one launch (start us, length us, event | category | flops | bytes accessed | tf_op | source)
XLA Modules:
  0.0 209.1 jit_solution(1301444569433682727)
XLA Ops:
  7.2 2.0 convolution_convert_fusion.1
  11.5 6.0 %all-to-all-start = ((bf16[8,128,1024]{2,1,0:T(8,128)(2,1)}), bf16[8,128,1024]{2,1,0:T(8,128)(2,1)}, u32[]{:S(2)}, u32[]{:S(2)}) async-start(bf16[8,128,1024]{2,1,0:T(8,128)(2,1)} %broadcast_in_dim.47), calls=%async_computation | async-start | bytes 4194304 | tf_op jit(solution)/shard_map/all_to_all | solution.py:192
  17.8 26.4 %all_gather.3.kv = bf16[1024,256]{1,0:T(8,128)(2,1)} all-gather(bf16[128,256]{1,0:T(8,128)(2,1)S(1)} %convolution_convert_fusion.2), channel_id=1, replica_groups=mesh['x'=4,'z'=8,'yl'=2,'yh'=2,'core'=2] {'z'}, dimensions={0}, use_global_device_ids=true | all-gather | bytes 589824 | tf_op jit(solution)/shard_map/all_gather | solution.py:219
  44.2 3.0 %all-to-all-done.qd = bf16[8,128,1024]{2,1,0:T(8,128)(2,1)} async-done(((bf16[8,128,1024]{2,1,0:T(8,128)(2,1)}), bf16[8,128,1024]{2,1,0:T(8,128)(2,1)}, u32[]{:S(2)}, u32[]{:S(2)}) %all-to-all-start) | async-done | bytes 2097184 | tf_op jit(solution)/shard_map/all_to_all | solution.py:192
  47.2 9.8 %shard_map.92 = (bf16[8,128,512]{2,1,0:T(8,128)(2,1)}, f32[16,512]{1,0:T(8,128)}) custom-call(bf16[8,128,1024]{2,1,0:T(8,128)(2,1)} %all-to-all-done.qd, bf16[1024,256]{1,0:T(8,128)(2,1)} %all_gather.3.kv), custom_call_target="tpu_custom_call" | custom-call | flops 10000000000 | bytes 6000000 | tf_op jit(solution)/shard_map/pallas_call | solution.py:176
  57.8 8.9 %all_to_all.35.stats_ref = f32[8,16,512]{2,1,0:T(8,128)} all-to-all(f32[8,16,512]{2,1,0:T(8,128)S(1)} %broadcast_in_dim.48), channel_id=1, replica_groups=mesh['x'=4,'z'=8,'yl'=2,'yh'=2,'core'=2] {'x','yl'}, dimensions={0} | all-to-all | bytes 524288 | tf_op jit(solution)/shard_map/all_to_all | solution.py:192
  66.7 3.6 %all-to-all-start.2 = ((bf16[8,128,512]{2,1,0:T(8,128)(2,1)}), bf16[8,128,512]{2,1,0:T(8,128)(2,1)S(1)}, u32[]{:S(2)}, u32[]{:S(2)}) async-start(bf16[8,128,512]{2,1,0:T(8,128)(2,1)} %get-tuple-element.31), calls=%async_computation.2 | async-start | bytes 2097152 | tf_op jit(solution)/shard_map/all_to_all | solution.py:192
  70.2 14.5 %shard_map.93 = (bf16[8,128,512]{2,1,0:T(8,128)(2,1)}, bf16[1024,256]{1,0:T(8,128)(2,1)}) custom-call(bf16[8,128,1024]{2,1,0:T(8,128)(2,1)} %all-to-all-done.qd, f32[8,16,512]{2,1,0:T(8,128)} %all_to_all.35.stats_ref, bf16[1024,256]{1,0:T(8,128)(2,1)} %all_gather.3.kv), custom_call_target="tpu_custom_call" | custom-call | flops 16000000000 | bytes 6000000 | tf_op jit(solution)/shard_map/pallas_call | solution.py:176
  84.7 9.1 %all-to-all-start.3 = ((bf16[8,128,256]{2,1,0:T(8,128)(2,1)}), bf16[8,128,256]{2,1,0:T(8,128)(2,1)S(1)}, u32[]{:S(2)}, u32[]{:S(2)}) async-start(bf16[8,128,256]{2,1,0:T(8,128)(2,1)} %bitcast.37), calls=%async_computation.3 | async-start | bytes 1048576 | tf_op jit(solution)/shard_map/all_to_all | solution.py:192
  94.5 4.1 %shard_map.94 = (bf16[128,1536]{1,0:T(8,128)(2,1)}, bf16[512,768]{1,0:T(8,128)(2,1)}, bf16[512,768]{1,0:T(8,128)(2,1)}) custom-call(s32[2]{0:T(128)} %pad_add_fusion.place, bf16[8,128,512]{2,1,0:T(8,128)(2,1)} %copy-done.2, f32[8,16,512]{2,1,0:T(8,128)} %all_to_all.35.stats_ref, bf16[128,1536]{1,0:T(8,128)(2,1)} %bitcast.30, bf16[128,1536]{1,0:T(8,128)(2,1)} %bitcast.34, ...), custom_call_target="tpu_custom_call" | custom-call | flops 600000000 | bytes 6000000 | tf_op jit(solution)/shard_map/pallas_call | solution.py:176
  98.6 9.6 %all-to-all-done.3.dkv_ref = bf16[8,128,256]{2,1,0:T(8,128)(2,1)S(1)} async-done(((bf16[8,128,256]{2,1,0:T(8,128)(2,1)}), bf16[8,128,256]{2,1,0:T(8,128)(2,1)S(1)}, u32[]{:S(2)}, u32[]{:S(2)}) %all-to-all-start.3) | async-done | bytes 524320 | tf_op jit(solution)/shard_map/all_to_all | solution.py:192
  108.2 4.1 %collective-permute-start = (bf16[512,768]{1,0:T(8,128)(2,1)}, bf16[512,768]{1,0:T(8,128)(2,1)S(1)}, u32[]{:S(2)}, u32[]{:S(2)}) collective-permute-start(bf16[512,768]{1,0:T(8,128)(2,1)} %get-tuple-element.38), channel_id=1, source_target_pairs={{0,1},{1,0},{2,3},{3,2},{4,5},{5,4},{6,7},{7,6},{8,9},{9,8},{10,11... | collective-permute-start | bytes 2359304 | tf_op jit(solution)/shard_map/ppermute | solution.py:35
  112.3 2.1 %collective-permute-done = bf16[512,768]{1,0:T(8,128)(2,1)S(1)} collective-permute-done((bf16[512,768]{1,0:T(8,128)(2,1)}, bf16[512,768]{1,0:T(8,128)(2,1)S(1)}, u32[]{:S(2)}, u32[]{:S(2)}) %collective-permute-start) | collective-permute-done | bytes 786464 | tf_op jit(solution)/shard_map/ppermute | solution.py:35
  118.2 20.3 %all_to_all.36.dq_ref = bf16[8,128,512]{2,1,0:T(8,128)(2,1)} all-to-all(bf16[8,128,512]{2,1,0:T(8,128)(2,1)S(1)} %copy-done.6), channel_id=1, replica_groups=mesh['x'=4,'z'=8,'yl'=2,'yh'=2,'core'=2] {'x','yl'}, dimensions={0} | all-to-all | bytes 2097152 | tf_op jit(solution)/shard_map/all_to_all | solution.py:192
  138.5 5.0 %shard_map.95 = (bf16[128,1536]{1,0:T(8,128)(2,1)}, bf16[1536,384]{1,0:T(8,128)(2,1)}, bf16[1536,384]{1,0:T(8,128)(2,1)}) custom-call(s32[2]{0:T(128)} %pad_add_fusion.place, bf16[8,128,512]{2,1,0:T(8,128)(2,1)} %all_to_all.36.dq_ref, bf16[8,128,256]{2,1,0:T(8,128)(2,1)} %copy-done.4, bf16[128,1536]{1,0:T(8,128)(2,1)} %bitcast.31, ...), custom_call_target="tpu_custom_call" | custom-call | flops 900000000 | bytes 6000000 | tf_op jit(solution)/shard_map/pallas_call | solution.py:176
  143.5 2.1 %collective-permute-start.1 = (bf16[1536,384]{1,0:T(8,128)(2,1)}, bf16[1536,384]{1,0:T(8,128)(2,1)S(1)}, u32[]{:S(2)}, u32[]{:S(2)}) collective-permute-start(bf16[1536,384]{1,0:T(8,128)(2,1)} %get-tuple-element.44), channel_id=1, source_target_pairs={{0,1},{1,0},{2,3},{3,2},{4,5},{5,4},{6,7},{7,6},{8,9},{9,8},{10,11... | collective-permute-start | bytes 3538952 | tf_op jit(solution)/shard_map/ppermute | solution.py:35
  145.6 2.7 %collective-permute-done.1 = bf16[1536,384]{1,0:T(8,128)(2,1)S(1)} collective-permute-done((bf16[1536,384]{1,0:T(8,128)(2,1)}, bf16[1536,384]{1,0:T(8,128)(2,1)S(1)}, u32[]{:S(2)}, u32[]{:S(2)}) %collective-permute-start.1) | collective-permute-done | bytes 1179680 | tf_op jit(solution)/shard_map/ppermute | solution.py:35
  148.3 1.6 add_convert_fusion
  153.1 4.0 %all-to-all-start.5 = ((bf16[4,448,384]{2,1,0:T(8,128)(2,1)}), bf16[4,448,384]{2,1,0:T(8,128)(2,1)S(1)}, u32[]{:S(2)}, u32[]{:S(2)}) async-start(bf16[4,448,384]{2,1,0:T(8,128)(2,1)} %pad_maximum_fusion), calls=%async_computation.6 | async-start | bytes 2752512 | tf_op jit(solution)/shard_map/all_to_all | solution.py:192
  157.2 17.6 %all-to-all-done.5 = bf16[4,448,384]{2,1,0:T(8,128)(2,1)S(1)} async-done(((bf16[4,448,384]{2,1,0:T(8,128)(2,1)}), bf16[4,448,384]{2,1,0:T(8,128)(2,1)S(1)}, u32[]{:S(2)}, u32[]{:S(2)}) %all-to-all-start.5) | async-done | bytes 1376288 | tf_op jit(solution)/shard_map/all_to_all | solution.py:192
  175.2 14.7 %all_to_all.37 = bf16[16,32,384]{2,1,0:T(8,128)(2,1)S(1)} all-to-all(bf16[16,32,384]{2,1,0:T(8,128)(2,1)S(1)} %pad_maximum_fusion.1), channel_id=1, replica_groups=mesh['x'=4,'z'=8,'yl'=2,'yh'=2,'core'=2] {'z','yl'}, dimensions={0} | all-to-all | bytes 786432 | tf_op jit(solution)/shard_map/all_to_all | solution.py:192
  190.0 3.1 %collective-permute-start.2 = (f32[32,384]{1,0:T(8,128)S(1)}, f32[32,384]{1,0:T(8,128)S(1)}, u32[]{:S(2)}, u32[]{:S(2)}) collective-permute-start(f32[32,384]{1,0:T(8,128)S(1)} %convert_reduce_fusion.1), channel_id=1, source_target_pairs={{0,2},{2,0},{1,3},{3,1},{4,6},{6,4},{5,7},{7,5},{8,10},{10,8},{9,1... | collective-permute-start | bytes 147464 | tf_op jit(solution)/shard_map/ppermute | solution.py:35
  193.1 1.6 collective-permute-done.2
  194.7 4.8 %collective-permute-start.3 = (f32[40,384]{1,0:T(8,128)S(1)}, f32[40,384]{1,0:T(8,128)S(1)}, u32[]{:S(2)}, u32[]{:S(2)}) collective-permute-start(f32[40,384]{1,0:T(8,128)S(1)} %pad_maximum_fusion.3), channel_id=1, source_target_pairs={{0,1},{1,0},{2,3},{3,2},{4,5},{5,4},{6,7},{7,6},{8,9},{9,8},{10,11... | collective-permute-start | bytes 184328 | tf_op jit(solution)/shard_map/ppermute | solution.py:35
  (50 shorter events, 14.1 us)
Async XLA Ops:
  7.2 2.1 copy-start.1
  7.2 2.1 copy-start.5
  11.5 6.0 %copy-start = (bf16[1,128,1536]{2,1,0:T(8,128)(2,1)S(1)}, bf16[1,128,1536]{2,1,0:T(8,128)(2,1)}, u32[]{:S(2)}) copy-start(bf16[1,128,1536]{2,1,0:T(8,128)(2,1)} %param.5) | copy-start | bytes 1179652
  11.5 6.0 %copy-start.3 = (bf16[1536,256]{1,0:T(8,128)(2,1)S(1)}, bf16[1536,256]{1,0:T(8,128)(2,1)}, u32[]{:S(2)}) copy-start(bf16[1536,256]{1,0:T(8,128)(2,1)} %w_keyval_ref.1) | copy-start | bytes 2359300
  11.5 35.7 %all-to-all-start = ((bf16[8,128,1024]{2,1,0:T(8,128)(2,1)}), bf16[8,128,1024]{2,1,0:T(8,128)(2,1)}, u32[]{:S(2)}, u32[]{:S(2)}) async-start(bf16[8,128,1024]{2,1,0:T(8,128)(2,1)} %broadcast_in_dim.47), calls=%async_computation | async-start | bytes 4194304 | tf_op jit(solution)/shard_map/all_to_all | solution.py:192
  66.7 18.1 %all-to-all-start.2 = ((bf16[8,128,512]{2,1,0:T(8,128)(2,1)}), bf16[8,128,512]{2,1,0:T(8,128)(2,1)S(1)}, u32[]{:S(2)}, u32[]{:S(2)}) async-start(bf16[8,128,512]{2,1,0:T(8,128)(2,1)} %get-tuple-element.31), calls=%async_computation.2 | async-start | bytes 2097152 | tf_op jit(solution)/shard_map/all_to_all | solution.py:192
  84.7 9.8 %copy-start.2 = (bf16[8,128,512]{2,1,0:T(8,128)(2,1)}, bf16[8,128,512]{2,1,0:T(8,128)(2,1)S(1)}, u32[]{:S(2)}) copy-start(bf16[8,128,512]{2,1,0:T(8,128)(2,1)S(1)} %all-to-all-done.2.parts) | copy-start | bytes 3145732
  84.7 23.4 %all-to-all-start.3 = ((bf16[8,128,256]{2,1,0:T(8,128)(2,1)}), bf16[8,128,256]{2,1,0:T(8,128)(2,1)S(1)}, u32[]{:S(2)}, u32[]{:S(2)}) async-start(bf16[8,128,256]{2,1,0:T(8,128)(2,1)} %bitcast.37), calls=%async_computation.3 | async-start | bytes 1048576 | tf_op jit(solution)/shard_map/all_to_all | solution.py:192
  93.8 57.0 %reduce-scatter.2.cloned.1.call-start = ((), (), s32[]{:S(2)}) async-start(), calls=%async_computation.8 | async-start | bytes 1966080 | tf_op jit(solution)/shard_map/reduce_scatter | solution.py:269
  108.2 7.5 %copy-start.4 = (bf16[8,128,256]{2,1,0:T(8,128)(2,1)}, bf16[8,128,256]{2,1,0:T(8,128)(2,1)S(1)}, u32[]{:S(2)}) copy-start(bf16[8,128,256]{2,1,0:T(8,128)(2,1)S(1)} %all-to-all-done.3.dkv_ref) | copy-start | bytes 1572868
  108.2 6.2 %collective-permute-start = (bf16[512,768]{1,0:T(8,128)(2,1)}, bf16[512,768]{1,0:T(8,128)(2,1)S(1)}, u32[]{:S(2)}, u32[]{:S(2)}) collective-permute-start(bf16[512,768]{1,0:T(8,128)(2,1)} %get-tuple-element.38), channel_id=1, source_target_pairs={{0,1},{1,0},{2,3},{3,2},{4,5},{5,4},{6,7},{7,6},{8,9},{9,8},{10,11... | collective-permute-start | bytes 2359304 | tf_op jit(solution)/shard_map/ppermute | solution.py:35
  117.0 1.2 copy-start.6
  143.5 4.8 %collective-permute-start.1 = (bf16[1536,384]{1,0:T(8,128)(2,1)}, bf16[1536,384]{1,0:T(8,128)(2,1)S(1)}, u32[]{:S(2)}, u32[]{:S(2)}) collective-permute-start(bf16[1536,384]{1,0:T(8,128)(2,1)} %get-tuple-element.44), channel_id=1, source_target_pairs={{0,1},{1,0},{2,3},{3,2},{4,5},{5,4},{6,7},{7,6},{8,9},{9,8},{10,11... | collective-permute-start | bytes 3538952 | tf_op jit(solution)/shard_map/ppermute | solution.py:35
  153.1 21.7 %all-to-all-start.5 = ((bf16[4,448,384]{2,1,0:T(8,128)(2,1)}), bf16[4,448,384]{2,1,0:T(8,128)(2,1)S(1)}, u32[]{:S(2)}, u32[]{:S(2)}) async-start(bf16[4,448,384]{2,1,0:T(8,128)(2,1)} %pad_maximum_fusion), calls=%async_computation.6 | async-start | bytes 2752512 | tf_op jit(solution)/shard_map/all_to_all | solution.py:192
  190.0 4.7 %collective-permute-start.2 = (f32[32,384]{1,0:T(8,128)S(1)}, f32[32,384]{1,0:T(8,128)S(1)}, u32[]{:S(2)}, u32[]{:S(2)}) collective-permute-start(f32[32,384]{1,0:T(8,128)S(1)} %convert_reduce_fusion.1), channel_id=1, source_target_pairs={{0,2},{2,0},{1,3},{3,1},{4,6},{6,4},{5,7},{7,5},{8,10},{10,8},{9,1... | collective-permute-start | bytes 147464 | tf_op jit(solution)/shard_map/ppermute | solution.py:35
  194.7 5.7 %collective-permute-start.3 = (f32[40,384]{1,0:T(8,128)S(1)}, f32[40,384]{1,0:T(8,128)S(1)}, u32[]{:S(2)}, u32[]{:S(2)}) collective-permute-start(f32[40,384]{1,0:T(8,128)S(1)} %pad_maximum_fusion.3), channel_id=1, source_target_pairs={{0,1},{1,0},{2,3},{3,2},{4,5},{5,4},{6,7},{7,6},{8,9},{9,8},{10,11... | collective-permute-start | bytes 184328 | tf_op jit(solution)/shard_map/ppermute | solution.py:35
Sparse Core Ops, SparseCore 0:
  117.1 33.6 reduce-scatter.1

commit v3 on v2

--- a/solution.py
+++ b/solution.py
@@ -91,7 +91,7 @@
     return top + jnp.log(total), jnp.sum(weights * bars, axis=0), weights
 
 
-def backward_kernel(qd, stats_ref, kv, dq, dkv_out, kt, stat, dkv, *scratch):
+def backward_kernel(qd, stats_ref, kv, dq, dkv, kt, stat, *scratch):
     kt[...] = kv[:, :HEAD_DIM].T
     logsum, delta, unused = combine(stats_ref[:, :8, :], stats_ref[:, 8:, :])
     stat[:8, :] = logsum * LOG2E
@@ -125,8 +125,7 @@
         return carry
 
     lax.fori_loop(0, GROUP, block, 0)
-    dkv_out[:, :HEAD_DIM] = (dkv[:, :HEAD_DIM] * SCALE).astype(BF16)
-    dkv_out[:, HEAD_DIM:] = dkv[:, HEAD_DIM:].astype(BF16)
+    dkv[:, :HEAD_DIM] = dkv[:, :HEAD_DIM] * SCALE
 
 
 def output_kernel(place, parts, stats_ref, tokens_ref, upstream_ref, w_out_ref, *outs):
@@ -149,16 +148,14 @@
     give_ref[...] = dot(mixed_rows, jnp.where(first, high, low)).astype(BF16)
 
 
-def input_kernel(place, dq_ref, dkv_ref, tokens_ref, w_query_ref, w_keyval_ref, *outs):
-    grad_ref, keep_ref, give_ref = outs
+def input_kernel(place, dq_ref, dkv_ref, tokens_ref, both_ref, keep_ref, give_ref):
     dq_t = jnp.sum(dq_ref[...].astype(F32), axis=0)
     dquery = jnp.concatenate(
         [dq_t[:, h * POS : (h + 1) * POS].T for h in range(HEADS)], axis=1
     ).astype(BF16)
-    dkeyval = jnp.sum(dkv_ref[...].astype(F32), axis=0).astype(BF16)
-    grad_ref[...] = (
-        dot(dquery, w_query_ref[...], NT) + dot(dkeyval, w_keyval_ref[...], NT)
-    ).astype(BF16)
+    dkeyval = dkv_ref[...].astype(BF16)
+    both_ref[:, :ROWS] = dquery
+    both_ref[:, ROWS:] = dkeyval
     first = place[0] == 0
     q_low, q_high = dquery[:, :256], dquery[:, 256:]
     kv_low, kv_high = dkeyval[:, :128], dkeyval[:, 128:]
@@ -166,6 +163,17 @@
     high = jnp.concatenate([q_high, kv_high], axis=1)
     keep_ref[...] = dot(tokens_ref[...], jnp.where(first, low, high), TN).astype(BF16)
     give_ref[...] = dot(tokens_ref[...], jnp.where(first, high, low), TN).astype(BF16)
+
+
+def tokens_kernel(both_ref, w_query_ref, w_keyval_ref, grad_ref):
+    grad_ref[...] = (
+        dot(both_ref[:, :ROWS], w_query_ref[...], NT)
+        + dot(both_ref[:, ROWS:], w_keyval_ref[...], NT)
+    ).astype(BF16)
+
+
+def plus(a, b):
+    return (a.astype(F32) + b.astype(F32)).astype(BF16)
 
 
 VM = pl.BlockSpec(memory_space=pltpu.VMEM)
@@ -198,10 +206,6 @@
 
 def added(blocks):
     return jnp.sum(blocks.astype(F32), axis=0)
-
-
-def plus(a, b):
-    return (a.astype(F32) + b.astype(F32)).astype(BF16)
 
 
 def body(tokens, upstream, w_query, w_keyval, w_out):
@@ -239,19 +243,18 @@
     dq_parts, dkv_parts = call(
         backward_kernel,
         [qds, all_stats, kvs],
-        [shape(8, HEAD_DIM, ROWS), shape(KEYS, 2 * HEAD_DIM)],
+        [shape(8, HEAD_DIM, ROWS), shape(KEYS, 2 * HEAD_DIM, dtype=F32)],
         [VM] * 3,
         [VM] * 2,
         [
             pltpu.VMEM((HEAD_DIM, KEYS), BF16),
             pltpu.VMEM((16, ROWS), F32),
-            pltpu.VMEM((KEYS, 2 * HEAD_DIM), F32),
         ]
         + [pltpu.VMEM((CHUNK, ROWS), t) for t in (F32, F32, BF16, BF16)] * (KEYS // CHUNK),
         16_000_000_000,
     )
-    dq_parts, dkv_parts, mine = lax.optimization_barrier((dq_parts, dkv_parts, mine))
-    dkv = swap(dkv_parts.reshape(8, POS, 2 * HEAD_DIM), "z")
+    dq_parts, mine = lax.optimization_barrier((dq_parts, mine))
+    dkv = lax.psum_scatter(dkv_parts, "z", scatter_dimension=0, tiled=True)
     attended, keep_o, give_o = call(
         output_kernel,
         [place, mine, all_stats, local, cotangent, w_out],
@@ -261,42 +264,42 @@
         [],
         600_000_000,
     )
-    give_o, dkv, dq_parts = lax.optimization_barrier((give_o, dkv, dq_parts))
-    term_o = keep_o.astype(F32) + send(give_o, "core", 2, 1).astype(F32)
+    term_o = plus(keep_o, send(give_o, "core", 2, 1))
+    term_o, dq_parts = lax.optimization_barrier((term_o, dq_parts))
     dqs = swap(dq_parts, ("x", "yl"))
-    unused, dqs = lax.optimization_barrier((term_o, dqs))
-    term_o = term_o.reshape(32, 2, 8, 2, 384).transpose(3, 1, 0, 2, 4).reshape(1024, 384)
-    term_o = lax.psum_scatter(term_o, ("yh", "yl"), scatter_dimension=0, tiled=True)
-
-    grad_tokens, keep_i, give_i = call(
+    term_o = added(swap(term_o.reshape(4, 128, 768), "x"))
+    term_o = term_o.reshape(16, 8, 2, 384).transpose(0, 2, 1, 3).reshape(16, 16, 384)
+    dkv, term_o = lax.optimization_barrier((dkv, term_o))
+
+    both, keep_i, give_i = call(
         input_kernel,
-        [place, dqs, dkv, local, w_query, w_keyval],
-        [shape(*local.shape), shape(1536, 384), shape(1536, 384)],
-        [SM] + [VM] * 5,
+        [place, dqs, dkv, local],
+        [shape(POS, 768), shape(1536, 384), shape(1536, 384)],
+        [SM] + [VM] * 3,
         [VM] * 3,
         [],
-        900_000_000,
-    )
-    term_i = plus(keep_i, send(give_i, "core", 2, 1)).reshape(4, 384, 384)
-    terms = jnp.concatenate([term_i, term_o.astype(BF16).reshape(4, 64, 384)], axis=1)
-    terms = added(swap(terms, "x"))
-    term_i = terms[:384].reshape(8, 2, 24, 384)
-    here = (jnp.arange(2) == lax.axis_index("yl"))[None, :, None, None]
-    term_o = jnp.where(here, terms[384:].reshape(8, 1, 8, 384), 0.0)
-    ends = jnp.concatenate([term_i, term_o], axis=2).astype(BF16).reshape(16, 32, 384)
+        600_000_000,
+    )
+    term_i = plus(keep_i, send(give_i, "core", 2, 1))
+    grad_tokens = call(
+        tokens_kernel,
+        [both, w_query, w_keyval],
+        shape(*local.shape),
+        [VM] * 3,
+        VM,
+        [],
+        300_000_000,
+    )
+    term_i = swap(term_i.reshape(4, 384, 384), "x")
+    grad_tokens, term_i = lax.optimization_barrier((grad_tokens, term_i))
+    term_i = added(term_i)
+    ends = jnp.concatenate([term_i.reshape(16, 24, 384), term_o], axis=1).astype(BF16)
     ends = added(swap(ends, ("z", "yl")))
-    got = send(ends, "yh", 2, 1)
-    yh = lax.axis_index("yh")
-    ends = jnp.concatenate(
-        [
-            ends[:24] + got[:24],
-            jnp.where(yh == 0, ends[24:], got[24:]),
-            jnp.where(yh == 0, got[24:], ends[24:]),
-        ]
-    )
+    ends = ends + send(ends, "yh", 2, 1)
     other = send(ends, "core", 2, 1)
     low, high = jnp.where(core == 0, ends, other), jnp.where(core == 0, other, ends)
-    grad_o = jnp.concatenate([low[24:32], low[32:], high[24:32], high[32:]], axis=1)
+    grad_o = jnp.stack([low[24:], high[24:]]).reshape(2, 2, 8, 384)
+    grad_o = grad_o.transpose(2, 0, 1, 3).reshape(8, 1536)
     return (
         attended[None],
         grad_tokens[None],

time: 210 us -> 206 us (0.981)
  blocking collectives: 70.2 us -> 61.2 us
  waiting for transfers between devices: 38.3 us -> 42.7 us
  other arithmetic: 8.02 us -> 5.81 us
    reduce_scatter x1, waiting for transfers between devices: 0.86 us -> 13.4 us  [body(): dkv = lax.psum_scatter(dkv_parts, 'z', scatter_dimension=0, tiled=True)]
    all_to_all x3 -> x2, blocking collectives: 43.8 us -> 34.8 us  [swap(): return lax.all_to_all(blocks, axes, 0, 0)]
    all_to_all x4 -> x5, waiting for transfers between devices: 30.1 us -> 21.5 us  [swap(): return lax.all_to_all(blocks, axes, 0, 0)]
    ppermute x4, starting transfers between devices: 14.2 us -> 17.1 us  [send(): lax.ppermute(array, axis, [(i, (i + step) % size) for i in range(size)])]
    all_to_all x4 -> x5, starting transfers between devices: 22.7 us -> 20.5 us  [swap(): return lax.all_to_all(blocks, axes, 0, 0)]
    pallas_call x4 -> x5, Pallas kernels: 33.5 us -> 35.4 us  [call(): pl.pallas_call(kernel, out_shape=outs, in_specs=in_specs, out_specs=out_s...]
  transfers between devices with their start and end apart: 9 -> 10, of which waited for: 8 -> 9; matrix products, arithmetic and copies ran while one was open for 1% -> 1% of each run, Pallas kernels for 11% -> 9%
where the time goes in v3:
time: 206 us; the launch traced here: 205 us
  blocking collectives  61.2 us (30%)
  waiting for transfers between devices  42.7 us (21%)
  starting transfers between devices  37.7 us (18%)
  Pallas kernels  35.4 us (17%)
  between operations  14.2 us (7%)
  other arithmetic  5.81 us (3%)
  local copies, waits for them, and re-layouts  5.1 us (2%)
  matrix products  2.94 us (1%)
    pallas_call x5, Pallas kernels, call(): pl.pallas_call(kernel, out_shape=outs, in_specs=in_specs, out_specs=out_s...  35.4 us
    all_to_all x2, blocking collectives, swap(): return lax.all_to_all(blocks, axes, 0, 0)  34.8 us
    all_gather x1, blocking collectives, body(): kvs = lax.all_gather(keyval, 'z', axis=0, tiled=True)  26.4 us
    all_to_all x5, waiting for transfers between devices, swap(): return lax.all_to_all(blocks, axes, 0, 0)  21.5 us
    all_to_all x5, starting transfers between devices, swap(): return lax.all_to_all(blocks, axes, 0, 0)  20.5 us
    ppermute x4, starting transfers between devices, send(): lax.ppermute(array, axis, [(i, (i + step) % size) for i in range(size)])  17.1 us
    reduce_scatter x1, waiting for transfers between devices, body(): dkv = lax.psum_scatter(dkv_parts, 'z', scatter_dimension=0, tiled=True)  13.4 us
    ppermute x4, waiting for transfers between devices, send(): lax.ppermute(array, axis, [(i, (i + step) % size) for i in range(size)])  7.89 us
  transfers between devices with their start and end apart: 10, of which 9 were waited for; matrix products, arithmetic and copies ran while one was open for 1% of the time, Pallas kernels for 9%

profile of v3, /device:TPU:1, one launch (start us, length us, event | category | flops | bytes accessed | tf_op | source)
XLA Modules:
  0.0 205.1 jit_solution(8800754434094203663)
XLA Ops:
  7.2 2.3 %convolution_convert_fusion = bf16[128,512]{1,0:T(8,128)(2,1)S(1)} fusion(bf16[512,1536]{1,0:T(8,128)(2,1)} %w_out_ref.1, bf16[1,128,1536]{2,1,0:T(8,128)(2,1)} %param.6), kind=kOutput, calls=%fused_computation.3 | convolution fusion | flops 201392128 | bytes 2097152 | tf_op jit(solution)/shard_map/dot_general | solution.py:218
  11.5 6.0 %all-to-all-start = ((bf16[8,128,1024]{2,1,0:T(8,128)(2,1)}), bf16[8,128,1024]{2,1,0:T(8,128)(2,1)}, u32[]{:S(2)}, u32[]{:S(2)}) async-start(bf16[8,128,1024]{2,1,0:T(8,128)(2,1)} %broadcast_in_dim.8), calls=%async_computation | async-start | bytes 4194304 | tf_op jit(solution)/shard_map/all_to_all | solution.py:200
  17.8 26.4 %all_gather.3.kv = bf16[1024,256]{1,0:T(8,128)(2,1)} all-gather(bf16[128,256]{1,0:T(8,128)(2,1)S(1)} %convolution_convert_fusion.2), channel_id=1, replica_groups=mesh['x'=4,'z'=8,'yl'=2,'yh'=2,'core'=2] {'z'}, dimensions={0}, use_global_device_ids=true | all-gather | bytes 589824 | tf_op jit(solution)/shard_map/all_gather | solution.py:223
  44.2 3.0 %all-to-all-done.qd = bf16[8,128,1024]{2,1,0:T(8,128)(2,1)} async-done(((bf16[8,128,1024]{2,1,0:T(8,128)(2,1)}), bf16[8,128,1024]{2,1,0:T(8,128)(2,1)}, u32[]{:S(2)}, u32[]{:S(2)}) %all-to-all-start) | async-done | bytes 2097184 | tf_op jit(solution)/shard_map/all_to_all | solution.py:200
  47.2 9.8 %shard_map.92 = (bf16[8,128,512]{2,1,0:T(8,128)(2,1)}, f32[16,512]{1,0:T(8,128)}) custom-call(bf16[8,128,1024]{2,1,0:T(8,128)(2,1)} %all-to-all-done.qd, bf16[1024,256]{1,0:T(8,128)(2,1)} %all_gather.3.kv), custom_call_target="tpu_custom_call" | custom-call | flops 10000000000 | bytes 6000000 | tf_op jit(solution)/shard_map/pallas_call | solution.py:184
  58.5 3.4 %all-to-all-start.1 = ((f32[8,16,512]{2,1,0:T(8,128)}), f32[8,16,512]{2,1,0:T(8,128)S(1)}, u32[]{:S(2)}, u32[]{:S(2)}) async-start(f32[8,16,512]{2,1,0:T(8,128)} %broadcast_in_dim.9), calls=%async_computation.1 | async-start | bytes 524288 | tf_op jit(solution)/shard_map/all_to_all | solution.py:200
  62.5 5.1 %all-to-all-done.1.stats_ref = f32[8,16,512]{2,1,0:T(8,128)S(1)} async-done(((f32[8,16,512]{2,1,0:T(8,128)}), f32[8,16,512]{2,1,0:T(8,128)S(1)}, u32[]{:S(2)}, u32[]{:S(2)}) %all-to-all-start.1) | async-done | bytes 262176 | tf_op jit(solution)/shard_map/all_to_all | solution.py:200
  67.6 3.6 %all-to-all-start.2 = ((bf16[8,128,512]{2,1,0:T(8,128)(2,1)}), bf16[8,128,512]{2,1,0:T(8,128)(2,1)S(1)}, u32[]{:S(2)}, u32[]{:S(2)}) async-start(bf16[8,128,512]{2,1,0:T(8,128)(2,1)} %get-tuple-element.31), calls=%async_computation.2 | async-start | bytes 2097152 | tf_op jit(solution)/shard_map/all_to_all | solution.py:200
  71.3 14.6 %shard_map.93 = (bf16[8,128,512]{2,1,0:T(8,128)(2,1)}, f32[1024,256]{1,0:T(8,128)}) custom-call(bf16[8,128,1024]{2,1,0:T(8,128)(2,1)} %all-to-all-done.qd, f32[8,16,512]{2,1,0:T(8,128)} %copy-done.5, bf16[1024,256]{1,0:T(8,128)(2,1)} %all_gather.3.kv), custom_call_target="tpu_custom_call" | custom-call | flops 16000000000 | bytes 6000000 | tf_op jit(solution)/shard_map/pallas_call | solution.py:184
  86.8 4.1 %shard_map.94 = (bf16[128,1536]{1,0:T(8,128)(2,1)}, bf16[512,768]{1,0:T(8,128)(2,1)}, bf16[512,768]{1,0:T(8,128)(2,1)}) custom-call(s32[2]{0:T(128)} %pad_add_fusion.place, bf16[8,128,512]{2,1,0:T(8,128)(2,1)} %copy-done.1, f32[8,16,512]{2,1,0:T(8,128)} %copy-done.5, bf16[128,1536]{1,0:T(8,128)(2,1)} %bitcast.29, bf16[128,1536]{1,0:T(8,128)(2,1)} %bitcast.33, ...), custom_call_target="tpu_custom_call" | custom-call | flops 600000000 | bytes 6000000 | tf_op jit(solution)/shard_map/pallas_call | solution.py:184
  91.0 6.1 %collective-permute-start = (bf16[512,768]{1,0:T(8,128)(2,1)}, bf16[512,768]{1,0:T(8,128)(2,1)S(1)}, u32[]{:S(2)}, u32[]{:S(2)}) collective-permute-start(bf16[512,768]{1,0:T(8,128)(2,1)} %get-tuple-element.35), channel_id=1, source_target_pairs={{0,1},{1,0},{2,3},{3,2},{4,5},{5,4},{6,7},{7,6},{8,9},{9,8},{10,11... | collective-permute-start | bytes 2359304 | tf_op jit(solution)/shard_map/ppermute | solution.py:35
  99.4 15.6 %all_to_all.35 = bf16[4,128,768]{2,1,0:T(8,128)(2,1)S(1)} all-to-all(bf16[4,128,768]{2,1,0:T(8,128)(2,1)S(1)} %bitcast.32), channel_id=1, replica_groups=mesh['x'=4,'z'=8,'yl'=2,'yh'=2,'core'=2] {'x'}, dimensions={0} | all-to-all | bytes 1572864 | tf_op jit(solution)/shard_map/all_to_all | solution.py:200
  115.0 3.6 %all-to-all-start.3 = ((bf16[8,128,512]{2,1,0:T(8,128)(2,1)}), bf16[8,128,512]{2,1,0:T(8,128)(2,1)S(1)}, u32[]{:S(2)}, u32[]{:S(2)}) async-start(bf16[8,128,512]{2,1,0:T(8,128)(2,1)} %get-tuple-element.37), calls=%async_computation.3 | async-start | bytes 2097152 | tf_op jit(solution)/shard_map/all_to_all | solution.py:200
  118.6 13.4 %reduce-scatter.2.cloned.1.call-done.dkv_ref = f32[128,256]{1,0:T(8,128)} async-done(((f32[1024,256]{1,0:T(8,128)}), f32[128,256]{1,0:T(8,128)}) %reduce-scatter.2.cloned.1.call-update) | async-done | bytes 131088 | tf_op jit(solution)/shard_map/reduce_scatter | solution.py:257
  133.7 3.6 %shard_map.95 = (bf16[128,768]{1,0:T(8,128)(2,1)}, bf16[1536,384]{1,0:T(8,128)(2,1)}, bf16[1536,384]{1,0:T(8,128)(2,1)}) custom-call(s32[2]{0:T(128)} %pad_add_fusion.place, bf16[8,128,512]{2,1,0:T(8,128)(2,1)} %copy-done.4, f32[128,256]{1,0:T(8,128)} %reduce-scatter.2.cloned.1.call-done.dkv_ref, bf16[128,1536]{1,0:T(8,128)(2,1)} %bitcast.30), custom_call_target="tpu_custom_call" | custom-call | flops 600000000 | bytes 6000000 | tf_op jit(solution)/shard_map/pallas_call | solution.py:184
  137.3 4.0 %collective-permute-start.1 = (bf16[1536,384]{1,0:T(8,128)(2,1)}, bf16[1536,384]{1,0:T(8,128)(2,1)S(1)}, u32[]{:S(2)}, u32[]{:S(2)}) collective-permute-start(bf16[1536,384]{1,0:T(8,128)(2,1)} %get-tuple-element.43), channel_id=1, source_target_pairs={{0,1},{1,0},{2,3},{3,2},{4,5},{5,4},{6,7},{7,6},{8,9},{9,8},{10,11... | collective-permute-start | bytes 3538952 | tf_op jit(solution)/shard_map/ppermute | solution.py:35
  141.3 2.7 %collective-permute-done.1 = bf16[1536,384]{1,0:T(8,128)(2,1)S(1)} collective-permute-done((bf16[1536,384]{1,0:T(8,128)(2,1)}, bf16[1536,384]{1,0:T(8,128)(2,1)S(1)}, u32[]{:S(2)}, u32[]{:S(2)}) %collective-permute-start.1) | collective-permute-done | bytes 1179680 | tf_op jit(solution)/shard_map/ppermute | solution.py:35
  144.0 2.6 %add_convert_fusion = bf16[1536,384]{1,0:T(8,128)(2,1)} fusion(bf16[1536,384]{1,0:T(8,128)(2,1)S(1)} %collective-permute-done.1, bf16[1536,384]{1,0:T(8,128)(2,1)} %get-tuple-element.42), kind=kLoop, calls=%fused_computation | loop fusion | flops 2359296 | bytes 3538944 | tf_op jit(solution)/shard_map/convert_element_type | solution.py:176
  146.6 4.0 %all-to-all-start.5 = ((bf16[4,384,384]{2,1,0:T(8,128)(2,1)}), bf16[4,384,384]{2,1,0:T(8,128)(2,1)S(1)}, u32[]{:S(2)}, u32[]{:S(2)}) async-start(bf16[4,384,384]{2,1,0:T(8,128)(2,1)} %bitcast.9), calls=%async_computation.6 | async-start | bytes 2359296 | tf_op jit(solution)/shard_map/all_to_all | solution.py:200
  150.6 3.3 %shard_map.96 = bf16[128,1536]{1,0:T(8,128)(2,1)} custom-call(bf16[128,768]{1,0:T(8,128)(2,1)} %get-tuple-element.41.both_ref, bf16[1536,512]{1,0:T(8,128)(2,1)} %w_query_ref.1, bf16[1536,256]{1,0:T(8,128)(2,1)} %w_keyval_ref.1), custom_call_target="tpu_custom_call" | custom-call | flops 300000000 | bytes 6000000 | tf_op jit(solution)/shard_map/pallas_call | solution.py:184
  153.9 12.6 %all-to-all-done.5 = bf16[4,384,384]{2,1,0:T(8,128)(2,1)S(1)} async-done(((bf16[4,384,384]{2,1,0:T(8,128)(2,1)}), bf16[4,384,384]{2,1,0:T(8,128)(2,1)S(1)}, u32[]{:S(2)}, u32[]{:S(2)}) %all-to-all-start.5) | async-done | bytes 1179680 | tf_op jit(solution)/shard_map/all_to_all | solution.py:200
  166.9 19.2 %all_to_all.36 = bf16[16,40,384]{2,1,0:T(8,128)(2,1)S(1)} all-to-all(bf16[16,40,384]{2,1,0:T(8,128)(2,1)S(1)} %pad_maximum_fusion), channel_id=1, replica_groups=mesh['x'=4,'z'=8,'yl'=2,'yh'=2,'core'=2] {'z','yl'}, dimensions={0} | all-to-all | bytes 983040 | tf_op jit(solution)/shard_map/all_to_all | solution.py:200
  186.2 2.5 %collective-permute-start.2 = (f32[40,384]{1,0:T(8,128)S(1)}, f32[40,384]{1,0:T(8,128)S(1)}, u32[]{:S(2)}, u32[]{:S(2)}) collective-permute-start(f32[40,384]{1,0:T(8,128)S(1)} %convert_reduce_fusion.1), channel_id=1, source_target_pairs={{0,2},{2,0},{1,3},{3,1},{4,6},{6,4},{5,7},{7,5},{8,10},{10,8},{9,1... | collective-permute-start | bytes 184328 | tf_op jit(solution)/shard_map/ppermute | solution.py:35
  190.8 4.6 %collective-permute-start.3 = (f32[40,384]{1,0:T(8,128)S(1)}, f32[40,384]{1,0:T(8,128)S(1)}, u32[]{:S(2)}, u32[]{:S(2)}) collective-permute-start(f32[40,384]{1,0:T(8,128)S(1)} %add.17), channel_id=1, source_target_pairs={{0,1},{1,0},{2,3},{3,2},{4,5},{5,4},{6,7},{7,6},{8,9},{9,8},{10,11... | collective-permute-start | bytes 184328 | tf_op jit(solution)/shard_map/ppermute | solution.py:35
  (42 shorter events, 14.9 us)
Async XLA Ops:
  7.2 2.3 %copy-start.2 = (bf16[1,128,1536]{2,1,0:T(8,128)(2,1)S(1)}, bf16[1,128,1536]{2,1,0:T(8,128)(2,1)}, u32[]{:S(2)}) copy-start(bf16[1,128,1536]{2,1,0:T(8,128)(2,1)} %param.5) | copy-start | bytes 1179652
  7.2 2.3 %copy-start = (bf16[1536,512]{1,0:T(8,128)(2,1)S(1)}, bf16[1536,512]{1,0:T(8,128)(2,1)}, u32[]{:S(2)}) copy-start(bf16[1536,512]{1,0:T(8,128)(2,1)} %w_query_ref.1) | copy-start | bytes 4718596
  11.5 6.0 %copy-start.3 = (bf16[1536,256]{1,0:T(8,128)(2,1)S(1)}, bf16[1536,256]{1,0:T(8,128)(2,1)}, u32[]{:S(2)}) copy-start(bf16[1536,256]{1,0:T(8,128)(2,1)} %w_keyval_ref.1) | copy-start | bytes 2359300
  11.5 35.7 %all-to-all-start = ((bf16[8,128,1024]{2,1,0:T(8,128)(2,1)}), bf16[8,128,1024]{2,1,0:T(8,128)(2,1)}, u32[]{:S(2)}, u32[]{:S(2)}) async-start(bf16[8,128,1024]{2,1,0:T(8,128)(2,1)} %broadcast_in_dim.8), calls=%async_computation | async-start | bytes 4194304 | tf_op jit(solution)/shard_map/all_to_all | solution.py:200
  58.5 9.1 %all-to-all-start.1 = ((f32[8,16,512]{2,1,0:T(8,128)}), f32[8,16,512]{2,1,0:T(8,128)S(1)}, u32[]{:S(2)}, u32[]{:S(2)}) async-start(f32[8,16,512]{2,1,0:T(8,128)} %broadcast_in_dim.9), calls=%async_computation.1 | async-start | bytes 524288 | tf_op jit(solution)/shard_map/all_to_all | solution.py:200
  67.6 3.6 %copy-start.5 = (f32[8,16,512]{2,1,0:T(8,128)}, f32[8,16,512]{2,1,0:T(8,128)S(1)}, u32[]{:S(2)}) copy-start(f32[8,16,512]{2,1,0:T(8,128)S(1)} %all-to-all-done.1.stats_ref) | copy-start | bytes 786436
  67.6 18.2 %all-to-all-start.2 = ((bf16[8,128,512]{2,1,0:T(8,128)(2,1)}), bf16[8,128,512]{2,1,0:T(8,128)(2,1)S(1)}, u32[]{:S(2)}, u32[]{:S(2)}) async-start(bf16[8,128,512]{2,1,0:T(8,128)(2,1)} %get-tuple-element.31), calls=%async_computation.2 | async-start | bytes 2097152 | tf_op jit(solution)/shard_map/all_to_all | solution.py:200
  71.2 60.8 %reduce-scatter.2.cloned.1.call-start = ((), (), s32[]{:S(2)}) async-start(), calls=%async_computation.8 | async-start | bytes 1179648 | tf_op jit(solution)/shard_map/reduce_scatter | solution.py:257
  85.9 1.0 copy-start.1
  91.0 8.2 %copy-start.6 = (bf16[512,768]{1,0:T(8,128)(2,1)S(1)}, bf16[512,768]{1,0:T(8,128)(2,1)}, u32[]{:S(2)}) copy-start(bf16[512,768]{1,0:T(8,128)(2,1)} %get-tuple-element.34) | copy-start | bytes 2359300
  91.0 8.2 %collective-permute-start = (bf16[512,768]{1,0:T(8,128)(2,1)}, bf16[512,768]{1,0:T(8,128)(2,1)S(1)}, u32[]{:S(2)}, u32[]{:S(2)}) collective-permute-start(bf16[512,768]{1,0:T(8,128)(2,1)} %get-tuple-element.35), channel_id=1, source_target_pairs={{0,1},{1,0},{2,3},{3,2},{4,5},{5,4},{6,7},{7,6},{8,9},{9,8},{10,11... | collective-permute-start | bytes 2359304 | tf_op jit(solution)/shard_map/ppermute | solution.py:35
  115.0 17.8 %all-to-all-start.3 = ((bf16[8,128,512]{2,1,0:T(8,128)(2,1)}), bf16[8,128,512]{2,1,0:T(8,128)(2,1)S(1)}, u32[]{:S(2)}, u32[]{:S(2)}) async-start(bf16[8,128,512]{2,1,0:T(8,128)(2,1)} %get-tuple-element.37), calls=%async_computation.3 | async-start | bytes 2097152 | tf_op jit(solution)/shard_map/all_to_all | solution.py:200
  132.7 1.0 copy-start.4
  137.3 6.7 %collective-permute-start.1 = (bf16[1536,384]{1,0:T(8,128)(2,1)}, bf16[1536,384]{1,0:T(8,128)(2,1)S(1)}, u32[]{:S(2)}, u32[]{:S(2)}) collective-permute-start(bf16[1536,384]{1,0:T(8,128)(2,1)} %get-tuple-element.43), channel_id=1, source_target_pairs={{0,1},{1,0},{2,3},{3,2},{4,5},{5,4},{6,7},{7,6},{8,9},{9,8},{10,11... | collective-permute-start | bytes 3538952 | tf_op jit(solution)/shard_map/ppermute | solution.py:35
  146.6 19.9 %all-to-all-start.5 = ((bf16[4,384,384]{2,1,0:T(8,128)(2,1)}), bf16[4,384,384]{2,1,0:T(8,128)(2,1)S(1)}, u32[]{:S(2)}, u32[]{:S(2)}) async-start(bf16[4,384,384]{2,1,0:T(8,128)(2,1)} %bitcast.9), calls=%async_computation.6 | async-start | bytes 2359296 | tf_op jit(solution)/shard_map/all_to_all | solution.py:200
  186.2 4.7 %collective-permute-start.2 = (f32[40,384]{1,0:T(8,128)S(1)}, f32[40,384]{1,0:T(8,128)S(1)}, u32[]{:S(2)}, u32[]{:S(2)}) collective-permute-start(f32[40,384]{1,0:T(8,128)S(1)} %convert_reduce_fusion.1), channel_id=1, source_target_pairs={{0,2},{2,0},{1,3},{3,1},{4,6},{6,4},{5,7},{7,5},{8,10},{10,8},{9,1... | collective-permute-start | bytes 184328 | tf_op jit(solution)/shard_map/ppermute | solution.py:35
  190.8 5.5 %collective-permute-start.3 = (f32[40,384]{1,0:T(8,128)S(1)}, f32[40,384]{1,0:T(8,128)S(1)}, u32[]{:S(2)}, u32[]{:S(2)}) collective-permute-start(f32[40,384]{1,0:T(8,128)S(1)} %add.17), channel_id=1, source_target_pairs={{0,1},{1,0},{2,3},{3,2},{4,5},{5,4},{6,7},{7,6},{8,9},{9,8},{10,11... | collective-permute-start | bytes 184328 | tf_op jit(solution)/shard_map/ppermute | solution.py:35
Sparse Core Ops, SparseCore 0:
  97.2 34.7 reduce-scatter.1

commit v4 on v3

--- a/solution.py
+++ b/solution.py
@@ -13,7 +13,6 @@
 ROWS = HEADS * POS
 GROUP = 8
 KEYS = 8 * POS
-CHUNK = 512
 TILE = 32
 SCALE = 1.0 / HEAD_DIM**0.5
 LOG2E = math.log2(math.e)
@@ -98,54 +97,57 @@
     stat[8:, :] = delta
     dkv[...] = jnp.zeros_like(dkv)
 
-    def block(p, carry):
-        both = qd[p]
-        q4 = rows_of(both[:, :ROWS])
-        d4 = rows_of(both[:, ROWS:])
+    def rows(p):
+        return rows_of(qd[p, :, :ROWS]), rows_of(qd[p, :, ROWS:])
+
+    def products(p, score, dprob):
+        q4, d4 = rows(p)
+        score[...] = dot(kv[:, :HEAD_DIM], q4, NT)
+        dprob[...] = dot(kv[:, HEAD_DIM:], d4, NT)
+
+    def gradients(p, score, dprob, weight, dscore):
         base = stat[pl.ds(p, 1), :]
         delta = stat[pl.ds(8 + p, 1), :]
-        acc = jnp.zeros((HEAD_DIM, ROWS), F32)
-        count = KEYS // CHUNK
-        for c in range(count):
-            part = slice(c * CHUNK, (c + 1) * CHUNK)
-            score, dprob = scratch[4 * c : 4 * c + 2]
-            score[...] = dot(kv[part, :HEAD_DIM], q4, NT)
-            dprob[...] = dot(kv[part, HEAD_DIM:], d4, NT)
-        for c in range(count):
-            part = slice(c * CHUNK, (c + 1) * CHUNK)
-            score, dprob, weight, dscore = scratch[4 * c : 4 * c + 4]
-            for tile in tiles(CHUNK):
-                prob = jnp.exp2(score[tile, :] * (SCALE * LOG2E) - base)
-                weight[tile, :] = prob.astype(BF16)
-                dscore[tile, :] = (prob * (dprob[tile, :] - delta)).astype(BF16)
-            dkv[part, HEAD_DIM:] += dot(weight[...], d4)
-            dkv[part, :HEAD_DIM] += dot(dscore[...], q4)
-            acc = acc + dot(kt[:, part], dscore[...])
-        dq[p] = (acc * SCALE).astype(BF16)
+        for tile in tiles(KEYS):
+            prob = jnp.exp2(score[tile, :] * (SCALE * LOG2E) - base)
+            weight[tile, :] = prob.astype(BF16)
+            dscore[tile, :] = (prob * (dprob[tile, :] - delta)).astype(BF16)
+        q4, d4 = rows(p)
+        dkv[:, HEAD_DIM:] += dot(weight[...], d4)
+        dkv[:, :HEAD_DIM] += dot(dscore[...], q4)
+        dq[p] = (dot(kt[...], dscore[...]) * SCALE).astype(BF16)
+
+    def block(i, carry):
+        for n in range(2):
+            products(2 * i + n, *scratch[4 * n : 4 * n + 2])
+        for n in range(2):
+            gradients(2 * i + n, *scratch[4 * n : 4 * n + 4])
         return carry
 
-    lax.fori_loop(0, GROUP, block, 0)
+    lax.fori_loop(0, GROUP // 2, block, 0)
     dkv[:, :HEAD_DIM] = dkv[:, :HEAD_DIM] * SCALE
 
 
-def output_kernel(place, parts, stats_ref, tokens_ref, upstream_ref, w_out_ref, *outs):
-    attended_ref, keep_ref, give_ref = outs
+def output_kernel(place, parts, stats_ref, upstream_ref, mixed_ref, keep_ref, give_ref):
     mine = place[1]
     unused, unused, weights = combine(
         stats_ref[:, pl.ds(mine, 1), :], stats_ref[:, pl.ds(8 + mine, 1), :]
     )
     mixed_t = jnp.sum(weights * parts[...].astype(F32), axis=0)
     heads_t = [mixed_t[:, h * POS : (h + 1) * POS] for h in range(HEADS)]
-    mixed = jnp.concatenate([m.T for m in heads_t], axis=1).astype(BF16)
+    mixed_ref[...] = jnp.concatenate([m.T for m in heads_t], axis=1).astype(BF16)
     mixed_rows = jnp.concatenate(heads_t, axis=0).astype(BF16)
-    attended_ref[...] = (
-        tokens_ref[...].astype(F32) + dot(mixed, w_out_ref[...])
-    ).astype(BF16)
     half = upstream_ref.shape[1] // 2
     first = place[0] == 0
     low, high = upstream_ref[:, :half], upstream_ref[:, half:]
     keep_ref[...] = dot(mixed_rows, jnp.where(first, low, high)).astype(BF16)
     give_ref[...] = dot(mixed_rows, jnp.where(first, high, low)).astype(BF16)
+
+
+def attended_kernel(tokens_ref, mixed_ref, w_out_ref, attended_ref):
+    attended_ref[...] = (
+        tokens_ref[...].astype(F32) + dot(mixed_ref[...], w_out_ref[...])
+    ).astype(BF16)
 
 
 def input_kernel(place, dq_ref, dkv_ref, tokens_ref, both_ref, keep_ref, give_ref):
@@ -250,23 +252,23 @@
             pltpu.VMEM((HEAD_DIM, KEYS), BF16),
             pltpu.VMEM((16, ROWS), F32),
         ]
-        + [pltpu.VMEM((CHUNK, ROWS), t) for t in (F32, F32, BF16, BF16)] * (KEYS // CHUNK),
+        + [pltpu.VMEM((KEYS, ROWS), t) for t in (F32, F32, BF16, BF16)] * 2,
         16_000_000_000,
     )
     dq_parts, mine = lax.optimization_barrier((dq_parts, mine))
     dkv = lax.psum_scatter(dkv_parts, "z", scatter_dimension=0, tiled=True)
-    attended, keep_o, give_o = call(
+    mixed, keep_o, give_o = call(
         output_kernel,
-        [place, mine, all_stats, local, cotangent, w_out],
-        [shape(*local.shape), shape(512, 768), shape(512, 768)],
-        [SM] + [VM] * 5,
+        [place, mine, all_stats, cotangent],
+        [shape(POS, ROWS), shape(512, 768), shape(512, 768)],
+        [SM] + [VM] * 3,
         [VM] * 3,
         [],
-        600_000_000,
+        400_000_000,
     )
     term_o = plus(keep_o, send(give_o, "core", 2, 1))
-    term_o, dq_parts = lax.optimization_barrier((term_o, dq_parts))
     dqs = swap(dq_parts, ("x", "yl"))
+    term_o, dqs = lax.optimization_barrier((term_o, dqs))
     term_o = added(swap(term_o.reshape(4, 128, 768), "x"))
     term_o = term_o.reshape(16, 8, 2, 384).transpose(0, 2, 1, 3).reshape(16, 16, 384)
     dkv, term_o = lax.optimization_barrier((dkv, term_o))
@@ -294,7 +296,18 @@
     grad_tokens, term_i = lax.optimization_barrier((grad_tokens, term_i))
     term_i = added(term_i)
     ends = jnp.concatenate([term_i.reshape(16, 24, 384), term_o], axis=1).astype(BF16)
-    ends = added(swap(ends, ("z", "yl")))
+    attended = call(
+        attended_kernel,
+        [local, mixed, w_out],
+        shape(*local.shape),
+        [VM] * 3,
+        VM,
+        [],
+        200_000_000,
+    )
+    ends = swap(ends, ("z", "yl"))
+    attended, ends = lax.optimization_barrier((attended, ends))
+    ends = added(ends)
     ends = ends + send(ends, "yh", 2, 1)
     other = send(ends, "core", 2, 1)
     low, high = jnp.where(core == 0, ends, other), jnp.where(core == 0, other, ends)

time: 206 us -> 202 us (0.981)
  blocking collectives: 61.2 us -> 48.4 us
  waiting for transfers between devices: 42.7 us -> 49.3 us
  starting transfers between devices: 37.7 us -> 39.9 us
    all_to_all x5, waiting for transfers between devices: 21.5 us -> 43.7 us  [swap(): return lax.all_to_all(blocks, axes, 0, 0)]
    reduce_scatter x1, waiting for transfers between devices: 13.4 us -> 0.02 us  [body(): dkv = lax.psum_scatter(dkv_parts, 'z', scatter_dimension=0, tiled=True)]
    all_to_all x2, blocking collectives: 34.8 us -> 22 us  [swap(): return lax.all_to_all(blocks, axes, 0, 0)]
    all_to_all x5, starting transfers between devices: 20.5 us -> 24.2 us  [swap(): return lax.all_to_all(blocks, axes, 0, 0)]
    ppermute x4, waiting for transfers between devices: 7.89 us -> 5.53 us  [send(): lax.ppermute(array, axis, [(i, (i + step) % size) for i in range(size)])]
    pallas_call x5 -> x6, Pallas kernels: 35.4 us -> 36.4 us  [call(): pl.pallas_call(kernel, out_shape=outs, in_specs=in_specs, out_specs=out_s...]
  transfers between devices with their start and end apart: 10 -> 10, of which waited for: 9 -> 7; matrix products, arithmetic and copies ran while one was open for 1% -> 1% of each run, Pallas kernels for 9% -> 11%
where the time goes in v4:
time: 202 us; the launch traced here: 201 us
  waiting for transfers between devices  49.3 us (24%)
  blocking collectives  48.4 us (24%)
  starting transfers between devices  39.9 us (20%)
  Pallas kernels  36.4 us (18%)
  between operations  14.2 us (7%)
  other arithmetic  6.59 us (3%)
  local copies, waits for them, and re-layouts  3.4 us (2%)
  matrix products  2.94 us (1%)
    all_to_all x5, waiting for transfers between devices, swap(): return lax.all_to_all(blocks, axes, 0, 0)  43.7 us
    pallas_call x6, Pallas kernels, call(): pl.pallas_call(kernel, out_shape=outs, in_specs=in_specs, out_specs=out_s...  36.4 us
    all_gather x1, blocking collectives, body(): kvs = lax.all_gather(keyval, 'z', axis=0, tiled=True)  26.4 us
    all_to_all x5, starting transfers between devices, swap(): return lax.all_to_all(blocks, axes, 0, 0)  24.2 us
    all_to_all x2, blocking collectives, swap(): return lax.all_to_all(blocks, axes, 0, 0)  22 us
    ppermute x4, starting transfers between devices, send(): lax.ppermute(array, axis, [(i, (i + step) % size) for i in range(size)])  15.7 us
    ppermute x4, waiting for transfers between devices, send(): lax.ppermute(array, axis, [(i, (i + step) % size) for i in range(size)])  5.53 us
  transfers between devices with their start and end apart: 10, of which 7 were waited for; matrix products, arithmetic and copies ran while one was open for 1% of the time, Pallas kernels for 11%

profile of v4, /device:TPU:1, one launch (start us, length us, event | category | flops | bytes accessed | tf_op | source)
XLA Modules:
  0.0 201.1 jit_solution(1581103297003656476)
XLA Ops:
  11.5 6.0 %all-to-all-start = ((bf16[8,128,1024]{2,1,0:T(8,128)(2,1)}), bf16[8,128,1024]{2,1,0:T(8,128)(2,1)}, u32[]{:S(2)}, u32[]{:S(2)}) async-start(bf16[8,128,1024]{2,1,0:T(8,128)(2,1)} %broadcast_in_dim.8), calls=%async_computation | async-start | bytes 4194304 | tf_op jit(solution)/shard_map/all_to_all | solution.py:202
  17.8 26.4 %all_gather.3.kv = bf16[1024,256]{1,0:T(8,128)(2,1)} all-gather(bf16[128,256]{1,0:T(8,128)(2,1)S(1)} %convolution_convert_fusion.2), channel_id=1, replica_groups=mesh['x'=4,'z'=8,'yl'=2,'yh'=2,'core'=2] {'z'}, dimensions={0}, use_global_device_ids=true | all-gather | bytes 589824 | tf_op jit(solution)/shard_map/all_gather | solution.py:225
  44.2 3.0 %all-to-all-done.qd = bf16[8,128,1024]{2,1,0:T(8,128)(2,1)} async-done(((bf16[8,128,1024]{2,1,0:T(8,128)(2,1)}), bf16[8,128,1024]{2,1,0:T(8,128)(2,1)}, u32[]{:S(2)}, u32[]{:S(2)}) %all-to-all-start) | async-done | bytes 2097184 | tf_op jit(solution)/shard_map/all_to_all | solution.py:202
  47.2 9.8 %shard_map.92 = (bf16[8,128,512]{2,1,0:T(8,128)(2,1)}, f32[16,512]{1,0:T(8,128)}) custom-call(bf16[8,128,1024]{2,1,0:T(8,128)(2,1)} %all-to-all-done.qd, bf16[1024,256]{1,0:T(8,128)(2,1)} %all_gather.3.kv), custom_call_target="tpu_custom_call" | custom-call | flops 10000000000 | bytes 6000000 | tf_op jit(solution)/shard_map/pallas_call | solution.py:186
  57.8 8.9 %all_to_all.35.stats_ref = f32[8,16,512]{2,1,0:T(8,128)} all-to-all(f32[8,16,512]{2,1,0:T(8,128)S(1)} %broadcast_in_dim.9), channel_id=1, replica_groups=mesh['x'=4,'z'=8,'yl'=2,'yh'=2,'core'=2] {'x','yl'}, dimensions={0} | all-to-all | bytes 524288 | tf_op jit(solution)/shard_map/all_to_all | solution.py:202
  66.7 3.6 %all-to-all-start.2 = ((bf16[8,128,512]{2,1,0:T(8,128)(2,1)}), bf16[8,128,512]{2,1,0:T(8,128)(2,1)S(1)}, u32[]{:S(2)}, u32[]{:S(2)}) async-start(bf16[8,128,512]{2,1,0:T(8,128)(2,1)} %get-tuple-element.33), calls=%async_computation.2 | async-start | bytes 2097152 | tf_op jit(solution)/shard_map/all_to_all | solution.py:202
  70.3 13.7 %shard_map.93 = (bf16[8,128,512]{2,1,0:T(8,128)(2,1)}, f32[1024,256]{1,0:T(8,128)}) custom-call(bf16[8,128,1024]{2,1,0:T(8,128)(2,1)} %all-to-all-done.qd, f32[8,16,512]{2,1,0:T(8,128)} %all_to_all.35.stats_ref, bf16[1024,256]{1,0:T(8,128)(2,1)} %all_gather.3.kv), custom_call_target="tpu_custom_call" | custom-call | flops 16000000000 | bytes 6000000 | tf_op jit(solution)/shard_map/pallas_call | solution.py:186
  85.6 3.2 %shard_map.94 = (bf16[128,512]{1,0:T(8,128)(2,1)}, bf16[512,768]{1,0:T(8,128)(2,1)}, bf16[512,768]{1,0:T(8,128)(2,1)}) custom-call(s32[2]{0:T(128)} %pad_add_fusion.place, bf16[8,128,512]{2,1,0:T(8,128)(2,1)} %copy-done.1, f32[8,16,512]{2,1,0:T(8,128)} %all_to_all.35.stats_ref, bf16[128,1536]{1,0:T(8,128)(2,1)} %bitcast.33), custom_call_target="tpu_custom_call" | custom-call | flops 400000000 | bytes 6000000 | tf_op jit(solution)/shard_map/pallas_call | solution.py:186
  88.9 6.2 %collective-permute-start = (bf16[512,768]{1,0:T(8,128)(2,1)}, bf16[512,768]{1,0:T(8,128)(2,1)S(1)}, u32[]{:S(2)}, u32[]{:S(2)}) collective-permute-start(bf16[512,768]{1,0:T(8,128)(2,1)} %get-tuple-element.37), channel_id=1, source_target_pairs={{0,1},{1,0},{2,3},{3,2},{4,5},{5,4},{6,7},{7,6},{8,9},{9,8},{10,11... | collective-permute-start | bytes 2359304 | tf_op jit(solution)/shard_map/ppermute | solution.py:34
  95.1 5.3 %all-to-all-start.3 = ((bf16[8,128,512]{2,1,0:T(8,128)(2,1)}), bf16[8,128,512]{2,1,0:T(8,128)(2,1)S(1)}, u32[]{:S(2)}, u32[]{:S(2)}) async-start(bf16[8,128,512]{2,1,0:T(8,128)(2,1)} %get-tuple-element.38), calls=%async_computation.3 | async-start | bytes 2097152 | tf_op jit(solution)/shard_map/all_to_all | solution.py:202
  100.6 16.0 %all-to-all-done.3.dq_ref = bf16[8,128,512]{2,1,0:T(8,128)(2,1)S(1)} async-done(((bf16[8,128,512]{2,1,0:T(8,128)(2,1)}), bf16[8,128,512]{2,1,0:T(8,128)(2,1)S(1)}, u32[]{:S(2)}, u32[]{:S(2)}) %all-to-all-start.3) | async-done | bytes 1048608 | tf_op jit(solution)/shard_map/all_to_all | solution.py:202
  116.6 13.2 %all_to_all.36 = bf16[4,128,768]{2,1,0:T(8,128)(2,1)S(1)} all-to-all(bf16[4,128,768]{2,1,0:T(8,128)(2,1)S(1)} %bitcast.32), channel_id=1, replica_groups=mesh['x'=4,'z'=8,'yl'=2,'yh'=2,'core'=2] {'x'}, dimensions={0} | all-to-all | bytes 1572864 | tf_op jit(solution)/shard_map/all_to_all | solution.py:202
  129.9 3.6 %shard_map.96 = (bf16[128,768]{1,0:T(8,128)(2,1)}, bf16[1536,384]{1,0:T(8,128)(2,1)}, bf16[1536,384]{1,0:T(8,128)(2,1)}) custom-call(s32[2]{0:T(128)} %pad_add_fusion.place, bf16[8,128,512]{2,1,0:T(8,128)(2,1)} %copy-done.4, f32[128,256]{1,0:T(8,128)} %reduce-scatter.2.cloned.1.call-done.dkv_ref, bf16[128,1536]{1,0:T(8,128)(2,1)} %bitcast.29), custom_call_target="tpu_custom_call" | custom-call | flops 600000000 | bytes 6000000 | tf_op jit(solution)/shard_map/pallas_call | solution.py:186
  133.5 2.5 %collective-permute-start.1 = (bf16[1536,384]{1,0:T(8,128)(2,1)}, bf16[1536,384]{1,0:T(8,128)(2,1)S(1)}, u32[]{:S(2)}, u32[]{:S(2)}) collective-permute-start(bf16[1536,384]{1,0:T(8,128)(2,1)} %get-tuple-element.45), channel_id=1, source_target_pairs={{0,1},{1,0},{2,3},{3,2},{4,5},{5,4},{6,7},{7,6},{8,9},{9,8},{10,11... | collective-permute-start | bytes 3538952 | tf_op jit(solution)/shard_map/ppermute | solution.py:34
  135.9 2.7 %collective-permute-done.1 = bf16[1536,384]{1,0:T(8,128)(2,1)S(1)} collective-permute-done((bf16[1536,384]{1,0:T(8,128)(2,1)}, bf16[1536,384]{1,0:T(8,128)(2,1)S(1)}, u32[]{:S(2)}, u32[]{:S(2)}) %collective-permute-start.1) | collective-permute-done | bytes 1179680 | tf_op jit(solution)/shard_map/ppermute | solution.py:34
  138.6 2.6 %add_convert_fusion = bf16[1536,384]{1,0:T(8,128)(2,1)} fusion(bf16[1536,384]{1,0:T(8,128)(2,1)S(1)} %collective-permute-done.1, bf16[1536,384]{1,0:T(8,128)(2,1)} %get-tuple-element.44), kind=kLoop, calls=%fused_computation | loop fusion | flops 2359296 | bytes 3538944 | tf_op jit(solution)/shard_map/convert_element_type | solution.py:178
  141.2 3.5 %all-to-all-start.5 = ((bf16[4,384,384]{2,1,0:T(8,128)(2,1)}), bf16[4,384,384]{2,1,0:T(8,128)(2,1)S(1)}, u32[]{:S(2)}, u32[]{:S(2)}) async-start(bf16[4,384,384]{2,1,0:T(8,128)(2,1)} %bitcast.8), calls=%async_computation.6 | async-start | bytes 2359296 | tf_op jit(solution)/shard_map/all_to_all | solution.py:202
  144.8 3.3 %shard_map.97 = bf16[128,1536]{1,0:T(8,128)(2,1)} custom-call(bf16[128,768]{1,0:T(8,128)(2,1)} %get-tuple-element.43.both_ref, bf16[1536,512]{1,0:T(8,128)(2,1)} %w_query_ref.1, bf16[1536,256]{1,0:T(8,128)(2,1)} %w_keyval_ref.1), custom_call_target="tpu_custom_call" | custom-call | flops 300000000 | bytes 6000000 | tf_op jit(solution)/shard_map/pallas_call | solution.py:186
  148.1 12.9 %all-to-all-done.5 = bf16[4,384,384]{2,1,0:T(8,128)(2,1)S(1)} async-done(((bf16[4,384,384]{2,1,0:T(8,128)(2,1)}), bf16[4,384,384]{2,1,0:T(8,128)(2,1)S(1)}, u32[]{:S(2)}, u32[]{:S(2)}) %all-to-all-start.5) | async-done | bytes 1179680 | tf_op jit(solution)/shard_map/all_to_all | solution.py:202
  162.1 5.8 %all-to-all-start.6 = ((bf16[16,40,384]{2,1,0:T(8,128)(2,1)}), bf16[16,40,384]{2,1,0:T(8,128)(2,1)S(1)}, u32[]{:S(2)}, u32[]{:S(2)}) async-start(bf16[16,40,384]{2,1,0:T(8,128)(2,1)} %pad_maximum_fusion), calls=%async_computation.7 | async-start | bytes 983040 | tf_op jit(solution)/shard_map/all_to_all | solution.py:202
  167.9 2.7 %shard_map.95 = bf16[128,1536]{1,0:T(8,128)(2,1)} custom-call(bf16[128,1536]{1,0:T(8,128)(2,1)} %bitcast.30, bf16[128,512]{1,0:T(8,128)(2,1)} %get-tuple-element.35.mixed_ref, bf16[512,1536]{1,0:T(8,128)(2,1)} %w_out_ref.1), custom_call_target="tpu_custom_call" | custom-call | flops 200000000 | bytes 6000000 | tf_op jit(solution)/shard_map/pallas_call | solution.py:186
  170.6 11.8 %all-to-all-done.6 = bf16[16,40,384]{2,1,0:T(8,128)(2,1)S(1)} async-done(((bf16[16,40,384]{2,1,0:T(8,128)(2,1)}), bf16[16,40,384]{2,1,0:T(8,128)(2,1)S(1)}, u32[]{:S(2)}, u32[]{:S(2)}) %all-to-all-start.6) | async-done | bytes 491552 | tf_op jit(solution)/shard_map/all_to_all | solution.py:202
  182.5 2.7 %collective-permute-start.2 = (f32[40,384]{1,0:T(8,128)S(1)}, f32[40,384]{1,0:T(8,128)S(1)}, u32[]{:S(2)}, u32[]{:S(2)}) collective-permute-start(f32[40,384]{1,0:T(8,128)S(1)} %convert_reduce_fusion.1), channel_id=1, source_target_pairs={{0,2},{2,0},{1,3},{3,1},{4,6},{6,4},{5,7},{7,5},{8,10},{10,8},{9,1... | collective-permute-start | bytes 184328 | tf_op jit(solution)/shard_map/ppermute | solution.py:34
  187.2 4.2 %collective-permute-start.3 = (f32[40,384]{1,0:T(8,128)S(1)}, f32[40,384]{1,0:T(8,128)S(1)}, u32[]{:S(2)}, u32[]{:S(2)}) collective-permute-start(f32[40,384]{1,0:T(8,128)S(1)} %add.17), channel_id=1, source_target_pairs={{0,1},{1,0},{2,3},{3,2},{4,5},{5,4},{6,7},{7,6},{8,9},{9,8},{10,11... | collective-permute-start | bytes 184328 | tf_op jit(solution)/shard_map/ppermute | solution.py:34
  (41 shorter events, 13.2 us)
Async XLA Ops:
  7.2 2.3 %copy-start.2 = (bf16[1,128,1536]{2,1,0:T(8,128)(2,1)S(1)}, bf16[1,128,1536]{2,1,0:T(8,128)(2,1)}, u32[]{:S(2)}) copy-start(bf16[1,128,1536]{2,1,0:T(8,128)(2,1)} %param.5) | copy-start | bytes 1179652
  7.2 2.3 %copy-start = (bf16[1536,512]{1,0:T(8,128)(2,1)S(1)}, bf16[1536,512]{1,0:T(8,128)(2,1)}, u32[]{:S(2)}) copy-start(bf16[1536,512]{1,0:T(8,128)(2,1)} %w_query_ref.1) | copy-start | bytes 4718596
  11.5 6.0 %copy-start.3 = (bf16[1536,256]{1,0:T(8,128)(2,1)S(1)}, bf16[1536,256]{1,0:T(8,128)(2,1)}, u32[]{:S(2)}) copy-start(bf16[1536,256]{1,0:T(8,128)(2,1)} %w_keyval_ref.1) | copy-start | bytes 2359300
  11.5 35.7 %all-to-all-start = ((bf16[8,128,1024]{2,1,0:T(8,128)(2,1)}), bf16[8,128,1024]{2,1,0:T(8,128)(2,1)}, u32[]{:S(2)}, u32[]{:S(2)}) async-start(bf16[8,128,1024]{2,1,0:T(8,128)(2,1)} %broadcast_in_dim.8), calls=%async_computation | async-start | bytes 4194304 | tf_op jit(solution)/shard_map/all_to_all | solution.py:202
  66.7 18.0 %all-to-all-start.2 = ((bf16[8,128,512]{2,1,0:T(8,128)(2,1)}), bf16[8,128,512]{2,1,0:T(8,128)(2,1)S(1)}, u32[]{:S(2)}, u32[]{:S(2)}) async-start(bf16[8,128,512]{2,1,0:T(8,128)(2,1)} %get-tuple-element.33), calls=%async_computation.2 | async-start | bytes 2097152 | tf_op jit(solution)/shard_map/all_to_all | solution.py:202
  70.2 59.6 %reduce-scatter.2.cloned.1.call-start = ((), (), s32[]{:S(2)}) async-start(), calls=%async_computation.8 | async-start | bytes 1179648 | tf_op jit(solution)/shard_map/reduce_scatter | solution.py:259
  84.6 1.0 copy-start.1
  88.9 11.6 %copy-start.5 = (bf16[512,768]{1,0:T(8,128)(2,1)S(1)}, bf16[512,768]{1,0:T(8,128)(2,1)}, u32[]{:S(2)}) copy-start(bf16[512,768]{1,0:T(8,128)(2,1)} %get-tuple-element.36) | copy-start | bytes 2359300
  88.9 11.6 %collective-permute-start = (bf16[512,768]{1,0:T(8,128)(2,1)}, bf16[512,768]{1,0:T(8,128)(2,1)S(1)}, u32[]{:S(2)}, u32[]{:S(2)}) collective-permute-start(bf16[512,768]{1,0:T(8,128)(2,1)} %get-tuple-element.37), channel_id=1, source_target_pairs={{0,1},{1,0},{2,3},{3,2},{4,5},{5,4},{6,7},{7,6},{8,9},{9,8},{10,11... | collective-permute-start | bytes 2359304 | tf_op jit(solution)/shard_map/ppermute | solution.py:34
  95.1 21.5 %all-to-all-start.3 = ((bf16[8,128,512]{2,1,0:T(8,128)(2,1)}), bf16[8,128,512]{2,1,0:T(8,128)(2,1)S(1)}, u32[]{:S(2)}, u32[]{:S(2)}) async-start(bf16[8,128,512]{2,1,0:T(8,128)(2,1)} %get-tuple-element.38), calls=%async_computation.3 | async-start | bytes 2097152 | tf_op jit(solution)/shard_map/all_to_all | solution.py:202
  116.6 13.3 %copy-start.4 = (bf16[8,128,512]{2,1,0:T(8,128)(2,1)}, bf16[8,128,512]{2,1,0:T(8,128)(2,1)S(1)}, u32[]{:S(2)}) copy-start(bf16[8,128,512]{2,1,0:T(8,128)(2,1)S(1)} %all-to-all-done.3.dq_ref) | copy-start | bytes 3145732
  133.5 5.2 %collective-permute-start.1 = (bf16[1536,384]{1,0:T(8,128)(2,1)}, bf16[1536,384]{1,0:T(8,128)(2,1)S(1)}, u32[]{:S(2)}, u32[]{:S(2)}) collective-permute-start(bf16[1536,384]{1,0:T(8,128)(2,1)} %get-tuple-element.45), channel_id=1, source_target_pairs={{0,1},{1,0},{2,3},{3,2},{4,5},{5,4},{6,7},{7,6},{8,9},{9,8},{10,11... | collective-permute-start | bytes 3538952 | tf_op jit(solution)/shard_map/ppermute | solution.py:34
  141.2 19.8 %all-to-all-start.5 = ((bf16[4,384,384]{2,1,0:T(8,128)(2,1)}), bf16[4,384,384]{2,1,0:T(8,128)(2,1)S(1)}, u32[]{:S(2)}, u32[]{:S(2)}) async-start(bf16[4,384,384]{2,1,0:T(8,128)(2,1)} %bitcast.8), calls=%async_computation.6 | async-start | bytes 2359296 | tf_op jit(solution)/shard_map/all_to_all | solution.py:202
  162.1 20.3 %all-to-all-start.6 = ((bf16[16,40,384]{2,1,0:T(8,128)(2,1)}), bf16[16,40,384]{2,1,0:T(8,128)(2,1)S(1)}, u32[]{:S(2)}, u32[]{:S(2)}) async-start(bf16[16,40,384]{2,1,0:T(8,128)(2,1)} %pad_maximum_fusion), calls=%async_computation.7 | async-start | bytes 983040 | tf_op jit(solution)/shard_map/all_to_all | solution.py:202
  182.5 4.7 %collective-permute-start.2 = (f32[40,384]{1,0:T(8,128)S(1)}, f32[40,384]{1,0:T(8,128)S(1)}, u32[]{:S(2)}, u32[]{:S(2)}) collective-permute-start(f32[40,384]{1,0:T(8,128)S(1)} %convert_reduce_fusion.1), channel_id=1, source_target_pairs={{0,2},{2,0},{1,3},{3,1},{4,6},{6,4},{5,7},{7,5},{8,10},{10,8},{9,1... | collective-permute-start | bytes 184328 | tf_op jit(solution)/shard_map/ppermute | solution.py:34
  187.2 5.1 %collective-permute-start.3 = (f32[40,384]{1,0:T(8,128)S(1)}, f32[40,384]{1,0:T(8,128)S(1)}, u32[]{:S(2)}, u32[]{:S(2)}) collective-permute-start(f32[40,384]{1,0:T(8,128)S(1)} %add.17), channel_id=1, source_target_pairs={{0,1},{1,0},{2,3},{3,2},{4,5},{5,4},{6,7},{7,6},{8,9},{9,8},{10,11... | collective-permute-start | bytes 184328 | tf_op jit(solution)/shard_map/ppermute | solution.py:34
Sparse Core Ops, SparseCore 0:
  84.2 40.5 reduce-scatter.1

commit v5 on v4

--- a/solution.py
+++ b/solution.py
@@ -150,7 +150,7 @@
     ).astype(BF16)
 
 
-def input_kernel(place, dq_ref, dkv_ref, tokens_ref, both_ref, keep_ref, give_ref):
+def input_kernel(place, dq_ref, dkv_ref, both_ref, keep_ref, give_ref):
     dq_t = jnp.sum(dq_ref[...].astype(F32), axis=0)
     dquery = jnp.concatenate(
         [dq_t[:, h * POS : (h + 1) * POS].T for h in range(HEADS)], axis=1
@@ -159,12 +159,16 @@
     both_ref[:, :ROWS] = dquery
     both_ref[:, ROWS:] = dkeyval
     first = place[0] == 0
-    q_low, q_high = dquery[:, :256], dquery[:, 256:]
-    kv_low, kv_high = dkeyval[:, :128], dkeyval[:, 128:]
-    low = jnp.concatenate([q_low, kv_low], axis=1)
-    high = jnp.concatenate([q_high, kv_high], axis=1)
-    keep_ref[...] = dot(tokens_ref[...], jnp.where(first, low, high), TN).astype(BF16)
-    give_ref[...] = dot(tokens_ref[...], jnp.where(first, high, low), TN).astype(BF16)
+    low = jnp.concatenate([dquery[:, :256], dkeyval[:, :128]], axis=1)
+    high = jnp.concatenate([dquery[:, 256:], dkeyval[:, 128:]], axis=1)
+    keep_ref[...] = jnp.where(first, low, high)
+    give_ref[...] = jnp.where(first, high, low)
+
+
+def term_kernel(tokens_ref, other_ref, keep_ref, got_ref, term_ref):
+    tokens = jnp.concatenate([tokens_ref[...], other_ref[...]], axis=0)
+    grads = jnp.concatenate([keep_ref[...], got_ref[...]], axis=0)
+    term_ref[...] = dot(tokens, grads, TN).astype(BF16)
 
 
 def tokens_kernel(both_ref, w_query_ref, w_keyval_ref, grad_ref):
@@ -223,6 +227,8 @@
     qd, early = lax.optimization_barrier((qd, local))
     keyval = jnp.dot(early, w_keyval, preferred_element_type=F32).astype(BF16)
     kvs = lax.all_gather(keyval, "z", axis=0, tiled=True)
+    tokens_other = send(early, "core", 2, 1)
+    kvs, tokens_other = lax.optimization_barrier((kvs, tokens_other))
 
     mixed_parts, stats = call(
         forward_kernel,
@@ -267,22 +273,39 @@
         400_000_000,
     )
     term_o = plus(keep_o, send(give_o, "core", 2, 1))
+    attended = call(
+        attended_kernel,
+        [local, mixed, w_out],
+        shape(*local.shape),
+        [VM] * 3,
+        VM,
+        [],
+        200_000_000,
+    )
+    term_o, attended, dq_parts = lax.optimization_barrier((term_o, attended, dq_parts))
     dqs = swap(dq_parts, ("x", "yl"))
-    term_o, dqs = lax.optimization_barrier((term_o, dqs))
     term_o = added(swap(term_o.reshape(4, 128, 768), "x"))
     term_o = term_o.reshape(16, 8, 2, 384).transpose(0, 2, 1, 3).reshape(16, 16, 384)
     dkv, term_o = lax.optimization_barrier((dkv, term_o))
 
     both, keep_i, give_i = call(
         input_kernel,
-        [place, dqs, dkv, local],
-        [shape(POS, 768), shape(1536, 384), shape(1536, 384)],
-        [SM] + [VM] * 3,
-        [VM] * 3,
-        [],
-        600_000_000,
-    )
-    term_i = plus(keep_i, send(give_i, "core", 2, 1))
+        [place, dqs, dkv],
+        [shape(POS, 768), shape(POS, 384), shape(POS, 384)],
+        [SM] + [VM] * 2,
+        [VM] * 3,
+        [],
+        10_000_000,
+    )
+    term_i = call(
+        term_kernel,
+        [local, tokens_other, keep_i, send(give_i, "core", 2, 1)],
+        shape(1536, 384),
+        [VM] * 4,
+        VM,
+        [],
+        300_000_000,
+    )
     grad_tokens = call(
         tokens_kernel,
         [both, w_query, w_keyval],
@@ -296,17 +319,7 @@
     grad_tokens, term_i = lax.optimization_barrier((grad_tokens, term_i))
     term_i = added(term_i)
     ends = jnp.concatenate([term_i.reshape(16, 24, 384), term_o], axis=1).astype(BF16)
-    attended = call(
-        attended_kernel,
-        [local, mixed, w_out],
-        shape(*local.shape),
-        [VM] * 3,
-        VM,
-        [],
-        200_000_000,
-    )
     ends = swap(ends, ("z", "yl"))
-    attended, ends = lax.optimization_barrier((attended, ends))
     ends = added(ends)
     ends = ends + send(ends, "yh", 2, 1)
     other = send(ends, "core", 2, 1)

time: 202 us -> 203 us (level)
  blocking collectives: 48.4 us -> 62.6 us
  waiting for transfers between devices: 49.3 us -> 38.1 us
  other arithmetic: 6.59 us -> 3.19 us
  starting transfers between devices: 39.9 us -> 37.3 us
  local copies, waits for them, and re-layouts: 3.4 us -> 5.7 us
    all_to_all x5, waiting for transfers between devices: 43.7 us -> 22.5 us  [swap(): return lax.all_to_all(blocks, axes, 0, 0)]
    all_to_all x2, blocking collectives: 22 us -> 36.6 us  [swap(): return lax.all_to_all(blocks, axes, 0, 0)]
    reduce_scatter x1, waiting for transfers between devices: 0.02 us -> 11.6 us  [body(): dkv = lax.psum_scatter(dkv_parts, 'z', scatter_dimension=0, tiled=True)]
    all_to_all x5, starting transfers between devices: 24.2 us -> 20.5 us  [swap(): return lax.all_to_all(blocks, axes, 0, 0)]
    convert_element_type x2 -> x1, other arithmetic: 2.8 us -> 0.18 us  [plus(): return (a.astype(F32) + b.astype(F32)).astype(BF16)]
    ppermute x4 -> x5, waiting for transfers between devices: 5.53 us -> 3.99 us  [send(): lax.ppermute(array, axis, [(i, (i + step) % size) for i in range(size)])]
    pallas_call x6 -> x7, Pallas kernels: 36.4 us -> 37.8 us  [call(): pl.pallas_call(kernel, out_shape=outs, in_specs=in_specs, out_specs=out_s...]
    ppermute x4 -> x5, starting transfers between devices: 15.7 us -> 16.7 us  [send(): lax.ppermute(array, axis, [(i, (i + step) % size) for i in range(size)])]
  transfers between devices with their start and end apart: 10 -> 11, of which waited for: 7 -> 8; matrix products, arithmetic and copies ran while one was open for 1% -> 1% of each run, Pallas kernels for 11% -> 10%
where the time goes in v5:
time: 203 us; the launch traced here: 202 us
  blocking collectives  62.6 us (31%)
  waiting for transfers between devices  38.1 us (19%)
  Pallas kernels  37.8 us (19%)
  starting transfers between devices  37.3 us (18%)
  between operations  14.2 us (7%)
  local copies, waits for them, and re-layouts  5.7 us (3%)
  other arithmetic  3.19 us (2%)
  matrix products  2.93 us (1%)
    pallas_call x7, Pallas kernels, call(): pl.pallas_call(kernel, out_shape=outs, in_specs=in_specs, out_specs=out_s...  37.8 us
    all_to_all x2, blocking collectives, swap(): return lax.all_to_all(blocks, axes, 0, 0)  36.6 us
    all_gather x1, blocking collectives, body(): kvs = lax.all_gather(keyval, 'z', axis=0, tiled=True)  26 us
    all_to_all x5, waiting for transfers between devices, swap(): return lax.all_to_all(blocks, axes, 0, 0)  22.5 us
    all_to_all x5, starting transfers between devices, swap(): return lax.all_to_all(blocks, axes, 0, 0)  20.5 us
    ppermute x5, starting transfers between devices, send(): lax.ppermute(array, axis, [(i, (i + step) % size) for i in range(size)])  16.7 us
    reduce_scatter x1, waiting for transfers between devices, body(): dkv = lax.psum_scatter(dkv_parts, 'z', scatter_dimension=0, tiled=True)  11.6 us
  transfers between devices with their start and end apart: 11, of which 8 were waited for; matrix products, arithmetic and copies ran while one was open for 1% of the time, Pallas kernels for 10%

profile of v5, /device:TPU:1, one launch (start us, length us, event | category | flops | bytes accessed | tf_op | source)
XLA Modules:
  0.0 201.9 jit_solution(17069940575856549380)
XLA Ops:
  7.2 2.3 %convolution_convert_fusion = bf16[128,512]{1,0:T(8,128)(2,1)S(1)} fusion(bf16[512,1536]{1,0:T(8,128)(2,1)} %w_out_ref.1, bf16[1,128,1536]{2,1,0:T(8,128)(2,1)} %param.6), kind=kOutput, calls=%fused_computation.2 | convolution fusion | flops 201392128 | bytes 2097152 | tf_op jit(solution)/shard_map/dot_general | solution.py:224
  11.5 6.0 %all-to-all-start = ((bf16[8,128,1024]{2,1,0:T(8,128)(2,1)}), bf16[8,128,1024]{2,1,0:T(8,128)(2,1)}, u32[]{:S(2)}, u32[]{:S(2)}) async-start(bf16[8,128,1024]{2,1,0:T(8,128)(2,1)} %broadcast_in_dim.8), calls=%async_computation | async-start | bytes 4194304 | tf_op jit(solution)/shard_map/all_to_all | solution.py:206
  19.6 26.0 %all_gather.3.kv = bf16[1024,256]{1,0:T(8,128)(2,1)} all-gather(bf16[128,256]{1,0:T(8,128)(2,1)S(1)} %convolution_convert_fusion.2), channel_id=1, replica_groups=mesh['x'=4,'z'=8,'yl'=2,'yh'=2,'core'=2] {'z'}, dimensions={0}, use_global_device_ids=true | all-gather | bytes 589824 | tf_op jit(solution)/shard_map/all_gather | solution.py:229
  47.2 9.8 %shard_map.92 = (bf16[8,128,512]{2,1,0:T(8,128)(2,1)}, f32[16,512]{1,0:T(8,128)}) custom-call(bf16[8,128,1024]{2,1,0:T(8,128)(2,1)} %all-to-all-done.qd, bf16[1024,256]{1,0:T(8,128)(2,1)} %all_gather.3.kv), custom_call_target="tpu_custom_call" | custom-call | flops 10000000000 | bytes 6000000 | tf_op jit(solution)/shard_map/pallas_call | solution.py:190
  58.5 3.4 %all-to-all-start.1 = ((f32[8,16,512]{2,1,0:T(8,128)}), f32[8,16,512]{2,1,0:T(8,128)S(1)}, u32[]{:S(2)}, u32[]{:S(2)}) async-start(f32[8,16,512]{2,1,0:T(8,128)} %broadcast_in_dim.9), calls=%async_computation.1 | async-start | bytes 524288 | tf_op jit(solution)/shard_map/all_to_all | solution.py:206
  62.5 5.1 %all-to-all-done.1.stats_ref = f32[8,16,512]{2,1,0:T(8,128)S(1)} async-done(((f32[8,16,512]{2,1,0:T(8,128)}), f32[8,16,512]{2,1,0:T(8,128)S(1)}, u32[]{:S(2)}, u32[]{:S(2)}) %all-to-all-start.1) | async-done | bytes 262176 | tf_op jit(solution)/shard_map/all_to_all | solution.py:206
  67.6 3.6 %all-to-all-start.2 = ((bf16[8,128,512]{2,1,0:T(8,128)(2,1)}), bf16[8,128,512]{2,1,0:T(8,128)(2,1)S(1)}, u32[]{:S(2)}, u32[]{:S(2)}) async-start(bf16[8,128,512]{2,1,0:T(8,128)(2,1)} %get-tuple-element.35), calls=%async_computation.2 | async-start | bytes 2097152 | tf_op jit(solution)/shard_map/all_to_all | solution.py:206
  71.2 13.7 %shard_map.93 = (bf16[8,128,512]{2,1,0:T(8,128)(2,1)}, f32[1024,256]{1,0:T(8,128)}) custom-call(bf16[8,128,1024]{2,1,0:T(8,128)(2,1)} %all-to-all-done.qd, f32[8,16,512]{2,1,0:T(8,128)} %copy-done.5, bf16[1024,256]{1,0:T(8,128)(2,1)} %all_gather.3.kv), custom_call_target="tpu_custom_call" | custom-call | flops 16000000000 | bytes 6000000 | tf_op jit(solution)/shard_map/pallas_call | solution.py:190
  85.9 3.2 %shard_map.94 = (bf16[128,512]{1,0:T(8,128)(2,1)}, bf16[512,768]{1,0:T(8,128)(2,1)}, bf16[512,768]{1,0:T(8,128)(2,1)}) custom-call(s32[2]{0:T(128)} %pad_add_fusion.place, bf16[8,128,512]{2,1,0:T(8,128)(2,1)} %copy-done.2, f32[8,16,512]{2,1,0:T(8,128)} %copy-done.5, bf16[128,1536]{1,0:T(8,128)(2,1)} %bitcast.35), custom_call_target="tpu_custom_call" | custom-call | flops 400000000 | bytes 6000000 | tf_op jit(solution)/shard_map/pallas_call | solution.py:190
  89.2 6.2 %collective-permute-start.1 = (bf16[512,768]{1,0:T(8,128)(2,1)}, bf16[512,768]{1,0:T(8,128)(2,1)S(1)}, u32[]{:S(2)}, u32[]{:S(2)}) collective-permute-start(bf16[512,768]{1,0:T(8,128)(2,1)} %get-tuple-element.38), channel_id=1, source_target_pairs={{0,1},{1,0},{2,3},{3,2},{4,5},{5,4},{6,7},{7,6},{8,9},{9,8},{10,11... | collective-permute-start | bytes 2359304 | tf_op jit(solution)/shard_map/ppermute | solution.py:34
  95.4 2.8 %shard_map.95 = bf16[128,1536]{1,0:T(8,128)(2,1)} custom-call(bf16[128,1536]{1,0:T(8,128)(2,1)} %bitcast.29, bf16[128,512]{1,0:T(8,128)(2,1)} %get-tuple-element.39.mixed_ref, bf16[512,1536]{1,0:T(8,128)(2,1)} %w_out_ref.1), custom_call_target="tpu_custom_call" | custom-call | flops 200000000 | bytes 6000000 | tf_op jit(solution)/shard_map/pallas_call | solution.py:190
  98.4 16.3 %all_to_all.35 = bf16[4,128,768]{2,1,0:T(8,128)(2,1)S(1)} all-to-all(bf16[4,128,768]{2,1,0:T(8,128)(2,1)S(1)} %bitcast.34), channel_id=1, replica_groups=mesh['x'=4,'z'=8,'yl'=2,'yh'=2,'core'=2] {'x'}, dimensions={0} | all-to-all | bytes 1572864 | tf_op jit(solution)/shard_map/all_to_all | solution.py:206
  114.7 3.6 %all-to-all-start.3 = ((bf16[8,128,512]{2,1,0:T(8,128)(2,1)}), bf16[8,128,512]{2,1,0:T(8,128)(2,1)S(1)}, u32[]{:S(2)}, u32[]{:S(2)}) async-start(bf16[8,128,512]{2,1,0:T(8,128)(2,1)} %get-tuple-element.42), calls=%async_computation.3 | async-start | bytes 2097152 | tf_op jit(solution)/shard_map/all_to_all | solution.py:206
  118.4 11.6 %reduce-scatter.2.cloned.1.call-done.dkv_ref = f32[128,256]{1,0:T(8,128)} async-done(((f32[1024,256]{1,0:T(8,128)}), f32[128,256]{1,0:T(8,128)}) %reduce-scatter.2.cloned.1.call-update) | async-done | bytes 131088 | tf_op jit(solution)/shard_map/reduce_scatter | solution.py:265
  130.1 3.1 %all-to-all-done.3.dq_ref = bf16[8,128,512]{2,1,0:T(8,128)(2,1)S(1)} async-done(((bf16[8,128,512]{2,1,0:T(8,128)(2,1)}), bf16[8,128,512]{2,1,0:T(8,128)(2,1)S(1)}, u32[]{:S(2)}, u32[]{:S(2)}) %all-to-all-start.3) | async-done | bytes 1048608 | tf_op jit(solution)/shard_map/all_to_all | solution.py:206
  134.2 2.2 %shard_map.96 = (bf16[128,768]{1,0:T(8,128)(2,1)}, bf16[128,384]{1,0:T(8,128)(2,1)}, bf16[128,384]{1,0:T(8,128)(2,1)}) custom-call(s32[2]{0:T(128)} %pad_add_fusion.place, bf16[8,128,512]{2,1,0:T(8,128)(2,1)} %copy-done.3, f32[128,256]{1,0:T(8,128)} %reduce-scatter.2.cloned.1.call-done.dkv_ref), custom_call_target="tpu_custom_call" | custom-call | flops 10000000 | bytes 6000000 | tf_op jit(solution)/shard_map/pallas_call | solution.py:190
  139.9 2.8 %shard_map.98 = bf16[1536,384]{1,0:T(8,128)(2,1)} custom-call(bf16[128,1536]{1,0:T(8,128)(2,1)} %bitcast.30, bf16[128,1536]{1,0:T(8,128)(2,1)} %copy-done.7, bf16[128,384]{1,0:T(8,128)(2,1)} %get-tuple-element.48.keep_ref, bf16[128,384]{1,0:T(8,128)(2,1)} %copy-done.8), custom_call_target="tpu_custom_call" | custom-call | flops 300000000 | bytes 6000000 | tf_op jit(solution)/shard_map/pallas_call | solution.py:190
  142.7 4.0 %all-to-all-start.5 = ((bf16[4,384,384]{2,1,0:T(8,128)(2,1)}), bf16[4,384,384]{2,1,0:T(8,128)(2,1)S(1)}, u32[]{:S(2)}, u32[]{:S(2)}) async-start(bf16[4,384,384]{2,1,0:T(8,128)(2,1)} %bitcast.33), calls=%async_computation.6 | async-start | bytes 2359296 | tf_op jit(solution)/shard_map/all_to_all | solution.py:206
  146.7 3.3 %shard_map.97 = bf16[128,1536]{1,0:T(8,128)(2,1)} custom-call(bf16[128,768]{1,0:T(8,128)(2,1)} %get-tuple-element.46.both_ref, bf16[1536,512]{1,0:T(8,128)(2,1)} %w_query_ref.1, bf16[1536,256]{1,0:T(8,128)(2,1)} %w_keyval_ref.1), custom_call_target="tpu_custom_call" | custom-call | flops 300000000 | bytes 6000000 | tf_op jit(solution)/shard_map/pallas_call | solution.py:190
  150.0 12.7 %all-to-all-done.5 = bf16[4,384,384]{2,1,0:T(8,128)(2,1)S(1)} async-done(((bf16[4,384,384]{2,1,0:T(8,128)(2,1)}), bf16[4,384,384]{2,1,0:T(8,128)(2,1)S(1)}, u32[]{:S(2)}, u32[]{:S(2)}) %all-to-all-start.5) | async-done | bytes 1179680 | tf_op jit(solution)/shard_map/all_to_all | solution.py:206
  163.0 20.3 %all_to_all.36 = bf16[16,40,384]{2,1,0:T(8,128)(2,1)S(1)} all-to-all(bf16[16,40,384]{2,1,0:T(8,128)(2,1)S(1)} %pad_maximum_fusion), channel_id=1, replica_groups=mesh['x'=4,'z'=8,'yl'=2,'yh'=2,'core'=2] {'z','yl'}, dimensions={0} | all-to-all | bytes 983040 | tf_op jit(solution)/shard_map/all_to_all | solution.py:206
  183.3 2.7 %collective-permute-start.3 = (f32[40,384]{1,0:T(8,128)S(1)}, f32[40,384]{1,0:T(8,128)S(1)}, u32[]{:S(2)}, u32[]{:S(2)}) collective-permute-start(f32[40,384]{1,0:T(8,128)S(1)} %convert_reduce_fusion.1), channel_id=1, source_target_pairs={{0,2},{2,0},{1,3},{3,1},{4,6},{6,4},{5,7},{7,5},{8,10},{10,8},{9,1... | collective-permute-start | bytes 184328 | tf_op jit(solution)/shard_map/ppermute | solution.py:34
  186.1 1.9 collective-permute-done.3
  188.0 4.2 %collective-permute-start.4 = (f32[40,384]{1,0:T(8,128)S(1)}, f32[40,384]{1,0:T(8,128)S(1)}, u32[]{:S(2)}, u32[]{:S(2)}) collective-permute-start(f32[40,384]{1,0:T(8,128)S(1)} %add.13), channel_id=1, source_target_pairs={{0,1},{1,0},{2,3},{3,2},{4,5},{5,4},{6,7},{7,6},{8,9},{9,8},{10,11... | collective-permute-start | bytes 184328 | tf_op jit(solution)/shard_map/ppermute | solution.py:34
  (49 shorter events, 16.8 us)
Async XLA Ops:
  7.2 2.3 %copy-start.1 = (bf16[1,128,1536]{2,1,0:T(8,128)(2,1)S(1)}, bf16[1,128,1536]{2,1,0:T(8,128)(2,1)}, u32[]{:S(2)}) copy-start(bf16[1,128,1536]{2,1,0:T(8,128)(2,1)} %param.5) | copy-start | bytes 1179652
  7.2 2.3 %copy-start = (bf16[1536,512]{1,0:T(8,128)(2,1)S(1)}, bf16[1536,512]{1,0:T(8,128)(2,1)}, u32[]{:S(2)}) copy-start(bf16[1536,512]{1,0:T(8,128)(2,1)} %w_query_ref.1) | copy-start | bytes 4718596
  11.5 7.8 %copy-start.4 = (bf16[1536,256]{1,0:T(8,128)(2,1)S(1)}, bf16[1536,256]{1,0:T(8,128)(2,1)}, u32[]{:S(2)}) copy-start(bf16[1536,256]{1,0:T(8,128)(2,1)} %w_keyval_ref.1) | copy-start | bytes 2359300
  11.5 35.7 %all-to-all-start = ((bf16[8,128,1024]{2,1,0:T(8,128)(2,1)}), bf16[8,128,1024]{2,1,0:T(8,128)(2,1)}, u32[]{:S(2)}, u32[]{:S(2)}) async-start(bf16[8,128,1024]{2,1,0:T(8,128)(2,1)} %broadcast_in_dim.8), calls=%async_computation | async-start | bytes 4194304 | tf_op jit(solution)/shard_map/all_to_all | solution.py:206
  17.5 28.1 %collective-permute-start = (bf16[128,1536]{1,0:T(8,128)(2,1)S(1)}, bf16[128,1536]{1,0:T(8,128)(2,1)S(1)}, u32[]{:S(2)}, u32[]{:S(2)}) collective-permute-start(bf16[128,1536]{1,0:T(8,128)(2,1)S(1)} %bitcast.31), channel_id=1, source_target_pairs={{0,1},{1,0},{2,3},{3,2},{4,5},{5,4},{6,7},{7,6},{8,9},{9,8},{10,11... | collective-permute-start | bytes 1179656 | tf_op jit(solution)/shard_map/ppermute | solution.py:34
  45.6 11.4 %copy-start.7 = (bf16[128,1536]{1,0:T(8,128)(2,1)}, bf16[128,1536]{1,0:T(8,128)(2,1)S(1)}, u32[]{:S(2)}) copy-start(bf16[128,1536]{1,0:T(8,128)(2,1)S(1)} %collective-permute-done.other_ref) | copy-start | bytes 1179652
  58.5 9.1 %all-to-all-start.1 = ((f32[8,16,512]{2,1,0:T(8,128)}), f32[8,16,512]{2,1,0:T(8,128)S(1)}, u32[]{:S(2)}, u32[]{:S(2)}) async-start(f32[8,16,512]{2,1,0:T(8,128)} %broadcast_in_dim.9), calls=%async_computation.1 | async-start | bytes 524288 | tf_op jit(solution)/shard_map/all_to_all | solution.py:206
  67.6 3.6 %copy-start.5 = (f32[8,16,512]{2,1,0:T(8,128)}, f32[8,16,512]{2,1,0:T(8,128)S(1)}, u32[]{:S(2)}) copy-start(f32[8,16,512]{2,1,0:T(8,128)S(1)} %all-to-all-done.1.stats_ref) | copy-start | bytes 786436
  67.6 17.3 %all-to-all-start.2 = ((bf16[8,128,512]{2,1,0:T(8,128)(2,1)}), bf16[8,128,512]{2,1,0:T(8,128)(2,1)S(1)}, u32[]{:S(2)}, u32[]{:S(2)}) async-start(bf16[8,128,512]{2,1,0:T(8,128)(2,1)} %get-tuple-element.35), calls=%async_computation.2 | async-start | bytes 2097152 | tf_op jit(solution)/shard_map/all_to_all | solution.py:206
  71.2 58.9 %reduce-scatter.2.cloned.1.call-start = ((), (), s32[]{:S(2)}) async-start(), calls=%async_computation.8 | async-start | bytes 1179648 | tf_op jit(solution)/shard_map/reduce_scatter | solution.py:265
  84.9 1.0 copy-start.2
  89.2 9.0 %collective-permute-start.1 = (bf16[512,768]{1,0:T(8,128)(2,1)}, bf16[512,768]{1,0:T(8,128)(2,1)S(1)}, u32[]{:S(2)}, u32[]{:S(2)}) collective-permute-start(bf16[512,768]{1,0:T(8,128)(2,1)} %get-tuple-element.38), channel_id=1, source_target_pairs={{0,1},{1,0},{2,3},{3,2},{4,5},{5,4},{6,7},{7,6},{8,9},{9,8},{10,11... | collective-permute-start | bytes 2359304 | tf_op jit(solution)/shard_map/ppermute | solution.py:34
  95.4 2.8 %copy-start.6 = (bf16[512,768]{1,0:T(8,128)(2,1)S(1)}, bf16[512,768]{1,0:T(8,128)(2,1)}, u32[]{:S(2)}) copy-start(bf16[512,768]{1,0:T(8,128)(2,1)} %get-tuple-element.37) | copy-start | bytes 2359300
  114.7 18.4 %all-to-all-start.3 = ((bf16[8,128,512]{2,1,0:T(8,128)(2,1)}), bf16[8,128,512]{2,1,0:T(8,128)(2,1)S(1)}, u32[]{:S(2)}, u32[]{:S(2)}) async-start(bf16[8,128,512]{2,1,0:T(8,128)(2,1)} %get-tuple-element.42), calls=%async_computation.3 | async-start | bytes 2097152 | tf_op jit(solution)/shard_map/all_to_all | solution.py:206
  133.2 1.0 copy-start.3
  136.4 2.9 %collective-permute-start.2 = (bf16[128,384]{1,0:T(8,128)(2,1)}, bf16[128,384]{1,0:T(8,128)(2,1)S(1)}, u32[]{:S(2)}, u32[]{:S(2)}) collective-permute-start(bf16[128,384]{1,0:T(8,128)(2,1)} %get-tuple-element.49), channel_id=1, source_target_pairs={{0,1},{1,0},{2,3},{3,2},{4,5},{5,4},{6,7},{7,6},{8,9},{9,8},{10,11... | collective-permute-start | bytes 294920 | tf_op jit(solution)/shard_map/ppermute | solution.py:34
  139.3 0.6 copy-start.8
  142.7 19.9 %all-to-all-start.5 = ((bf16[4,384,384]{2,1,0:T(8,128)(2,1)}), bf16[4,384,384]{2,1,0:T(8,128)(2,1)S(1)}, u32[]{:S(2)}, u32[]{:S(2)}) async-start(bf16[4,384,384]{2,1,0:T(8,128)(2,1)} %bitcast.33), calls=%async_computation.6 | async-start | bytes 2359296 | tf_op jit(solution)/shard_map/all_to_all | solution.py:206
  183.3 4.7 %collective-permute-start.3 = (f32[40,384]{1,0:T(8,128)S(1)}, f32[40,384]{1,0:T(8,128)S(1)}, u32[]{:S(2)}, u32[]{:S(2)}) collective-permute-start(f32[40,384]{1,0:T(8,128)S(1)} %convert_reduce_fusion.1), channel_id=1, source_target_pairs={{0,2},{2,0},{1,3},{3,1},{4,6},{6,4},{5,7},{7,5},{8,10},{10,8},{9,1... | collective-permute-start | bytes 184328 | tf_op jit(solution)/shard_map/ppermute | solution.py:34
  188.0 5.1 %collective-permute-start.4 = (f32[40,384]{1,0:T(8,128)S(1)}, f32[40,384]{1,0:T(8,128)S(1)}, u32[]{:S(2)}, u32[]{:S(2)}) collective-permute-start(f32[40,384]{1,0:T(8,128)S(1)} %add.13), channel_id=1, source_target_pairs={{0,1},{1,0},{2,3},{3,2},{4,5},{5,4},{6,7},{7,6},{8,9},{9,8},{10,11... | collective-permute-start | bytes 184328 | tf_op jit(solution)/shard_map/ppermute | solution.py:34
Sparse Core Ops, SparseCore 0:
  95.5 34.4 reduce-scatter.1

commit v6 on v5

--- a/solution.py
+++ b/solution.py
@@ -34,6 +34,13 @@
     return lax.ppermute(array, axis, [(i, (i + step) % size) for i in range(size)])
 
 
+def send_y(array, step_l, step_h):
+    pairs = [
+        (a * 2 + b, (a + step_l) % 2 * 2 + (b + step_h) % 2) for a in range(2) for b in range(2)
+    ]
+    return lax.ppermute(array, ("yl", "yh"), pairs)
+
+
 def rows_of(block):
     return jnp.concatenate(
         [block[:, h * HEAD_DIM : (h + 1) * HEAD_DIM] for h in range(HEADS)], axis=0
@@ -48,7 +55,7 @@
     return op(values.reshape(-1, 8, values.shape[1]), axis=0)
 
 
-def forward_kernel(qd, kv, mixed, stats_ref, vt, *scratch):
+def forward_kernel(qd, kv, mixed, stats_out, vt, stats_ref, *scratch):
     vt[...] = kv[:, HEAD_DIM:].T
 
     def scores(p, score):
@@ -80,6 +87,8 @@
         return carry
 
     lax.fori_loop(0, GROUP // 2, block, 0)
+    for i in range(GROUP):
+        stats_out[i] = stats_ref[...]
 
 
 def combine(logs, bars):
@@ -228,16 +237,17 @@
     keyval = jnp.dot(early, w_keyval, preferred_element_type=F32).astype(BF16)
     kvs = lax.all_gather(keyval, "z", axis=0, tiled=True)
     tokens_other = send(early, "core", 2, 1)
-    kvs, tokens_other = lax.optimization_barrier((kvs, tokens_other))
+    kvs, tokens_other, place = lax.optimization_barrier((kvs, tokens_other, place))
 
     mixed_parts, stats = call(
         forward_kernel,
         [qds, kvs],
-        [shape(8, HEAD_DIM, ROWS), shape(16, ROWS, dtype=F32)],
+        [shape(8, HEAD_DIM, ROWS), shape(8, 16, ROWS, dtype=F32)],
         [VM] * 2,
         [VM] * 2,
         [
             pltpu.VMEM((HEAD_DIM, KEYS), BF16),
+            pltpu.VMEM((16, ROWS), F32),
             pltpu.VMEM((KEYS, ROWS), F32),
             pltpu.VMEM((KEYS, ROWS), F32),
             pltpu.VMEM((KEYS, ROWS), BF16),
@@ -245,7 +255,7 @@
         ],
         10_000_000_000,
     )
-    all_stats = share(stats, ("x", "yl"), 8)
+    all_stats = swap(stats, ("x", "yl"))
     mixed_parts, all_stats = lax.optimization_barrier((mixed_parts, all_stats))
     mine = swap(mixed_parts, ("x", "yl"))
     dq_parts, dkv_parts = call(
@@ -280,13 +290,12 @@
         [VM] * 3,
         VM,
         [],
-        200_000_000,
+        20_000_000_000,
     )
     term_o, attended, dq_parts = lax.optimization_barrier((term_o, attended, dq_parts))
     dqs = swap(dq_parts, ("x", "yl"))
-    term_o = added(swap(term_o.reshape(4, 128, 768), "x"))
-    term_o = term_o.reshape(16, 8, 2, 384).transpose(0, 2, 1, 3).reshape(16, 16, 384)
-    dkv, term_o = lax.optimization_barrier((dkv, term_o))
+    term_o = swap(term_o.reshape(4, 128, 768), "x")
+    dqs, term_o = lax.optimization_barrier((dqs, term_o))
 
     both, keep_i, give_i = call(
         input_kernel,
@@ -315,17 +324,35 @@
         [],
         300_000_000,
     )
+    yl, yh = lax.axis_index("yl"), lax.axis_index("yh")
+    blocks = added(term_o).astype(BF16).reshape(8, 2, 8, 2, 384)
+    blocks = blocks.transpose(1, 3, 0, 2, 4).reshape(4, 64, 384)
+
+    def block(step_l, step_h):
+        at = (yl + step_l) % 2 * 2 + (yh + step_h) % 2
+        return lax.dynamic_index_in_dim(blocks, at, 0, keepdims=False)
+
+    steps = [(0, 1), (1, 0), (1, 1)]
+    term_o = block(0, 0).astype(F32)
+    term_o = term_o + sum(send_y(block(*step), *step).astype(F32) for step in steps)
     term_i = swap(term_i.reshape(4, 384, 384), "x")
-    grad_tokens, term_i = lax.optimization_barrier((grad_tokens, term_i))
-    term_i = added(term_i)
-    ends = jnp.concatenate([term_i.reshape(16, 24, 384), term_o], axis=1).astype(BF16)
-    ends = swap(ends, ("z", "yl"))
-    ends = added(ends)
-    ends = ends + send(ends, "yh", 2, 1)
+    grad_tokens, term_i, term_o = lax.optimization_barrier((grad_tokens, term_i, term_o))
+    term_i = added(term_i).reshape(8, 2, 24, 384)
+    here = (jnp.arange(2) == lax.axis_index("yl"))[None, :, None, None]
+    term_o = jnp.where(here, term_o.reshape(8, 1, 8, 384), 0.0)
+    ends = jnp.concatenate([term_i, term_o], axis=2).astype(BF16).reshape(16, 32, 384)
+    ends = added(swap(ends, ("z", "yl")))
+    got = send(ends, "yh", 2, 1)
+    ends = jnp.concatenate(
+        [
+            ends[:24] + got[:24],
+            jnp.where(yh == 0, ends[24:], got[24:]),
+            jnp.where(yh == 0, got[24:], ends[24:]),
+        ]
+    )
     other = send(ends, "core", 2, 1)
     low, high = jnp.where(core == 0, ends, other), jnp.where(core == 0, other, ends)
-    grad_o = jnp.stack([low[24:], high[24:]]).reshape(2, 2, 8, 384)
-    grad_o = grad_o.transpose(2, 0, 1, 3).reshape(8, 1536)
+    grad_o = jnp.concatenate([low[24:32], low[32:], high[24:32], high[32:]], axis=1)
     return (
         attended[None],
         grad_tokens[None],

time: 203 us -> 199 us (0.980)
  blocking collectives: 62.6 us -> 87.9 us
  waiting for transfers between devices: 38.1 us -> 13.9 us
  starting transfers between devices: 37.3 us -> 34 us
  local copies, waits for them, and re-layouts: 5.7 us -> 3.42 us
    all_to_all x2 -> x4, blocking collectives: 36.6 us -> 61.9 us  [swap(): return lax.all_to_all(blocks, axes, 0, 0)]
    all_to_all x5 -> x3, waiting for transfers between devices: 22.5 us -> 9.36 us  [swap(): return lax.all_to_all(blocks, axes, 0, 0)]
    reduce_scatter x1, waiting for transfers between devices: 11.6 us -> 0.01 us  [body(): dkv = lax.psum_scatter(dkv_parts, 'z', scatter_dimension=0, tiled=True)]
    all_to_all x5 -> x3, starting transfers between devices: 20.5 us -> 13.1 us  [swap(): return lax.all_to_all(blocks, axes, 0, 0)]
    ppermute x0 -> x3, starting transfers between devices: none -> 3.41 us  [send_y(): return lax.ppermute(array, ('yl', 'yh'), pairs)]
  transfers between devices with their start and end apart: 11 -> 12, of which waited for: 8 -> 6; matrix products, arithmetic and copies ran while one was open for 1% -> 1% of each run, Pallas kernels for 10% -> 12%
where the time goes in v6:
time: 199 us; the launch traced here: 198 us
  blocking collectives  87.9 us (44%)
  Pallas kernels  37.9 us (19%)
  starting transfers between devices  34 us (17%)
  between operations  14.3 us (7%)
  waiting for transfers between devices  13.9 us (7%)
  local copies, waits for them, and re-layouts  3.42 us (2%)
  other arithmetic  3.32 us (2%)
  matrix products  2.95 us (1%)
    all_to_all x4, blocking collectives, swap(): return lax.all_to_all(blocks, axes, 0, 0)  61.9 us
    pallas_call x7, Pallas kernels, call(): pl.pallas_call(kernel, out_shape=outs, in_specs=in_specs, out_specs=out_s...  37.9 us
    all_gather x1, blocking collectives, body(): kvs = lax.all_gather(keyval, 'z', axis=0, tiled=True)  26 us
    ppermute x5, starting transfers between devices, send(): lax.ppermute(array, axis, [(i, (i + step) % size) for i in range(size)])  17.4 us
    all_to_all x3, starting transfers between devices, swap(): return lax.all_to_all(blocks, axes, 0, 0)  13.1 us
    all_to_all x3, waiting for transfers between devices, swap(): return lax.all_to_all(blocks, axes, 0, 0)  9.36 us
  transfers between devices with their start and end apart: 12, of which 6 were waited for; matrix products, arithmetic and copies ran while one was open for 1% of the time, Pallas kernels for 12%

profile of v6, /device:TPU:1, one launch (start us, length us, event | category | flops | bytes accessed | tf_op | source)
XLA Modules:
  0.0 197.8 jit_solution(16200205661557753794)
XLA Ops:
  7.2 2.3 %convolution_convert_fusion = bf16[128,512]{1,0:T(8,128)(2,1)S(1)} fusion(bf16[512,1536]{1,0:T(8,128)(2,1)} %w_out_ref.1, bf16[1,128,1536]{2,1,0:T(8,128)(2,1)} %param.6), kind=kOutput, calls=%fused_computation.1 | convolution fusion | flops 201392128 | bytes 2097152 | tf_op jit(solution)/shard_map/dot_general | solution.py:233
  11.5 6.0 %all-to-all-start = ((bf16[8,128,1024]{2,1,0:T(8,128)(2,1)}), bf16[8,128,1024]{2,1,0:T(8,128)(2,1)}, u32[]{:S(2)}, u32[]{:S(2)}) async-start(bf16[8,128,1024]{2,1,0:T(8,128)(2,1)} %broadcast_in_dim.41), calls=%async_computation | async-start | bytes 4194304 | tf_op jit(solution)/shard_map/all_to_all | solution.py:215
  17.5 1.8 collective-permute-start
  20.2 26.0 %all_gather.3.kv = bf16[1024,256]{1,0:T(8,128)(2,1)} all-gather(bf16[128,256]{1,0:T(8,128)(2,1)S(1)} %convolution_convert_fusion.2), channel_id=1, replica_groups=mesh['x'=4,'z'=8,'yl'=2,'yh'=2,'core'=2] {'z'}, dimensions={0}, use_global_device_ids=true | all-gather | bytes 589824 | tf_op jit(solution)/shard_map/all_gather | solution.py:238
  47.2 9.9 %shard_map.92 = (bf16[8,128,512]{2,1,0:T(8,128)(2,1)}, f32[8,16,512]{2,1,0:T(8,128)}) custom-call(bf16[8,128,1024]{2,1,0:T(8,128)(2,1)} %all-to-all-done.qd, bf16[1024,256]{1,0:T(8,128)(2,1)} %all_gather.3.kv), custom_call_target="tpu_custom_call" | custom-call | flops 10000000000 | bytes 6000000 | tf_op jit(solution)/shard_map/pallas_call | solution.py:199
  57.1 9.8 %all_to_all.35.stats_ref = f32[8,16,512]{2,1,0:T(8,128)} all-to-all(f32[8,16,512]{2,1,0:T(8,128)} %get-tuple-element.35), channel_id=1, replica_groups=mesh['x'=4,'z'=8,'yl'=2,'yh'=2,'core'=2] {'x','yl'}, dimensions={0} | all-to-all | bytes 524288 | tf_op jit(solution)/shard_map/all_to_all | solution.py:215
  66.9 3.6 %all-to-all-start.2 = ((bf16[8,128,512]{2,1,0:T(8,128)(2,1)}), bf16[8,128,512]{2,1,0:T(8,128)(2,1)S(1)}, u32[]{:S(2)}, u32[]{:S(2)}) async-start(bf16[8,128,512]{2,1,0:T(8,128)(2,1)} %get-tuple-element.38), calls=%async_computation.2 | async-start | bytes 2097152 | tf_op jit(solution)/shard_map/all_to_all | solution.py:215
  70.5 13.7 %shard_map.93 = (bf16[8,128,512]{2,1,0:T(8,128)(2,1)}, f32[1024,256]{1,0:T(8,128)}) custom-call(bf16[8,128,1024]{2,1,0:T(8,128)(2,1)} %all-to-all-done.qd, f32[8,16,512]{2,1,0:T(8,128)} %all_to_all.35.stats_ref, bf16[1024,256]{1,0:T(8,128)(2,1)} %all_gather.3.kv), custom_call_target="tpu_custom_call" | custom-call | flops 16000000000 | bytes 6000000 | tf_op jit(solution)/shard_map/pallas_call | solution.py:199
  85.2 3.2 %shard_map.94 = (bf16[128,512]{1,0:T(8,128)(2,1)}, bf16[512,768]{1,0:T(8,128)(2,1)}, bf16[512,768]{1,0:T(8,128)(2,1)}) custom-call(s32[2]{0:T(128)} %pad_add_fusion.place, bf16[8,128,512]{2,1,0:T(8,128)(2,1)} %copy-done.1, f32[8,16,512]{2,1,0:T(8,128)} %all_to_all.35.stats_ref, bf16[128,1536]{1,0:T(8,128)(2,1)} %bitcast.39), custom_call_target="tpu_custom_call" | custom-call | flops 400000000 | bytes 6000000 | tf_op jit(solution)/shard_map/pallas_call | solution.py:199
  88.4 6.2 %collective-permute-start.1 = (bf16[512,768]{1,0:T(8,128)(2,1)}, bf16[512,768]{1,0:T(8,128)(2,1)S(1)}, u32[]{:S(2)}, u32[]{:S(2)}) collective-permute-start(bf16[512,768]{1,0:T(8,128)(2,1)} %get-tuple-element.41), channel_id=1, source_target_pairs={{0,1},{1,0},{2,3},{3,2},{4,5},{5,4},{6,7},{7,6},{8,9},{9,8},{10,11... | collective-permute-start | bytes 2359304 | tf_op jit(solution)/shard_map/ppermute | solution.py:34
  94.6 2.8 %shard_map.95 = bf16[128,1536]{1,0:T(8,128)(2,1)} custom-call(bf16[128,1536]{1,0:T(8,128)(2,1)} %bitcast.34, bf16[128,512]{1,0:T(8,128)(2,1)} %get-tuple-element.42.mixed_ref, bf16[512,1536]{1,0:T(8,128)(2,1)} %w_out_ref.1), custom_call_target="tpu_custom_call" | custom-call | flops 20000000000 | bytes 6000000 | tf_op jit(solution)/shard_map/pallas_call | solution.py:199
  97.6 16.4 %all_to_all.36 = bf16[4,128,768]{2,1,0:T(8,128)(2,1)S(1)} all-to-all(bf16[4,128,768]{2,1,0:T(8,128)(2,1)S(1)} %bitcast.38), channel_id=1, replica_groups=mesh['x'=4,'z'=8,'yl'=2,'yh'=2,'core'=2] {'x'}, dimensions={0} | all-to-all | bytes 1572864 | tf_op jit(solution)/shard_map/all_to_all | solution.py:215
  114.1 17.0 %all_to_all.37.dq_ref = bf16[8,128,512]{2,1,0:T(8,128)(2,1)} all-to-all(bf16[8,128,512]{2,1,0:T(8,128)(2,1)S(1)} %copy-done.4), channel_id=1, replica_groups=mesh['x'=4,'z'=8,'yl'=2,'yh'=2,'core'=2] {'x','yl'}, dimensions={0} | all-to-all | bytes 2097152 | tf_op jit(solution)/shard_map/all_to_all | solution.py:215
  131.0 2.2 %shard_map.96 = (bf16[128,768]{1,0:T(8,128)(2,1)}, bf16[128,384]{1,0:T(8,128)(2,1)}, bf16[128,384]{1,0:T(8,128)(2,1)}) custom-call(s32[2]{0:T(128)} %pad_add_fusion.place, bf16[8,128,512]{2,1,0:T(8,128)(2,1)} %all_to_all.37.dq_ref, f32[128,256]{1,0:T(8,128)} %reduce-scatter.2.cloned.1.call-done.dkv_ref), custom_call_target="tpu_custom_call" | custom-call | flops 10000000 | bytes 6000000 | tf_op jit(solution)/shard_map/pallas_call | solution.py:199
  133.3 2.4 %collective-permute-start.2 = (bf16[128,384]{1,0:T(8,128)(2,1)}, bf16[128,384]{1,0:T(8,128)(2,1)S(1)}, u32[]{:S(2)}, u32[]{:S(2)}) collective-permute-start(bf16[128,384]{1,0:T(8,128)(2,1)} %get-tuple-element.52), channel_id=1, source_target_pairs={{0,1},{1,0},{2,3},{3,2},{4,5},{5,4},{6,7},{7,6},{8,9},{9,8},{10,11... | collective-permute-start | bytes 294920 | tf_op jit(solution)/shard_map/ppermute | solution.py:34
  137.5 2.8 %shard_map.98 = bf16[1536,384]{1,0:T(8,128)(2,1)} custom-call(bf16[128,1536]{1,0:T(8,128)(2,1)} %bitcast.35, bf16[128,1536]{1,0:T(8,128)(2,1)} %copy-done.6, bf16[128,384]{1,0:T(8,128)(2,1)} %get-tuple-element.51.keep_ref, bf16[128,384]{1,0:T(8,128)(2,1)} %copy-done.7), custom_call_target="tpu_custom_call" | custom-call | flops 300000000 | bytes 6000000 | tf_op jit(solution)/shard_map/pallas_call | solution.py:199
  140.3 3.5 %all-to-all-start.5 = ((bf16[4,384,384]{2,1,0:T(8,128)(2,1)}), bf16[4,384,384]{2,1,0:T(8,128)(2,1)S(1)}, u32[]{:S(2)}, u32[]{:S(2)}) async-start(bf16[4,384,384]{2,1,0:T(8,128)(2,1)} %bitcast.33), calls=%async_computation.6 | async-start | bytes 2359296 | tf_op jit(solution)/shard_map/all_to_all | solution.py:215
  144.1 2.8 %collective-permute-start.3 = (bf16[64,384]{1,0:T(8,128)(2,1)S(1)}, bf16[64,384]{1,0:T(8,128)(2,1)S(1)}, u32[]{:S(2)}, u32[]{:S(2)}) collective-permute-start(bf16[64,384]{1,0:T(8,128)(2,1)S(1)} %get-tuple-element.57), channel_id=1, source_target_pairs={{0,2},{2,0},{4,6},{6,4},{1,3},{3,1},{5,7},{7,5},{8,10},{10,8},{12,... | collective-permute-start | bytes 147464 | tf_op jit(solution)/shard_map/ppermute | solution.py:41
  147.6 3.3 %shard_map.97 = bf16[128,1536]{1,0:T(8,128)(2,1)} custom-call(bf16[128,768]{1,0:T(8,128)(2,1)} %get-tuple-element.49.both_ref, bf16[1536,512]{1,0:T(8,128)(2,1)} %w_query_ref.1, bf16[1536,256]{1,0:T(8,128)(2,1)} %w_keyval_ref.1), custom_call_target="tpu_custom_call" | custom-call | flops 300000000 | bytes 6000000 | tf_op jit(solution)/shard_map/pallas_call | solution.py:199
  151.7 8.4 %all-to-all-done.5 = bf16[4,384,384]{2,1,0:T(8,128)(2,1)S(1)} async-done(((bf16[4,384,384]{2,1,0:T(8,128)(2,1)}), bf16[4,384,384]{2,1,0:T(8,128)(2,1)S(1)}, u32[]{:S(2)}, u32[]{:S(2)}) %all-to-all-start.5) | async-done | bytes 1179680 | tf_op jit(solution)/shard_map/all_to_all | solution.py:215
  160.5 18.7 %all_to_all.38 = bf16[16,32,384]{2,1,0:T(8,128)(2,1)S(1)} all-to-all(bf16[16,32,384]{2,1,0:T(8,128)(2,1)S(1)} %pad_maximum_fusion), channel_id=1, replica_groups=mesh['x'=4,'z'=8,'yl'=2,'yh'=2,'core'=2] {'z','yl'}, dimensions={0} | all-to-all | bytes 786432 | tf_op jit(solution)/shard_map/all_to_all | solution.py:215
  179.3 2.7 %collective-permute-start.6 = (f32[32,384]{1,0:T(8,128)S(1)}, f32[32,384]{1,0:T(8,128)S(1)}, u32[]{:S(2)}, u32[]{:S(2)}) collective-permute-start(f32[32,384]{1,0:T(8,128)S(1)} %convert_reduce_fusion), channel_id=1, source_target_pairs={{0,2},{2,0},{1,3},{3,1},{4,6},{6,4},{5,7},{7,5},{8,10},{10,8},{9,1... | collective-permute-start | bytes 147464 | tf_op jit(solution)/shard_map/ppermute | solution.py:34
  182.0 1.8 collective-permute-done.6
  183.8 4.3 %collective-permute-start.7 = (f32[40,384]{1,0:T(8,128)S(1)}, f32[40,384]{1,0:T(8,128)S(1)}, u32[]{:S(2)}, u32[]{:S(2)}) collective-permute-start(f32[40,384]{1,0:T(8,128)S(1)} %pad_maximum_fusion.2), channel_id=1, source_target_pairs={{0,1},{1,0},{2,3},{3,2},{4,5},{5,4},{6,7},{7,6},{8,9},{9,8},{10,11... | collective-permute-start | bytes 184328 | tf_op jit(solution)/shard_map/ppermute | solution.py:34
  (60 shorter events, 11.8 us)
Async XLA Ops:
  7.2 2.3 %copy-start.2 = (bf16[1,128,1536]{2,1,0:T(8,128)(2,1)S(1)}, bf16[1,128,1536]{2,1,0:T(8,128)(2,1)}, u32[]{:S(2)}) copy-start(bf16[1,128,1536]{2,1,0:T(8,128)(2,1)} %param.5) | copy-start | bytes 1179652
  7.2 2.3 %copy-start = (bf16[1536,512]{1,0:T(8,128)(2,1)S(1)}, bf16[1536,512]{1,0:T(8,128)(2,1)}, u32[]{:S(2)}) copy-start(bf16[1536,512]{1,0:T(8,128)(2,1)} %w_query_ref.1) | copy-start | bytes 4718596
  11.5 7.8 %copy-start.3 = (bf16[1536,256]{1,0:T(8,128)(2,1)S(1)}, bf16[1536,256]{1,0:T(8,128)(2,1)}, u32[]{:S(2)}) copy-start(bf16[1536,256]{1,0:T(8,128)(2,1)} %w_keyval_ref.1) | copy-start | bytes 2359300
  11.5 35.7 %all-to-all-start = ((bf16[8,128,1024]{2,1,0:T(8,128)(2,1)}), bf16[8,128,1024]{2,1,0:T(8,128)(2,1)}, u32[]{:S(2)}, u32[]{:S(2)}) async-start(bf16[8,128,1024]{2,1,0:T(8,128)(2,1)} %broadcast_in_dim.41), calls=%async_computation | async-start | bytes 4194304 | tf_op jit(solution)/shard_map/all_to_all | solution.py:215
  17.5 28.7 %collective-permute-start = (bf16[128,1536]{1,0:T(8,128)(2,1)S(1)}, bf16[128,1536]{1,0:T(8,128)(2,1)S(1)}, u32[]{:S(2)}, u32[]{:S(2)}) collective-permute-start(bf16[128,1536]{1,0:T(8,128)(2,1)S(1)} %bitcast.36), channel_id=1, source_target_pairs={{0,1},{1,0},{2,3},{3,2},{4,5},{5,4},{6,7},{7,6},{8,9},{9,8},{10,11... | collective-permute-start | bytes 1179656 | tf_op jit(solution)/shard_map/ppermute | solution.py:34
  46.2 10.9 %copy-start.6 = (bf16[128,1536]{1,0:T(8,128)(2,1)}, bf16[128,1536]{1,0:T(8,128)(2,1)S(1)}, u32[]{:S(2)}) copy-start(bf16[128,1536]{1,0:T(8,128)(2,1)S(1)} %collective-permute-done.other_ref) | copy-start | bytes 1179652
  66.9 17.3 %all-to-all-start.2 = ((bf16[8,128,512]{2,1,0:T(8,128)(2,1)}), bf16[8,128,512]{2,1,0:T(8,128)(2,1)S(1)}, u32[]{:S(2)}, u32[]{:S(2)}) async-start(bf16[8,128,512]{2,1,0:T(8,128)(2,1)} %get-tuple-element.38), calls=%async_computation.2 | async-start | bytes 2097152 | tf_op jit(solution)/shard_map/all_to_all | solution.py:215
  70.4 60.6 %reduce-scatter.2.cloned.1.call-start = ((), (), s32[]{:S(2)}) async-start(), calls=%async_computation.8 | async-start | bytes 1179648 | tf_op jit(solution)/shard_map/reduce_scatter | solution.py:275
  84.2 1.0 copy-start.1
  88.4 9.0 %collective-permute-start.1 = (bf16[512,768]{1,0:T(8,128)(2,1)}, bf16[512,768]{1,0:T(8,128)(2,1)S(1)}, u32[]{:S(2)}, u32[]{:S(2)}) collective-permute-start(bf16[512,768]{1,0:T(8,128)(2,1)} %get-tuple-element.41), channel_id=1, source_target_pairs={{0,1},{1,0},{2,3},{3,2},{4,5},{5,4},{6,7},{7,6},{8,9},{9,8},{10,11... | collective-permute-start | bytes 2359304 | tf_op jit(solution)/shard_map/ppermute | solution.py:34
  94.6 2.8 %copy-start.5 = (bf16[512,768]{1,0:T(8,128)(2,1)S(1)}, bf16[512,768]{1,0:T(8,128)(2,1)}, u32[]{:S(2)}) copy-start(bf16[512,768]{1,0:T(8,128)(2,1)} %get-tuple-element.40) | copy-start | bytes 2359300
  97.4 16.6 %copy-start.4 = (bf16[8,128,512]{2,1,0:T(8,128)(2,1)S(1)}, bf16[8,128,512]{2,1,0:T(8,128)(2,1)}, u32[]{:S(2)}) copy-start(bf16[8,128,512]{2,1,0:T(8,128)(2,1)} %get-tuple-element.45) | copy-start | bytes 3145732
  133.3 3.6 %collective-permute-start.2 = (bf16[128,384]{1,0:T(8,128)(2,1)}, bf16[128,384]{1,0:T(8,128)(2,1)S(1)}, u32[]{:S(2)}, u32[]{:S(2)}) collective-permute-start(bf16[128,384]{1,0:T(8,128)(2,1)} %get-tuple-element.52), channel_id=1, source_target_pairs={{0,1},{1,0},{2,3},{3,2},{4,5},{5,4},{6,7},{7,6},{8,9},{9,8},{10,11... | collective-permute-start | bytes 294920 | tf_op jit(solution)/shard_map/ppermute | solution.py:34
  136.9 0.6 copy-start.7
  140.3 19.8 %all-to-all-start.5 = ((bf16[4,384,384]{2,1,0:T(8,128)(2,1)}), bf16[4,384,384]{2,1,0:T(8,128)(2,1)S(1)}, u32[]{:S(2)}, u32[]{:S(2)}) async-start(bf16[4,384,384]{2,1,0:T(8,128)(2,1)} %bitcast.33), calls=%async_computation.6 | async-start | bytes 2359296 | tf_op jit(solution)/shard_map/all_to_all | solution.py:215
  144.1 6.8 %collective-permute-start.3 = (bf16[64,384]{1,0:T(8,128)(2,1)S(1)}, bf16[64,384]{1,0:T(8,128)(2,1)S(1)}, u32[]{:S(2)}, u32[]{:S(2)}) collective-permute-start(bf16[64,384]{1,0:T(8,128)(2,1)S(1)} %get-tuple-element.57), channel_id=1, source_target_pairs={{0,2},{2,0},{4,6},{6,4},{1,3},{3,1},{5,7},{7,5},{8,10},{10,8},{12,... | collective-permute-start | bytes 147464 | tf_op jit(solution)/shard_map/ppermute | solution.py:41
  146.9 4.1 %collective-permute-start.4 = (bf16[64,384]{1,0:T(8,128)(2,1)S(1)}, bf16[64,384]{1,0:T(8,128)(2,1)S(1)}, u32[]{:S(2)}, u32[]{:S(2)}) collective-permute-start(bf16[64,384]{1,0:T(8,128)(2,1)S(1)} %get-tuple-element.59), channel_id=1, source_target_pairs={{0,4},{2,6},{4,0},{6,2},{1,5},{3,7},{5,1},{7,3},{8,12},{10,14},{12... | collective-permute-start | bytes 147464 | tf_op jit(solution)/shard_map/ppermute | solution.py:41
  147.2 4.4 %collective-permute-start.5 = (bf16[64,384]{1,0:T(8,128)(2,1)S(1)}, bf16[64,384]{1,0:T(8,128)(2,1)S(1)}, u32[]{:S(2)}, u32[]{:S(2)}) collective-permute-start(bf16[64,384]{1,0:T(8,128)(2,1)S(1)} %get-tuple-element.58), channel_id=1, source_target_pairs={{0,6},{2,4},{4,2},{6,0},{1,7},{3,5},{5,3},{7,1},{8,14},{10,12},{12... | collective-permute-start | bytes 147464 | tf_op jit(solution)/shard_map/ppermute | solution.py:41
  179.3 4.5 %collective-permute-start.6 = (f32[32,384]{1,0:T(8,128)S(1)}, f32[32,384]{1,0:T(8,128)S(1)}, u32[]{:S(2)}, u32[]{:S(2)}) collective-permute-start(f32[32,384]{1,0:T(8,128)S(1)} %convert_reduce_fusion), channel_id=1, source_target_pairs={{0,2},{2,0},{1,3},{3,1},{4,6},{6,4},{5,7},{7,5},{8,10},{10,8},{9,1... | collective-permute-start | bytes 147464 | tf_op jit(solution)/shard_map/ppermute | solution.py:34
  183.8 5.2 %collective-permute-start.7 = (f32[40,384]{1,0:T(8,128)S(1)}, f32[40,384]{1,0:T(8,128)S(1)}, u32[]{:S(2)}, u32[]{:S(2)}) collective-permute-start(f32[40,384]{1,0:T(8,128)S(1)} %pad_maximum_fusion.2), channel_id=1, source_target_pairs={{0,1},{1,0},{2,3},{3,2},{4,5},{5,4},{6,7},{7,6},{8,9},{9,8},{10,11... | collective-permute-start | bytes 184328 | tf_op jit(solution)/shard_map/ppermute | solution.py:34
Sparse Core Ops, SparseCore 0:
  84.3 40.6 reduce-scatter.1

commit v7 on v6

--- a/solution.py
+++ b/solution.py
@@ -55,7 +55,7 @@
     return op(values.reshape(-1, 8, values.shape[1]), axis=0)
 
 
-def forward_kernel(qd, kv, mixed, stats_out, vt, stats_ref, *scratch):
+def forward_kernel(qd, kv, mixed, stats_out, tops, kept, vt, stats_ref, sem, *scratch):
     vt[...] = kv[:, HEAD_DIM:].T
 
     def scores(p, score):
@@ -67,6 +67,7 @@
             top = jnp.maximum(top, fold(score[part, :], jnp.max))
         top = jnp.max(top, axis=0, keepdims=True)
         base = top * (SCALE * LOG2E)
+        tops[pl.ds(p, 1), :] = top * SCALE
         total = jnp.zeros((8, ROWS), F32)
         for part in tiles(KEYS):
             e = jnp.exp2(score[part, :] * (SCALE * LOG2E) - base)
@@ -79,14 +80,25 @@
         d4 = rows_of(qd[p, :, ROWS:])
         stats_ref[pl.ds(8 + p, 1), :] = jnp.sum(acc * d4.T.astype(F32), axis=0, keepdims=True)
 
+    def keep(p, n):
+        return pltpu.make_async_copy(scratch[2 + n], kept.at[p], sem.at[n])
+
     def block(i, carry):
         for n in range(2):
             scores(2 * i + n, scratch[n])
         for n in range(2):
+
+            @pl.when(i > 0)
+            def _():
+                keep(2 * i + n - 2, n).wait()
+
             softmax(2 * i + n, scratch[n], scratch[2 + n])
+            keep(2 * i + n, n).start()
         return carry
 
     lax.fori_loop(0, GROUP // 2, block, 0)
+    for n in range(2):
+        keep(GROUP - 2 + n, n).wait()
     for i in range(GROUP):
         stats_out[i] = stats_ref[...]
 
@@ -99,38 +111,46 @@
     return top + jnp.log(total), jnp.sum(weights * bars, axis=0), weights
 
 
-def backward_kernel(qd, stats_ref, kv, dq, dkv, kt, stat, *scratch):
+def backward_kernel(qd, stats_ref, tops, kv, kept, dq, dkv, kt, stat, held, sem, *scratch):
+    def fetch(p, slot):
+        return pltpu.make_async_copy(kept.at[p], held.at[slot], sem.at[slot])
+
+    for n in range(2):
+        fetch(n, n).start()
     kt[...] = kv[:, :HEAD_DIM].T
     logsum, delta, unused = combine(stats_ref[:, :8, :], stats_ref[:, 8:, :])
-    stat[:8, :] = logsum * LOG2E
+    stat[:8, :] = jnp.exp(tops[...] - logsum)
     stat[8:, :] = delta
     dkv[...] = jnp.zeros_like(dkv)
 
-    def rows(p):
-        return rows_of(qd[p, :, :ROWS]), rows_of(qd[p, :, ROWS:])
-
-    def products(p, score, dprob):
-        q4, d4 = rows(p)
-        score[...] = dot(kv[:, :HEAD_DIM], q4, NT)
-        dprob[...] = dot(kv[:, HEAD_DIM:], d4, NT)
-
-    def gradients(p, score, dprob, weight, dscore):
-        base = stat[pl.ds(p, 1), :]
+    def rows(p, first):
+        return rows_of(qd[p, :, first : first + ROWS])
+
+    def gradients(p, slot, dprob, weight, dscore):
+        share_here = stat[pl.ds(p, 1), :]
         delta = stat[pl.ds(8 + p, 1), :]
         for tile in tiles(KEYS):
-            prob = jnp.exp2(score[tile, :] * (SCALE * LOG2E) - base)
+            prob = held[slot, tile, :].astype(F32) * share_here
             weight[tile, :] = prob.astype(BF16)
             dscore[tile, :] = (prob * (dprob[tile, :] - delta)).astype(BF16)
-        q4, d4 = rows(p)
-        dkv[:, HEAD_DIM:] += dot(weight[...], d4)
-        dkv[:, :HEAD_DIM] += dot(dscore[...], q4)
+        dkv[:, HEAD_DIM:] += dot(weight[...], rows(p, ROWS))
+        dkv[:, :HEAD_DIM] += dot(dscore[...], rows(p, 0))
         dq[p] = (dot(kt[...], dscore[...]) * SCALE).astype(BF16)
 
     def block(i, carry):
+        slot = i % 2 * 2
+
+        @pl.when(i + 1 < GROUP // 2)
+        def _():
+            for n in range(2):
+                fetch(2 * i + 2 + n, 2 - slot + n).start()
+
         for n in range(2):
-            products(2 * i + n, *scratch[4 * n : 4 * n + 2])
+            scratch[3 * n][...] = dot(kv[:, HEAD_DIM:], rows(2 * i + n, ROWS), NT)
         for n in range(2):
-            gradients(2 * i + n, *scratch[4 * n : 4 * n + 4])
+            fetch(2 * i + n, slot + n).wait()
+        for n in range(2):
+            gradients(2 * i + n, slot + n, *scratch[3 * n : 3 * n + 3])
         return carry
 
     lax.fori_loop(0, GROUP // 2, block, 0)
@@ -193,6 +213,7 @@
 
 VM = pl.BlockSpec(memory_space=pltpu.VMEM)
 SM = pl.BlockSpec(memory_space=pltpu.SMEM)
+HB = pl.BlockSpec(memory_space=pl.ANY)
 
 
 def call(kernel, ins, outs, in_specs, out_specs, scratch, flops):
@@ -239,15 +260,21 @@
     tokens_other = send(early, "core", 2, 1)
     kvs, tokens_other, place = lax.optimization_barrier((kvs, tokens_other, place))
 
-    mixed_parts, stats = call(
+    mixed_parts, stats, tops, kept = call(
         forward_kernel,
         [qds, kvs],
-        [shape(8, HEAD_DIM, ROWS), shape(8, 16, ROWS, dtype=F32)],
+        [
+            shape(8, HEAD_DIM, ROWS),
+            shape(8, 16, ROWS, dtype=F32),
+            shape(8, ROWS, dtype=F32),
+            shape(8, KEYS, ROWS),
+        ],
         [VM] * 2,
-        [VM] * 2,
+        [VM] * 3 + [HB],
         [
             pltpu.VMEM((HEAD_DIM, KEYS), BF16),
             pltpu.VMEM((16, ROWS), F32),
+            pltpu.SemaphoreType.DMA((2,)),
             pltpu.VMEM((KEYS, ROWS), F32),
             pltpu.VMEM((KEYS, ROWS), F32),
             pltpu.VMEM((KEYS, ROWS), BF16),
@@ -260,15 +287,17 @@
     mine = swap(mixed_parts, ("x", "yl"))
     dq_parts, dkv_parts = call(
         backward_kernel,
-        [qds, all_stats, kvs],
+        [qds, all_stats, tops, kvs, kept],
         [shape(8, HEAD_DIM, ROWS), shape(KEYS, 2 * HEAD_DIM, dtype=F32)],
-        [VM] * 3,
+        [VM] * 4 + [HB],
         [VM] * 2,
         [
             pltpu.VMEM((HEAD_DIM, KEYS), BF16),
             pltpu.VMEM((16, ROWS), F32),
+            pltpu.VMEM((4, KEYS, ROWS), BF16),
+            pltpu.SemaphoreType.DMA((4,)),
         ]
-        + [pltpu.VMEM((KEYS, ROWS), t) for t in (F32, F32, BF16, BF16)] * 2,
+        + [pltpu.VMEM((KEYS, ROWS), t) for t in (F32, BF16, BF16)] * 2,
         16_000_000_000,
     )
     dq_parts, mine = lax.optimization_barrier((dq_parts, mine))

time: 199 us -> 200 us (level)
  transfers between devices with their start and end apart: 12 -> 12, of which waited for: 6 -> 6; matrix products, arithmetic and copies ran while one was open for 1% -> 1% of each run, Pallas kernels for 12% -> 11%
where the time goes in v7:
time: 200 us; the launch traced here: 199 us
  blocking collectives  87.9 us (44%)
  Pallas kernels  39.2 us (20%)
  starting transfers between devices  34 us (17%)
  between operations  14.3 us (7%)
  waiting for transfers between devices  13.9 us (7%)
  local copies, waits for them, and re-layouts  3.45 us (2%)
  other arithmetic  3.32 us (2%)
  matrix products  2.95 us (1%)
    all_to_all x4, blocking collectives, swap(): return lax.all_to_all(blocks, axes, 0, 0)  62 us
    pallas_call x7, Pallas kernels, call(): pl.pallas_call(kernel, out_shape=outs, in_specs=in_specs, out_specs=out_s...  39.2 us
    all_gather x1, blocking collectives, body(): kvs = lax.all_gather(keyval, 'z', axis=0, tiled=True)  26 us
    ppermute x5, starting transfers between devices, send(): lax.ppermute(array, axis, [(i, (i + step) % size) for i in range(size)])  17.5 us
    all_to_all x3, starting transfers between devices, swap(): return lax.all_to_all(blocks, axes, 0, 0)  13.1 us
    all_to_all x3, waiting for transfers between devices, swap(): return lax.all_to_all(blocks, axes, 0, 0)  9.34 us
  transfers between devices with their start and end apart: 12, of which 6 were waited for; matrix products, arithmetic and copies ran while one was open for 1% of the time, Pallas kernels for 11%

profile of v7, /device:TPU:1, one launch (start us, length us, event | category | flops | bytes accessed | tf_op | source)
XLA Modules:
  0.0 199.1 jit_solution(6317241275431423019)
XLA Ops:
  7.2 2.3 %convolution_convert_fusion = bf16[128,512]{1,0:T(8,128)(2,1)S(1)} fusion(bf16[512,1536]{1,0:T(8,128)(2,1)} %w_out_ref.1, bf16[1,128,1536]{2,1,0:T(8,128)(2,1)} %param.6), kind=kOutput, calls=%fused_computation.1 | convolution fusion | flops 201392128 | bytes 2097152 | tf_op jit(solution)/shard_map/dot_general | solution.py:254
  11.5 6.0 %all-to-all-start = ((bf16[8,128,1024]{2,1,0:T(8,128)(2,1)}), bf16[8,128,1024]{2,1,0:T(8,128)(2,1)}, u32[]{:S(2)}, u32[]{:S(2)}) async-start(bf16[8,128,1024]{2,1,0:T(8,128)(2,1)} %broadcast_in_dim.41), calls=%async_computation | async-start | bytes 4194304 | tf_op jit(solution)/shard_map/all_to_all | solution.py:236
  17.5 1.8 collective-permute-start
  20.2 26.0 %all_gather.3.kv = bf16[1024,256]{1,0:T(8,128)(2,1)} all-gather(bf16[128,256]{1,0:T(8,128)(2,1)S(1)} %convolution_convert_fusion.2), channel_id=1, replica_groups=mesh['x'=4,'z'=8,'yl'=2,'yh'=2,'core'=2] {'z'}, dimensions={0}, use_global_device_ids=true | all-gather | bytes 589824 | tf_op jit(solution)/shard_map/all_gather | solution.py:259
  47.2 11.9 %shard_map.92 = (bf16[8,128,512]{2,1,0:T(8,128)(2,1)}, f32[8,16,512]{2,1,0:T(8,128)}, f32[8,512]{1,0:T(8,128)}, bf16[8,1024,512]{2,1,0:T(8,128)(2,1)}) custom-call(bf16[8,128,1024]{2,1,0:T(8,128)(2,1)} %all-to-all-done.qd, bf16[1024,256]{1,0:T(8,128)(2,1)} %all_gather.3.kv), custom_call_target="tpu_custom_call" | custom-call | flops 10000000000 | bytes 6000000 | tf_op jit(solution)/shard_map/pallas_call | solution.py:220
  59.1 9.8 %all_to_all.35.stats_ref = f32[8,16,512]{2,1,0:T(8,128)} all-to-all(f32[8,16,512]{2,1,0:T(8,128)} %get-tuple-element.37), channel_id=1, replica_groups=mesh['x'=4,'z'=8,'yl'=2,'yh'=2,'core'=2] {'x','yl'}, dimensions={0} | all-to-all | bytes 524288 | tf_op jit(solution)/shard_map/all_to_all | solution.py:236
  69.0 3.6 %all-to-all-start.2 = ((bf16[8,128,512]{2,1,0:T(8,128)(2,1)}), bf16[8,128,512]{2,1,0:T(8,128)(2,1)S(1)}, u32[]{:S(2)}, u32[]{:S(2)}) async-start(bf16[8,128,512]{2,1,0:T(8,128)(2,1)} %get-tuple-element.42), calls=%async_computation.2 | async-start | bytes 2097152 | tf_op jit(solution)/shard_map/all_to_all | solution.py:236
  72.6 13.0 %shard_map.93 = (bf16[8,128,512]{2,1,0:T(8,128)(2,1)}, f32[1024,256]{1,0:T(8,128)}) custom-call(bf16[8,128,1024]{2,1,0:T(8,128)(2,1)} %all-to-all-done.qd, f32[8,16,512]{2,1,0:T(8,128)} %all_to_all.35.stats_ref, f32[8,512]{1,0:T(8,128)} %get-tuple-element.39.tops, bf16[1024,256]{1,0:T(8,128)(2,1)} %all_gather.3.kv, bf16[8,1024,512]{2,1,0:T(8,128)(2,1)} %get-tuple-element.40.kept), custom_call_target="tpu_custom_call" | custom-call | flops 16000000000 | bytes 6000000 | tf_op jit(solution)/shard_map/pallas_call | solution.py:220
  86.6 3.1 %shard_map.94 = (bf16[128,512]{1,0:T(8,128)(2,1)}, bf16[512,768]{1,0:T(8,128)(2,1)}, bf16[512,768]{1,0:T(8,128)(2,1)}) custom-call(s32[2]{0:T(128)} %pad_add_fusion.place, bf16[8,128,512]{2,1,0:T(8,128)(2,1)} %copy-done.1, f32[8,16,512]{2,1,0:T(8,128)} %all_to_all.35.stats_ref, bf16[128,1536]{1,0:T(8,128)(2,1)} %bitcast.39), custom_call_target="tpu_custom_call" | custom-call | flops 400000000 | bytes 6000000 | tf_op jit(solution)/shard_map/pallas_call | solution.py:220
  89.7 6.2 %collective-permute-start.1 = (bf16[512,768]{1,0:T(8,128)(2,1)}, bf16[512,768]{1,0:T(8,128)(2,1)S(1)}, u32[]{:S(2)}, u32[]{:S(2)}) collective-permute-start(bf16[512,768]{1,0:T(8,128)(2,1)} %get-tuple-element.45), channel_id=1, source_target_pairs={{0,1},{1,0},{2,3},{3,2},{4,5},{5,4},{6,7},{7,6},{8,9},{9,8},{10,11... | collective-permute-start | bytes 2359304 | tf_op jit(solution)/shard_map/ppermute | solution.py:34
  95.9 2.8 %shard_map.95 = bf16[128,1536]{1,0:T(8,128)(2,1)} custom-call(bf16[128,1536]{1,0:T(8,128)(2,1)} %bitcast.34, bf16[128,512]{1,0:T(8,128)(2,1)} %get-tuple-element.46.mixed_ref, bf16[512,1536]{1,0:T(8,128)(2,1)} %w_out_ref.1), custom_call_target="tpu_custom_call" | custom-call | flops 20000000000 | bytes 6000000 | tf_op jit(solution)/shard_map/pallas_call | solution.py:220
  98.9 16.5 %all_to_all.36 = bf16[4,128,768]{2,1,0:T(8,128)(2,1)S(1)} all-to-all(bf16[4,128,768]{2,1,0:T(8,128)(2,1)S(1)} %bitcast.38), channel_id=1, replica_groups=mesh['x'=4,'z'=8,'yl'=2,'yh'=2,'core'=2] {'x'}, dimensions={0} | all-to-all | bytes 1572864 | tf_op jit(solution)/shard_map/all_to_all | solution.py:236
  115.4 17.0 %all_to_all.37.dq_ref = bf16[8,128,512]{2,1,0:T(8,128)(2,1)} all-to-all(bf16[8,128,512]{2,1,0:T(8,128)(2,1)S(1)} %copy-done.4), channel_id=1, replica_groups=mesh['x'=4,'z'=8,'yl'=2,'yh'=2,'core'=2] {'x','yl'}, dimensions={0} | all-to-all | bytes 2097152 | tf_op jit(solution)/shard_map/all_to_all | solution.py:236
  132.4 2.2 %shard_map.96 = (bf16[128,768]{1,0:T(8,128)(2,1)}, bf16[128,384]{1,0:T(8,128)(2,1)}, bf16[128,384]{1,0:T(8,128)(2,1)}) custom-call(s32[2]{0:T(128)} %pad_add_fusion.place, bf16[8,128,512]{2,1,0:T(8,128)(2,1)} %all_to_all.37.dq_ref, f32[128,256]{1,0:T(8,128)} %reduce-scatter.2.cloned.1.call-done.dkv_ref), custom_call_target="tpu_custom_call" | custom-call | flops 10000000 | bytes 6000000 | tf_op jit(solution)/shard_map/pallas_call | solution.py:220
  134.6 2.4 %collective-permute-start.2 = (bf16[128,384]{1,0:T(8,128)(2,1)}, bf16[128,384]{1,0:T(8,128)(2,1)S(1)}, u32[]{:S(2)}, u32[]{:S(2)}) collective-permute-start(bf16[128,384]{1,0:T(8,128)(2,1)} %get-tuple-element.56), channel_id=1, source_target_pairs={{0,1},{1,0},{2,3},{3,2},{4,5},{5,4},{6,7},{7,6},{8,9},{9,8},{10,11... | collective-permute-start | bytes 294920 | tf_op jit(solution)/shard_map/ppermute | solution.py:34
  138.8 2.8 %shard_map.98 = bf16[1536,384]{1,0:T(8,128)(2,1)} custom-call(bf16[128,1536]{1,0:T(8,128)(2,1)} %bitcast.35, bf16[128,1536]{1,0:T(8,128)(2,1)} %copy-done.6, bf16[128,384]{1,0:T(8,128)(2,1)} %get-tuple-element.55.keep_ref, bf16[128,384]{1,0:T(8,128)(2,1)} %copy-done.7), custom_call_target="tpu_custom_call" | custom-call | flops 300000000 | bytes 6000000 | tf_op jit(solution)/shard_map/pallas_call | solution.py:220
  141.6 3.5 %all-to-all-start.5 = ((bf16[4,384,384]{2,1,0:T(8,128)(2,1)}), bf16[4,384,384]{2,1,0:T(8,128)(2,1)S(1)}, u32[]{:S(2)}, u32[]{:S(2)}) async-start(bf16[4,384,384]{2,1,0:T(8,128)(2,1)} %bitcast.33), calls=%async_computation.6 | async-start | bytes 2359296 | tf_op jit(solution)/shard_map/all_to_all | solution.py:236
  145.4 2.8 %collective-permute-start.3 = (bf16[64,384]{1,0:T(8,128)(2,1)S(1)}, bf16[64,384]{1,0:T(8,128)(2,1)S(1)}, u32[]{:S(2)}, u32[]{:S(2)}) collective-permute-start(bf16[64,384]{1,0:T(8,128)(2,1)S(1)} %get-tuple-element.61), channel_id=1, source_target_pairs={{0,2},{2,0},{4,6},{6,4},{1,3},{3,1},{5,7},{7,5},{8,10},{10,8},{12,... | collective-permute-start | bytes 147464 | tf_op jit(solution)/shard_map/ppermute | solution.py:41
  149.0 3.3 %shard_map.97 = bf16[128,1536]{1,0:T(8,128)(2,1)} custom-call(bf16[128,768]{1,0:T(8,128)(2,1)} %get-tuple-element.53.both_ref, bf16[1536,512]{1,0:T(8,128)(2,1)} %w_query_ref.1, bf16[1536,256]{1,0:T(8,128)(2,1)} %w_keyval_ref.1), custom_call_target="tpu_custom_call" | custom-call | flops 300000000 | bytes 6000000 | tf_op jit(solution)/shard_map/pallas_call | solution.py:220
  153.0 8.4 %all-to-all-done.5 = bf16[4,384,384]{2,1,0:T(8,128)(2,1)S(1)} async-done(((bf16[4,384,384]{2,1,0:T(8,128)(2,1)}), bf16[4,384,384]{2,1,0:T(8,128)(2,1)S(1)}, u32[]{:S(2)}, u32[]{:S(2)}) %all-to-all-start.5) | async-done | bytes 1179680 | tf_op jit(solution)/shard_map/all_to_all | solution.py:236
  161.8 18.7 %all_to_all.38 = bf16[16,32,384]{2,1,0:T(8,128)(2,1)S(1)} all-to-all(bf16[16,32,384]{2,1,0:T(8,128)(2,1)S(1)} %pad_maximum_fusion), channel_id=1, replica_groups=mesh['x'=4,'z'=8,'yl'=2,'yh'=2,'core'=2] {'z','yl'}, dimensions={0} | all-to-all | bytes 786432 | tf_op jit(solution)/shard_map/all_to_all | solution.py:236
  180.6 2.7 %collective-permute-start.6 = (f32[32,384]{1,0:T(8,128)S(1)}, f32[32,384]{1,0:T(8,128)S(1)}, u32[]{:S(2)}, u32[]{:S(2)}) collective-permute-start(f32[32,384]{1,0:T(8,128)S(1)} %convert_reduce_fusion), channel_id=1, source_target_pairs={{0,2},{2,0},{1,3},{3,1},{4,6},{6,4},{5,7},{7,5},{8,10},{10,8},{9,1... | collective-permute-start | bytes 147464 | tf_op jit(solution)/shard_map/ppermute | solution.py:34
  183.3 1.8 collective-permute-done.6
  185.1 4.3 %collective-permute-start.7 = (f32[40,384]{1,0:T(8,128)S(1)}, f32[40,384]{1,0:T(8,128)S(1)}, u32[]{:S(2)}, u32[]{:S(2)}) collective-permute-start(f32[40,384]{1,0:T(8,128)S(1)} %pad_maximum_fusion.2), channel_id=1, source_target_pairs={{0,1},{1,0},{2,3},{3,2},{4,5},{5,4},{6,7},{7,6},{8,9},{9,8},{10,11... | collective-permute-start | bytes 184328 | tf_op jit(solution)/shard_map/ppermute | solution.py:34
  (60 shorter events, 11.9 us)
Async XLA Ops:
  7.2 2.3 %copy-start.2 = (bf16[1,128,1536]{2,1,0:T(8,128)(2,1)S(1)}, bf16[1,128,1536]{2,1,0:T(8,128)(2,1)}, u32[]{:S(2)}) copy-start(bf16[1,128,1536]{2,1,0:T(8,128)(2,1)} %param.5) | copy-start | bytes 1179652
  7.2 2.3 %copy-start = (bf16[1536,512]{1,0:T(8,128)(2,1)S(1)}, bf16[1536,512]{1,0:T(8,128)(2,1)}, u32[]{:S(2)}) copy-start(bf16[1536,512]{1,0:T(8,128)(2,1)} %w_query_ref.1) | copy-start | bytes 4718596
  11.5 7.8 %copy-start.3 = (bf16[1536,256]{1,0:T(8,128)(2,1)S(1)}, bf16[1536,256]{1,0:T(8,128)(2,1)}, u32[]{:S(2)}) copy-start(bf16[1536,256]{1,0:T(8,128)(2,1)} %w_keyval_ref.1) | copy-start | bytes 2359300
  11.5 35.6 %all-to-all-start = ((bf16[8,128,1024]{2,1,0:T(8,128)(2,1)}), bf16[8,128,1024]{2,1,0:T(8,128)(2,1)}, u32[]{:S(2)}, u32[]{:S(2)}) async-start(bf16[8,128,1024]{2,1,0:T(8,128)(2,1)} %broadcast_in_dim.41), calls=%async_computation | async-start | bytes 4194304 | tf_op jit(solution)/shard_map/all_to_all | solution.py:236
  17.5 28.7 %collective-permute-start = (bf16[128,1536]{1,0:T(8,128)(2,1)S(1)}, bf16[128,1536]{1,0:T(8,128)(2,1)S(1)}, u32[]{:S(2)}, u32[]{:S(2)}) collective-permute-start(bf16[128,1536]{1,0:T(8,128)(2,1)S(1)} %bitcast.36), channel_id=1, source_target_pairs={{0,1},{1,0},{2,3},{3,2},{4,5},{5,4},{6,7},{7,6},{8,9},{9,8},{10,11... | collective-permute-start | bytes 1179656 | tf_op jit(solution)/shard_map/ppermute | solution.py:34
  46.2 12.9 %copy-start.6 = (bf16[128,1536]{1,0:T(8,128)(2,1)}, bf16[128,1536]{1,0:T(8,128)(2,1)S(1)}, u32[]{:S(2)}) copy-start(bf16[128,1536]{1,0:T(8,128)(2,1)S(1)} %collective-permute-done.other_ref) | copy-start | bytes 1179652
  69.0 16.6 %all-to-all-start.2 = ((bf16[8,128,512]{2,1,0:T(8,128)(2,1)}), bf16[8,128,512]{2,1,0:T(8,128)(2,1)S(1)}, u32[]{:S(2)}, u32[]{:S(2)}) async-start(bf16[8,128,512]{2,1,0:T(8,128)(2,1)} %get-tuple-element.42), calls=%async_computation.2 | async-start | bytes 2097152 | tf_op jit(solution)/shard_map/all_to_all | solution.py:236
  72.5 59.8 %reduce-scatter.2.cloned.1.call-start = ((), (), s32[]{:S(2)}) async-start(), calls=%async_computation.8 | async-start | bytes 1179648 | tf_op jit(solution)/shard_map/reduce_scatter | solution.py:304
  85.6 1.0 copy-start.1
  89.7 9.0 %collective-permute-start.1 = (bf16[512,768]{1,0:T(8,128)(2,1)}, bf16[512,768]{1,0:T(8,128)(2,1)S(1)}, u32[]{:S(2)}, u32[]{:S(2)}) collective-permute-start(bf16[512,768]{1,0:T(8,128)(2,1)} %get-tuple-element.45), channel_id=1, source_target_pairs={{0,1},{1,0},{2,3},{3,2},{4,5},{5,4},{6,7},{7,6},{8,9},{9,8},{10,11... | collective-permute-start | bytes 2359304 | tf_op jit(solution)/shard_map/ppermute | solution.py:34
  95.9 2.8 %copy-start.5 = (bf16[512,768]{1,0:T(8,128)(2,1)S(1)}, bf16[512,768]{1,0:T(8,128)(2,1)}, u32[]{:S(2)}) copy-start(bf16[512,768]{1,0:T(8,128)(2,1)} %get-tuple-element.44) | copy-start | bytes 2359300
  98.7 16.7 %copy-start.4 = (bf16[8,128,512]{2,1,0:T(8,128)(2,1)S(1)}, bf16[8,128,512]{2,1,0:T(8,128)(2,1)}, u32[]{:S(2)}) copy-start(bf16[8,128,512]{2,1,0:T(8,128)(2,1)} %get-tuple-element.49) | copy-start | bytes 3145732
  134.6 3.6 %collective-permute-start.2 = (bf16[128,384]{1,0:T(8,128)(2,1)}, bf16[128,384]{1,0:T(8,128)(2,1)S(1)}, u32[]{:S(2)}, u32[]{:S(2)}) collective-permute-start(bf16[128,384]{1,0:T(8,128)(2,1)} %get-tuple-element.56), channel_id=1, source_target_pairs={{0,1},{1,0},{2,3},{3,2},{4,5},{5,4},{6,7},{7,6},{8,9},{9,8},{10,11... | collective-permute-start | bytes 294920 | tf_op jit(solution)/shard_map/ppermute | solution.py:34
  138.2 0.6 copy-start.7
  141.6 19.8 %all-to-all-start.5 = ((bf16[4,384,384]{2,1,0:T(8,128)(2,1)}), bf16[4,384,384]{2,1,0:T(8,128)(2,1)S(1)}, u32[]{:S(2)}, u32[]{:S(2)}) async-start(bf16[4,384,384]{2,1,0:T(8,128)(2,1)} %bitcast.33), calls=%async_computation.6 | async-start | bytes 2359296 | tf_op jit(solution)/shard_map/all_to_all | solution.py:236
  145.4 6.8 %collective-permute-start.3 = (bf16[64,384]{1,0:T(8,128)(2,1)S(1)}, bf16[64,384]{1,0:T(8,128)(2,1)S(1)}, u32[]{:S(2)}, u32[]{:S(2)}) collective-permute-start(bf16[64,384]{1,0:T(8,128)(2,1)S(1)} %get-tuple-element.61), channel_id=1, source_target_pairs={{0,2},{2,0},{4,6},{6,4},{1,3},{3,1},{5,7},{7,5},{8,10},{10,8},{12,... | collective-permute-start | bytes 147464 | tf_op jit(solution)/shard_map/ppermute | solution.py:41
  148.2 4.1 %collective-permute-start.4 = (bf16[64,384]{1,0:T(8,128)(2,1)S(1)}, bf16[64,384]{1,0:T(8,128)(2,1)S(1)}, u32[]{:S(2)}, u32[]{:S(2)}) collective-permute-start(bf16[64,384]{1,0:T(8,128)(2,1)S(1)} %get-tuple-element.63), channel_id=1, source_target_pairs={{0,4},{2,6},{4,0},{6,2},{1,5},{3,7},{5,1},{7,3},{8,12},{10,14},{12... | collective-permute-start | bytes 147464 | tf_op jit(solution)/shard_map/ppermute | solution.py:41
  148.5 4.4 %collective-permute-start.5 = (bf16[64,384]{1,0:T(8,128)(2,1)S(1)}, bf16[64,384]{1,0:T(8,128)(2,1)S(1)}, u32[]{:S(2)}, u32[]{:S(2)}) collective-permute-start(bf16[64,384]{1,0:T(8,128)(2,1)S(1)} %get-tuple-element.62), channel_id=1, source_target_pairs={{0,6},{2,4},{4,2},{6,0},{1,7},{3,5},{5,3},{7,1},{8,14},{10,12},{12... | collective-permute-start | bytes 147464 | tf_op jit(solution)/shard_map/ppermute | solution.py:41
  180.6 4.5 %collective-permute-start.6 = (f32[32,384]{1,0:T(8,128)S(1)}, f32[32,384]{1,0:T(8,128)S(1)}, u32[]{:S(2)}, u32[]{:S(2)}) collective-permute-start(f32[32,384]{1,0:T(8,128)S(1)} %convert_reduce_fusion), channel_id=1, source_target_pairs={{0,2},{2,0},{1,3},{3,1},{4,6},{6,4},{5,7},{7,5},{8,10},{10,8},{9,1... | collective-permute-start | bytes 147464 | tf_op jit(solution)/shard_map/ppermute | solution.py:34
  185.1 5.2 %collective-permute-start.7 = (f32[40,384]{1,0:T(8,128)S(1)}, f32[40,384]{1,0:T(8,128)S(1)}, u32[]{:S(2)}, u32[]{:S(2)}) collective-permute-start(f32[40,384]{1,0:T(8,128)S(1)} %pad_maximum_fusion.2), channel_id=1, source_target_pairs={{0,1},{1,0},{2,3},{3,2},{4,5},{5,4},{6,7},{7,6},{8,9},{9,8},{10,11... | collective-permute-start | bytes 184328 | tf_op jit(solution)/shard_map/ppermute | solution.py:34
Sparse Core Ops, SparseCore 0:
  85.7 40.6 reduce-scatter.1

commit v8 on v6

--- a/solution.py
+++ b/solution.py
@@ -13,7 +13,7 @@
 ROWS = HEADS * POS
 GROUP = 8
 KEYS = 8 * POS
-TILE = 32
+TILE = 16
 SCALE = 1.0 / HEAD_DIM**0.5
 LOG2E = math.log2(math.e)
 AXES = ("x", "z", "yl", "yh", "core")
@@ -203,7 +203,7 @@
         out_specs=out_specs,
         scratch_shapes=scratch,
         compiler_params=pltpu.CompilerParams(vmem_limit_bytes=VMEM_LIMIT),
-        cost_estimate=pl.CostEstimate(flops=flops, bytes_accessed=6_000_000, transcendentals=0),
+        cost_estimate=pl.CostEstimate(flops=flops, bytes_accessed=6_000_000 if flops else 0, transcendentals=0),
     )(*ins)
 
 
@@ -294,8 +294,8 @@
     )
     term_o, attended, dq_parts = lax.optimization_barrier((term_o, attended, dq_parts))
     dqs = swap(dq_parts, ("x", "yl"))
+    dqs, term_o = lax.optimization_barrier((dqs, term_o))
     term_o = swap(term_o.reshape(4, 128, 768), "x")
-    dqs, term_o = lax.optimization_barrier((dqs, term_o))
 
     both, keep_i, give_i = call(
         input_kernel,
@@ -304,7 +304,7 @@
         [SM] + [VM] * 2,
         [VM] * 3,
         [],
-        10_000_000,
+        0,
     )
     term_i = call(
         term_kernel,
@@ -313,8 +313,9 @@
         [VM] * 4,
         VM,
         [],
-        300_000_000,
-    )
+        0,
+    )
+    term_i, term_o = lax.optimization_barrier((term_i, term_o))
     grad_tokens = call(
         tokens_kernel,
         [both, w_query, w_keyval],

time: 199 us -> 194 us (0.975)
  blocking collectives: 87.9 us -> 73.2 us
  starting transfers between devices: 34 us -> 40.3 us
  waiting for transfers between devices: 13.9 us -> 16.4 us
    all_to_all x4 -> x3, blocking collectives: 61.9 us -> 47.2 us  [swap(): return lax.all_to_all(blocks, axes, 0, 0)]
    all_to_all x3 -> x4, starting transfers between devices: 13.1 us -> 16.9 us  [swap(): return lax.all_to_all(blocks, axes, 0, 0)]
    reduce_scatter x1, waiting for transfers between devices: 0.01 us -> 2.7 us  [body(): dkv = lax.psum_scatter(dkv_parts, 'z', scatter_dimension=0, tiled=True)]
    ppermute x5, starting transfers between devices: 17.4 us -> 19.7 us  [send(): lax.ppermute(array, axis, [(i, (i + step) % size) for i in range(size)])]
    all_to_all x3 -> x4, waiting for transfers between devices: 9.36 us -> 9.07 us  [swap(): return lax.all_to_all(blocks, axes, 0, 0)]
  transfers between devices with their start and end apart: 12 -> 13, of which waited for: 6 -> 7; matrix products, arithmetic and copies ran while one was open for 1% -> 1% of each run, Pallas kernels for 12% -> 15%
where the time goes in v8:
time: 194 us; the launch traced here: 193 us
  blocking collectives  73.2 us (38%)
  starting transfers between devices  40.3 us (21%)
  Pallas kernels  37.9 us (20%)
  waiting for transfers between devices  16.4 us (8%)
  between operations  14.3 us (7%)
  other arithmetic  4.21 us (2%)
  local copies, waits for them, and re-layouts  3.83 us (2%)
  matrix products  2.95 us (2%)
    all_to_all x3, blocking collectives, swap(): return lax.all_to_all(blocks, axes, 0, 0)  47.2 us
    pallas_call x7, Pallas kernels, call(): pl.pallas_call(kernel, out_shape=outs, in_specs=in_specs, out_specs=out_s...  37.9 us
    all_gather x1, blocking collectives, body(): kvs = lax.all_gather(keyval, 'z', axis=0, tiled=True)  26 us
    ppermute x5, starting transfers between devices, send(): lax.ppermute(array, axis, [(i, (i + step) % size) for i in range(size)])  19.7 us
    all_to_all x4, starting transfers between devices, swap(): return lax.all_to_all(blocks, axes, 0, 0)  16.9 us
    all_to_all x4, waiting for transfers between devices, swap(): return lax.all_to_all(blocks, axes, 0, 0)  9.07 us
    ppermute x5, waiting for transfers between devices, send(): lax.ppermute(array, axis, [(i, (i + step) % size) for i in range(size)])  4.06 us
  transfers between devices with their start and end apart: 13, of which 7 were waited for; matrix products, arithmetic and copies ran while one was open for 1% of the time, Pallas kernels for 15%

profile of v8, /device:TPU:1, one launch (start us, length us, event | category | flops | bytes accessed | tf_op | source)
XLA Modules:
  0.0 192.9 jit_solution(6130472873672569659)
XLA Ops:
  7.2 2.3 %convolution_convert_fusion = bf16[128,512]{1,0:T(8,128)(2,1)S(1)} fusion(bf16[512,1536]{1,0:T(8,128)(2,1)} %w_out_ref.1, bf16[1,128,1536]{2,1,0:T(8,128)(2,1)} %param.6), kind=kOutput, calls=%fused_computation.1 | convolution fusion | flops 201392128 | bytes 2097152 | tf_op jit(solution)/shard_map/dot_general | solution.py:233
  11.5 6.0 %all-to-all-start = ((bf16[8,128,1024]{2,1,0:T(8,128)(2,1)}), bf16[8,128,1024]{2,1,0:T(8,128)(2,1)}, u32[]{:S(2)}, u32[]{:S(2)}) async-start(bf16[8,128,1024]{2,1,0:T(8,128)(2,1)} %broadcast_in_dim.41), calls=%async_computation | async-start | bytes 4194304 | tf_op jit(solution)/shard_map/all_to_all | solution.py:215
  20.2 26.0 %all_gather.3.kv = bf16[1024,256]{1,0:T(8,128)(2,1)} all-gather(bf16[128,256]{1,0:T(8,128)(2,1)S(1)} %convolution_convert_fusion.2), channel_id=1, replica_groups=mesh['x'=4,'z'=8,'yl'=2,'yh'=2,'core'=2] {'z'}, dimensions={0}, use_global_device_ids=true | all-gather | bytes 589824 | tf_op jit(solution)/shard_map/all_gather | solution.py:238
  47.2 9.9 %shard_map.92 = (bf16[8,128,512]{2,1,0:T(8,128)(2,1)}, f32[8,16,512]{2,1,0:T(8,128)}) custom-call(bf16[8,128,1024]{2,1,0:T(8,128)(2,1)} %all-to-all-done.qd, bf16[1024,256]{1,0:T(8,128)(2,1)} %all_gather.3.kv), custom_call_target="tpu_custom_call" | custom-call | flops 10000000000 | bytes 6000000 | tf_op jit(solution)/shard_map/pallas_call | solution.py:199
  57.0 9.8 %all_to_all.35.stats_ref = f32[8,16,512]{2,1,0:T(8,128)} all-to-all(f32[8,16,512]{2,1,0:T(8,128)} %get-tuple-element.37), channel_id=1, replica_groups=mesh['x'=4,'z'=8,'yl'=2,'yh'=2,'core'=2] {'x','yl'}, dimensions={0} | all-to-all | bytes 524288 | tf_op jit(solution)/shard_map/all_to_all | solution.py:215
  66.8 3.6 %all-to-all-start.2 = ((bf16[8,128,512]{2,1,0:T(8,128)(2,1)}), bf16[8,128,512]{2,1,0:T(8,128)(2,1)S(1)}, u32[]{:S(2)}, u32[]{:S(2)}) async-start(bf16[8,128,512]{2,1,0:T(8,128)(2,1)} %get-tuple-element.40), calls=%async_computation.2 | async-start | bytes 2097152 | tf_op jit(solution)/shard_map/all_to_all | solution.py:215
  70.4 13.7 %shard_map.93 = (bf16[8,128,512]{2,1,0:T(8,128)(2,1)}, f32[1024,256]{1,0:T(8,128)}) custom-call(bf16[8,128,1024]{2,1,0:T(8,128)(2,1)} %all-to-all-done.qd, f32[8,16,512]{2,1,0:T(8,128)} %all_to_all.35.stats_ref, bf16[1024,256]{1,0:T(8,128)(2,1)} %all_gather.3.kv), custom_call_target="tpu_custom_call" | custom-call | flops 16000000000 | bytes 6000000 | tf_op jit(solution)/shard_map/pallas_call | solution.py:199
  85.2 3.2 %shard_map.94 = (bf16[128,512]{1,0:T(8,128)(2,1)}, bf16[512,768]{1,0:T(8,128)(2,1)}, bf16[512,768]{1,0:T(8,128)(2,1)}) custom-call(s32[2]{0:T(128)} %pad_add_fusion.place, bf16[8,128,512]{2,1,0:T(8,128)(2,1)} %copy-done.1, f32[8,16,512]{2,1,0:T(8,128)} %all_to_all.35.stats_ref, bf16[128,1536]{1,0:T(8,128)(2,1)} %bitcast.38), custom_call_target="tpu_custom_call" | custom-call | flops 400000000 | bytes 6000000 | tf_op jit(solution)/shard_map/pallas_call | solution.py:199
  88.4 6.2 %collective-permute-start.1 = (bf16[512,768]{1,0:T(8,128)(2,1)}, bf16[512,768]{1,0:T(8,128)(2,1)S(1)}, u32[]{:S(2)}, u32[]{:S(2)}) collective-permute-start(bf16[512,768]{1,0:T(8,128)(2,1)} %get-tuple-element.43), channel_id=1, source_target_pairs={{0,1},{1,0},{2,3},{3,2},{4,5},{5,4},{6,7},{7,6},{8,9},{9,8},{10,11... | collective-permute-start | bytes 2359304 | tf_op jit(solution)/shard_map/ppermute | solution.py:34
  94.6 2.8 %shard_map.95 = bf16[128,1536]{1,0:T(8,128)(2,1)} custom-call(bf16[128,1536]{1,0:T(8,128)(2,1)} %bitcast.34, bf16[128,512]{1,0:T(8,128)(2,1)} %get-tuple-element.44.mixed_ref, bf16[512,1536]{1,0:T(8,128)(2,1)} %w_out_ref.1), custom_call_target="tpu_custom_call" | custom-call | flops 20000000000 | bytes 6000000 | tf_op jit(solution)/shard_map/pallas_call | solution.py:199
  98.8 20.3 %all_to_all.36.dq_ref = bf16[8,128,512]{2,1,0:T(8,128)(2,1)} all-to-all(bf16[8,128,512]{2,1,0:T(8,128)(2,1)S(1)} %copy-done.4), channel_id=1, replica_groups=mesh['x'=4,'z'=8,'yl'=2,'yh'=2,'core'=2] {'x','yl'}, dimensions={0} | all-to-all | bytes 2097152 | tf_op jit(solution)/shard_map/all_to_all | solution.py:215
  119.2 3.5 %all-to-all-start.4 = ((bf16[4,128,768]{2,1,0:T(8,128)(2,1)}), bf16[4,128,768]{2,1,0:T(8,128)(2,1)S(1)}, u32[]{:S(2)}, u32[]{:S(2)}) async-start(bf16[4,128,768]{2,1,0:T(8,128)(2,1)} %bitcast.5), calls=%async_computation.5 | async-start | bytes 1572864 | tf_op jit(solution)/shard_map/all_to_all | solution.py:215
  122.7 2.7 %reduce-scatter.2.cloned.1.call-done.dkv_ref = f32[128,256]{1,0:T(8,128)} async-done(((f32[1024,256]{1,0:T(8,128)}), f32[128,256]{1,0:T(8,128)}) %reduce-scatter.2.cloned.1.call-update) | async-done | bytes 131088 | tf_op jit(solution)/shard_map/reduce_scatter | solution.py:275
  125.4 2.2 %shard_map.96 = (bf16[128,768]{1,0:T(8,128)(2,1)}, bf16[128,384]{1,0:T(8,128)(2,1)}, bf16[128,384]{1,0:T(8,128)(2,1)}) custom-call(s32[2]{0:T(128)} %pad_add_fusion.place, bf16[8,128,512]{2,1,0:T(8,128)(2,1)} %all_to_all.36.dq_ref, f32[128,256]{1,0:T(8,128)} %reduce-scatter.2.cloned.1.call-done.dkv_ref), custom_call_target="tpu_custom_call" | custom-call | tf_op jit(solution)/shard_map/pallas_call | solution.py:199
  127.6 4.4 %collective-permute-start.2 = (bf16[128,384]{1,0:T(8,128)(2,1)}, bf16[128,384]{1,0:T(8,128)(2,1)S(1)}, u32[]{:S(2)}, u32[]{:S(2)}) collective-permute-start(bf16[128,384]{1,0:T(8,128)(2,1)} %get-tuple-element.54), channel_id=1, source_target_pairs={{0,1},{1,0},{2,3},{3,2},{4,5},{5,4},{6,7},{7,6},{8,9},{9,8},{10,11... | collective-permute-start | bytes 294920 | tf_op jit(solution)/shard_map/ppermute | solution.py:34
  133.8 2.8 %shard_map.98 = bf16[1536,384]{1,0:T(8,128)(2,1)} custom-call(bf16[128,1536]{1,0:T(8,128)(2,1)} %bitcast.35, bf16[128,1536]{1,0:T(8,128)(2,1)} %copy-done.6, bf16[128,384]{1,0:T(8,128)(2,1)} %get-tuple-element.53.keep_ref, bf16[128,384]{1,0:T(8,128)(2,1)} %copy-done.7), custom_call_target="tpu_custom_call" | custom-call | tf_op jit(solution)/shard_map/pallas_call | solution.py:199
  136.6 3.9 %all-to-all-start.5 = ((bf16[4,384,384]{2,1,0:T(8,128)(2,1)}), bf16[4,384,384]{2,1,0:T(8,128)(2,1)S(1)}, u32[]{:S(2)}, u32[]{:S(2)}) async-start(bf16[4,384,384]{2,1,0:T(8,128)(2,1)} %bitcast.33), calls=%async_computation.6 | async-start | bytes 2359296 | tf_op jit(solution)/shard_map/all_to_all | solution.py:215
  140.7 2.9 %collective-permute-start.3 = (bf16[64,384]{1,0:T(8,128)(2,1)S(1)}, bf16[64,384]{1,0:T(8,128)(2,1)S(1)}, u32[]{:S(2)}, u32[]{:S(2)}) collective-permute-start(bf16[64,384]{1,0:T(8,128)(2,1)S(1)} %get-tuple-element.61), channel_id=1, source_target_pairs={{0,2},{2,0},{4,6},{6,4},{1,3},{3,1},{5,7},{7,5},{8,10},{10,8},{12,... | collective-permute-start | bytes 147464 | tf_op jit(solution)/shard_map/ppermute | solution.py:41
  144.5 3.3 %shard_map.97 = bf16[128,1536]{1,0:T(8,128)(2,1)} custom-call(bf16[128,768]{1,0:T(8,128)(2,1)} %get-tuple-element.51.both_ref, bf16[1536,512]{1,0:T(8,128)(2,1)} %w_query_ref.1, bf16[1536,256]{1,0:T(8,128)(2,1)} %w_keyval_ref.1), custom_call_target="tpu_custom_call" | custom-call | flops 300000000 | bytes 6000000 | tf_op jit(solution)/shard_map/pallas_call | solution.py:199
  148.4 8.1 %all-to-all-done.5 = bf16[4,384,384]{2,1,0:T(8,128)(2,1)S(1)} async-done(((bf16[4,384,384]{2,1,0:T(8,128)(2,1)}), bf16[4,384,384]{2,1,0:T(8,128)(2,1)S(1)}, u32[]{:S(2)}, u32[]{:S(2)}) %all-to-all-start.5) | async-done | bytes 1179680 | tf_op jit(solution)/shard_map/all_to_all | solution.py:215
  156.9 17.0 %all_to_all.37 = bf16[16,32,384]{2,1,0:T(8,128)(2,1)S(1)} all-to-all(bf16[16,32,384]{2,1,0:T(8,128)(2,1)S(1)} %pad_maximum_fusion), channel_id=1, replica_groups=mesh['x'=4,'z'=8,'yl'=2,'yh'=2,'core'=2] {'z','yl'}, dimensions={0} | all-to-all | bytes 786432 | tf_op jit(solution)/shard_map/all_to_all | solution.py:215
  174.0 2.5 %collective-permute-start.6 = (f32[32,384]{1,0:T(8,128)S(1)}, f32[32,384]{1,0:T(8,128)S(1)}, u32[]{:S(2)}, u32[]{:S(2)}) collective-permute-start(f32[32,384]{1,0:T(8,128)S(1)} %convert_reduce_fusion), channel_id=1, source_target_pairs={{0,2},{2,0},{1,3},{3,1},{4,6},{6,4},{5,7},{7,5},{8,10},{10,8},{9,1... | collective-permute-start | bytes 147464 | tf_op jit(solution)/shard_map/ppermute | solution.py:34
  176.5 2.0 %collective-permute-done.6 = f32[32,384]{1,0:T(8,128)S(1)} collective-permute-done((f32[32,384]{1,0:T(8,128)S(1)}, f32[32,384]{1,0:T(8,128)S(1)}, u32[]{:S(2)}, u32[]{:S(2)}) %collective-permute-start.6) | collective-permute-done | bytes 49184 | tf_op jit(solution)/shard_map/ppermute | solution.py:34
  178.6 4.7 %collective-permute-start.7 = (f32[40,384]{1,0:T(8,128)S(1)}, f32[40,384]{1,0:T(8,128)S(1)}, u32[]{:S(2)}, u32[]{:S(2)}) collective-permute-start(f32[40,384]{1,0:T(8,128)S(1)} %pad_maximum_fusion.2), channel_id=1, source_target_pairs={{0,1},{1,0},{2,3},{3,2},{4,5},{5,4},{6,7},{7,6},{8,9},{9,8},{10,11... | collective-permute-start | bytes 184328 | tf_op jit(solution)/shard_map/ppermute | solution.py:34
  (61 shorter events, 14.9 us)
Async XLA Ops:
  7.2 2.3 %copy-start.2 = (bf16[1,128,1536]{2,1,0:T(8,128)(2,1)S(1)}, bf16[1,128,1536]{2,1,0:T(8,128)(2,1)}, u32[]{:S(2)}) copy-start(bf16[1,128,1536]{2,1,0:T(8,128)(2,1)} %param.5) | copy-start | bytes 1179652
  7.2 2.3 %copy-start = (bf16[1536,512]{1,0:T(8,128)(2,1)S(1)}, bf16[1536,512]{1,0:T(8,128)(2,1)}, u32[]{:S(2)}) copy-start(bf16[1536,512]{1,0:T(8,128)(2,1)} %w_query_ref.1) | copy-start | bytes 4718596
  11.5 7.8 %copy-start.3 = (bf16[1536,256]{1,0:T(8,128)(2,1)S(1)}, bf16[1536,256]{1,0:T(8,128)(2,1)}, u32[]{:S(2)}) copy-start(bf16[1536,256]{1,0:T(8,128)(2,1)} %w_keyval_ref.1) | copy-start | bytes 2359300
  11.5 35.7 %all-to-all-start = ((bf16[8,128,1024]{2,1,0:T(8,128)(2,1)}), bf16[8,128,1024]{2,1,0:T(8,128)(2,1)}, u32[]{:S(2)}, u32[]{:S(2)}) async-start(bf16[8,128,1024]{2,1,0:T(8,128)(2,1)} %broadcast_in_dim.41), calls=%async_computation | async-start | bytes 4194304 | tf_op jit(solution)/shard_map/all_to_all | solution.py:215
  17.5 28.7 %collective-permute-start = (bf16[128,1536]{1,0:T(8,128)(2,1)S(1)}, bf16[128,1536]{1,0:T(8,128)(2,1)S(1)}, u32[]{:S(2)}, u32[]{:S(2)}) collective-permute-start(bf16[128,1536]{1,0:T(8,128)(2,1)S(1)} %bitcast.36), channel_id=1, source_target_pairs={{0,1},{1,0},{2,3},{3,2},{4,5},{5,4},{6,7},{7,6},{8,9},{9,8},{10,11... | collective-permute-start | bytes 1179656 | tf_op jit(solution)/shard_map/ppermute | solution.py:34
  46.2 10.8 %copy-start.6 = (bf16[128,1536]{1,0:T(8,128)(2,1)}, bf16[128,1536]{1,0:T(8,128)(2,1)S(1)}, u32[]{:S(2)}) copy-start(bf16[128,1536]{1,0:T(8,128)(2,1)S(1)} %collective-permute-done.other_ref) | copy-start | bytes 1179652
  66.8 17.3 %all-to-all-start.2 = ((bf16[8,128,512]{2,1,0:T(8,128)(2,1)}), bf16[8,128,512]{2,1,0:T(8,128)(2,1)S(1)}, u32[]{:S(2)}, u32[]{:S(2)}) async-start(bf16[8,128,512]{2,1,0:T(8,128)(2,1)} %get-tuple-element.40), calls=%async_computation.2 | async-start | bytes 2097152 | tf_op jit(solution)/shard_map/all_to_all | solution.py:215
  70.4 55.0 %reduce-scatter.2.cloned.1.call-start = ((), (), s32[]{:S(2)}) async-start(), calls=%async_computation.8 | async-start | bytes 1179648 | tf_op jit(solution)/shard_map/reduce_scatter | solution.py:275
  84.2 1.0 copy-start.1
  88.4 9.0 %collective-permute-start.1 = (bf16[512,768]{1,0:T(8,128)(2,1)}, bf16[512,768]{1,0:T(8,128)(2,1)S(1)}, u32[]{:S(2)}, u32[]{:S(2)}) collective-permute-start(bf16[512,768]{1,0:T(8,128)(2,1)} %get-tuple-element.43), channel_id=1, source_target_pairs={{0,1},{1,0},{2,3},{3,2},{4,5},{5,4},{6,7},{7,6},{8,9},{9,8},{10,11... | collective-permute-start | bytes 2359304 | tf_op jit(solution)/shard_map/ppermute | solution.py:34
  94.6 2.8 %copy-start.5 = (bf16[512,768]{1,0:T(8,128)(2,1)S(1)}, bf16[512,768]{1,0:T(8,128)(2,1)}, u32[]{:S(2)}) copy-start(bf16[512,768]{1,0:T(8,128)(2,1)} %get-tuple-element.42) | copy-start | bytes 2359300
  97.3 1.5 copy-start.4
  119.2 17.4 %all-to-all-start.4 = ((bf16[4,128,768]{2,1,0:T(8,128)(2,1)}), bf16[4,128,768]{2,1,0:T(8,128)(2,1)S(1)}, u32[]{:S(2)}, u32[]{:S(2)}) async-start(bf16[4,128,768]{2,1,0:T(8,128)(2,1)} %bitcast.5), calls=%async_computation.5 | async-start | bytes 1572864 | tf_op jit(solution)/shard_map/all_to_all | solution.py:215
  127.6 5.6 %collective-permute-start.2 = (bf16[128,384]{1,0:T(8,128)(2,1)}, bf16[128,384]{1,0:T(8,128)(2,1)S(1)}, u32[]{:S(2)}, u32[]{:S(2)}) collective-permute-start(bf16[128,384]{1,0:T(8,128)(2,1)} %get-tuple-element.54), channel_id=1, source_target_pairs={{0,1},{1,0},{2,3},{3,2},{4,5},{5,4},{6,7},{7,6},{8,9},{9,8},{10,11... | collective-permute-start | bytes 294920 | tf_op jit(solution)/shard_map/ppermute | solution.py:34
  133.2 0.6 copy-start.7
  136.6 19.8 %all-to-all-start.5 = ((bf16[4,384,384]{2,1,0:T(8,128)(2,1)}), bf16[4,384,384]{2,1,0:T(8,128)(2,1)S(1)}, u32[]{:S(2)}, u32[]{:S(2)}) async-start(bf16[4,384,384]{2,1,0:T(8,128)(2,1)} %bitcast.33), calls=%async_computation.6 | async-start | bytes 2359296 | tf_op jit(solution)/shard_map/all_to_all | solution.py:215
  140.7 7.1 %collective-permute-start.3 = (bf16[64,384]{1,0:T(8,128)(2,1)S(1)}, bf16[64,384]{1,0:T(8,128)(2,1)S(1)}, u32[]{:S(2)}, u32[]{:S(2)}) collective-permute-start(bf16[64,384]{1,0:T(8,128)(2,1)S(1)} %get-tuple-element.61), channel_id=1, source_target_pairs={{0,2},{2,0},{4,6},{6,4},{1,3},{3,1},{5,7},{7,5},{8,10},{10,8},{12,... | collective-permute-start | bytes 147464 | tf_op jit(solution)/shard_map/ppermute | solution.py:41
  143.6 4.2 %collective-permute-start.4 = (bf16[64,384]{1,0:T(8,128)(2,1)S(1)}, bf16[64,384]{1,0:T(8,128)(2,1)S(1)}, u32[]{:S(2)}, u32[]{:S(2)}) collective-permute-start(bf16[64,384]{1,0:T(8,128)(2,1)S(1)} %get-tuple-element.63), channel_id=1, source_target_pairs={{0,4},{2,6},{4,0},{6,2},{1,5},{3,7},{5,1},{7,3},{8,12},{10,14},{12... | collective-permute-start | bytes 147464 | tf_op jit(solution)/shard_map/ppermute | solution.py:41
  143.9 4.4 %collective-permute-start.5 = (bf16[64,384]{1,0:T(8,128)(2,1)S(1)}, bf16[64,384]{1,0:T(8,128)(2,1)S(1)}, u32[]{:S(2)}, u32[]{:S(2)}) collective-permute-start(bf16[64,384]{1,0:T(8,128)(2,1)S(1)} %get-tuple-element.62), channel_id=1, source_target_pairs={{0,6},{2,4},{4,2},{6,0},{1,7},{3,5},{5,3},{7,1},{8,14},{10,12},{12... | collective-permute-start | bytes 147464 | tf_op jit(solution)/shard_map/ppermute | solution.py:41
  174.0 4.5 %collective-permute-start.6 = (f32[32,384]{1,0:T(8,128)S(1)}, f32[32,384]{1,0:T(8,128)S(1)}, u32[]{:S(2)}, u32[]{:S(2)}) collective-permute-start(f32[32,384]{1,0:T(8,128)S(1)} %convert_reduce_fusion), channel_id=1, source_target_pairs={{0,2},{2,0},{1,3},{3,1},{4,6},{6,4},{5,7},{7,5},{8,10},{10,8},{9,1... | collective-permute-start | bytes 147464 | tf_op jit(solution)/shard_map/ppermute | solution.py:34
  178.6 5.6 %collective-permute-start.7 = (f32[40,384]{1,0:T(8,128)S(1)}, f32[40,384]{1,0:T(8,128)S(1)}, u32[]{:S(2)}, u32[]{:S(2)}) collective-permute-start(f32[40,384]{1,0:T(8,128)S(1)} %pad_maximum_fusion.2), channel_id=1, source_target_pairs={{0,1},{1,0},{2,3},{3,2},{4,5},{5,4},{6,7},{7,6},{8,9},{9,8},{10,11... | collective-permute-start | bytes 184328 | tf_op jit(solution)/shard_map/ppermute | solution.py:34
Sparse Core Ops, SparseCore 0:
  84.3 41.0 reduce-scatter.1

commit v9 on v8

--- a/solution.py
+++ b/solution.py
@@ -99,7 +99,7 @@
     return top + jnp.log(total), jnp.sum(weights * bars, axis=0), weights
 
 
-def backward_kernel(qd, stats_ref, kv, dq, dkv, kt, stat, *scratch):
+def backward_kernel(qd, stats_ref, kv, dq, dkv_out, kt, stat, dkv, *scratch):
     kt[...] = kv[:, :HEAD_DIM].T
     logsum, delta, unused = combine(stats_ref[:, :8, :], stats_ref[:, 8:, :])
     stat[:8, :] = logsum * LOG2E
@@ -134,7 +134,8 @@
         return carry
 
     lax.fori_loop(0, GROUP // 2, block, 0)
-    dkv[:, :HEAD_DIM] = dkv[:, :HEAD_DIM] * SCALE
+    dkv_out[:, :HEAD_DIM] = (dkv[:, :HEAD_DIM] * SCALE).astype(BF16)
+    dkv_out[:, HEAD_DIM:] = dkv[:, HEAD_DIM:].astype(BF16)
 
 
 def output_kernel(place, parts, stats_ref, upstream_ref, mixed_ref, keep_ref, give_ref):
@@ -261,12 +262,13 @@
     dq_parts, dkv_parts = call(
         backward_kernel,
         [qds, all_stats, kvs],
-        [shape(8, HEAD_DIM, ROWS), shape(KEYS, 2 * HEAD_DIM, dtype=F32)],
+        [shape(8, HEAD_DIM, ROWS), shape(KEYS, 2 * HEAD_DIM)],
         [VM] * 3,
         [VM] * 2,
         [
             pltpu.VMEM((HEAD_DIM, KEYS), BF16),
             pltpu.VMEM((16, ROWS), F32),
+            pltpu.VMEM((KEYS, 2 * HEAD_DIM), F32),
         ]
         + [pltpu.VMEM((KEYS, ROWS), t) for t in (F32, F32, BF16, BF16)] * 2,
         16_000_000_000,

time: 194 us -> 209 us (1.077)
  waiting for transfers between devices: 16.4 us -> 46.2 us
  blocking collectives: 73.2 us -> 52.9 us
  starting transfers between devices: 40.3 us -> 46.8 us
    all_to_all x3 -> x2, blocking collectives: 47.2 us -> 26.9 us  [swap(): return lax.all_to_all(blocks, axes, 0, 0)]
    all_to_all x4 -> x5, waiting for transfers between devices: 9.07 us -> 24.9 us  [swap(): return lax.all_to_all(blocks, axes, 0, 0)]
    reduce_scatter x1, waiting for transfers between devices: 2.7 us -> 16.1 us  [body(): dkv = lax.psum_scatter(dkv_parts, 'z', scatter_dimension=0, tiled=True)]
    all_to_all x4 -> x5, starting transfers between devices: 16.9 us -> 22.4 us  [swap(): return lax.all_to_all(blocks, axes, 0, 0)]
  transfers between devices with their start and end apart: 13 -> 14, of which waited for: 7 -> 8; matrix products, arithmetic and copies ran while one was open for 1% -> 1% of each run, Pallas kernels for 15% -> 12%
where the time goes in v9:
time: 209 us; the launch traced here: 208 us
  blocking collectives  52.9 us (25%)
  starting transfers between devices  46.8 us (22%)
  waiting for transfers between devices  46.2 us (22%)
  Pallas kernels  37.7 us (18%)
  between operations  14.2 us (7%)
  other arithmetic  4.21 us (2%)
  local copies, waits for them, and re-layouts  3.45 us (2%)
  matrix products  2.95 us (1%)
    pallas_call x7, Pallas kernels, call(): pl.pallas_call(kernel, out_shape=outs, in_specs=in_specs, out_specs=out_s...  37.7 us
    all_to_all x2, blocking collectives, swap(): return lax.all_to_all(blocks, axes, 0, 0)  26.9 us
    all_gather x1, blocking collectives, body(): kvs = lax.all_gather(keyval, 'z', axis=0, tiled=True)  26 us
    all_to_all x5, waiting for transfers between devices, swap(): return lax.all_to_all(blocks, axes, 0, 0)  24.9 us
    all_to_all x5, starting transfers between devices, swap(): return lax.all_to_all(blocks, axes, 0, 0)  22.4 us
    ppermute x5, starting transfers between devices, send(): lax.ppermute(array, axis, [(i, (i + step) % size) for i in range(size)])  20.7 us
    reduce_scatter x1, waiting for transfers between devices, body(): dkv = lax.psum_scatter(dkv_parts, 'z', scatter_dimension=0, tiled=True)  16.1 us
  transfers between devices with their start and end apart: 14, of which 8 were waited for; matrix products, arithmetic and copies ran while one was open for 1% of the time, Pallas kernels for 12%

profile of v9, /device:TPU:1, one launch (start us, length us, event | category | flops | bytes accessed | tf_op | source)
XLA Modules:
  0.0 208.4 jit_solution(7367443994401980299)
XLA Ops:
  7.2 2.3 %convolution_convert_fusion = bf16[128,512]{1,0:T(8,128)(2,1)S(1)} fusion(bf16[512,1536]{1,0:T(8,128)(2,1)} %w_out_ref.1, bf16[1,128,1536]{2,1,0:T(8,128)(2,1)} %param.6), kind=kOutput, calls=%fused_computation.1 | convolution fusion | flops 201392128 | bytes 2097152 | tf_op jit(solution)/shard_map/dot_general | solution.py:234
  11.5 6.0 %all-to-all-start = ((bf16[8,128,1024]{2,1,0:T(8,128)(2,1)}), bf16[8,128,1024]{2,1,0:T(8,128)(2,1)}, u32[]{:S(2)}, u32[]{:S(2)}) async-start(bf16[8,128,1024]{2,1,0:T(8,128)(2,1)} %broadcast_in_dim.41), calls=%async_computation | async-start | bytes 4194304 | tf_op jit(solution)/shard_map/all_to_all | solution.py:216
  20.2 26.0 %all_gather.3.kv = bf16[1024,256]{1,0:T(8,128)(2,1)} all-gather(bf16[128,256]{1,0:T(8,128)(2,1)S(1)} %convolution_convert_fusion.2), channel_id=1, replica_groups=mesh['x'=4,'z'=8,'yl'=2,'yh'=2,'core'=2] {'z'}, dimensions={0}, use_global_device_ids=true | all-gather | bytes 589824 | tf_op jit(solution)/shard_map/all_gather | solution.py:239
  47.2 9.9 %shard_map.92 = (bf16[8,128,512]{2,1,0:T(8,128)(2,1)}, f32[8,16,512]{2,1,0:T(8,128)}) custom-call(bf16[8,128,1024]{2,1,0:T(8,128)(2,1)} %all-to-all-done.qd, bf16[1024,256]{1,0:T(8,128)(2,1)} %all_gather.3.kv), custom_call_target="tpu_custom_call" | custom-call | flops 10000000000 | bytes 6000000 | tf_op jit(solution)/shard_map/pallas_call | solution.py:200
  57.0 9.8 %all_to_all.35.stats_ref = f32[8,16,512]{2,1,0:T(8,128)} all-to-all(f32[8,16,512]{2,1,0:T(8,128)} %get-tuple-element.37), channel_id=1, replica_groups=mesh['x'=4,'z'=8,'yl'=2,'yh'=2,'core'=2] {'x','yl'}, dimensions={0} | all-to-all | bytes 524288 | tf_op jit(solution)/shard_map/all_to_all | solution.py:216
  66.8 3.6 %all-to-all-start.2 = ((bf16[8,128,512]{2,1,0:T(8,128)(2,1)}), bf16[8,128,512]{2,1,0:T(8,128)(2,1)S(1)}, u32[]{:S(2)}, u32[]{:S(2)}) async-start(bf16[8,128,512]{2,1,0:T(8,128)(2,1)} %get-tuple-element.40), calls=%async_computation.2 | async-start | bytes 2097152 | tf_op jit(solution)/shard_map/all_to_all | solution.py:216
  70.4 13.6 %shard_map.93 = (bf16[8,128,512]{2,1,0:T(8,128)(2,1)}, bf16[1024,256]{1,0:T(8,128)(2,1)}) custom-call(bf16[8,128,1024]{2,1,0:T(8,128)(2,1)} %all-to-all-done.qd, f32[8,16,512]{2,1,0:T(8,128)} %all_to_all.35.stats_ref, bf16[1024,256]{1,0:T(8,128)(2,1)} %all_gather.3.kv), custom_call_target="tpu_custom_call" | custom-call | flops 16000000000 | bytes 6000000 | tf_op jit(solution)/shard_map/pallas_call | solution.py:200
  85.0 3.1 %shard_map.94 = (bf16[128,512]{1,0:T(8,128)(2,1)}, bf16[512,768]{1,0:T(8,128)(2,1)}, bf16[512,768]{1,0:T(8,128)(2,1)}) custom-call(s32[2]{0:T(128)} %pad_add_fusion.place, bf16[8,128,512]{2,1,0:T(8,128)(2,1)} %copy-done.1, f32[8,16,512]{2,1,0:T(8,128)} %all_to_all.35.stats_ref, bf16[128,1536]{1,0:T(8,128)(2,1)} %bitcast.38), custom_call_target="tpu_custom_call" | custom-call | flops 400000000 | bytes 6000000 | tf_op jit(solution)/shard_map/pallas_call | solution.py:200
  88.2 6.2 %collective-permute-start.1 = (bf16[512,768]{1,0:T(8,128)(2,1)}, bf16[512,768]{1,0:T(8,128)(2,1)S(1)}, u32[]{:S(2)}, u32[]{:S(2)}) collective-permute-start(bf16[512,768]{1,0:T(8,128)(2,1)} %get-tuple-element.43), channel_id=1, source_target_pairs={{0,1},{1,0},{2,3},{3,2},{4,5},{5,4},{6,7},{7,6},{8,9},{9,8},{10,11... | collective-permute-start | bytes 2359304 | tf_op jit(solution)/shard_map/ppermute | solution.py:34
  94.4 2.8 %shard_map.95 = bf16[128,1536]{1,0:T(8,128)(2,1)} custom-call(bf16[128,1536]{1,0:T(8,128)(2,1)} %bitcast.34, bf16[128,512]{1,0:T(8,128)(2,1)} %get-tuple-element.44.mixed_ref, bf16[512,1536]{1,0:T(8,128)(2,1)} %w_out_ref.1), custom_call_target="tpu_custom_call" | custom-call | flops 20000000000 | bytes 6000000 | tf_op jit(solution)/shard_map/pallas_call | solution.py:200
  98.2 5.4 %all-to-all-start.3 = ((bf16[8,128,512]{2,1,0:T(8,128)(2,1)}), bf16[8,128,512]{2,1,0:T(8,128)(2,1)S(1)}, u32[]{:S(2)}, u32[]{:S(2)}) async-start(bf16[8,128,512]{2,1,0:T(8,128)(2,1)} %get-tuple-element.47), calls=%async_computation.3 | async-start | bytes 2097152 | tf_op jit(solution)/shard_map/all_to_all | solution.py:216
  104.3 15.9 %all-to-all-done.3.dq_ref = bf16[8,128,512]{2,1,0:T(8,128)(2,1)S(1)} async-done(((bf16[8,128,512]{2,1,0:T(8,128)(2,1)}), bf16[8,128,512]{2,1,0:T(8,128)(2,1)S(1)}, u32[]{:S(2)}, u32[]{:S(2)}) %all-to-all-start.3) | async-done | bytes 1048608 | tf_op jit(solution)/shard_map/all_to_all | solution.py:216
  120.2 3.5 %all-to-all-start.4 = ((bf16[4,128,768]{2,1,0:T(8,128)(2,1)}), bf16[4,128,768]{2,1,0:T(8,128)(2,1)S(1)}, u32[]{:S(2)}, u32[]{:S(2)}) async-start(bf16[4,128,768]{2,1,0:T(8,128)(2,1)} %bitcast.5), calls=%async_computation.5 | async-start | bytes 1572864 | tf_op jit(solution)/shard_map/all_to_all | solution.py:216
  123.7 16.1 %reduce-scatter.2.cloned.1.call-done.dkv_ref = bf16[128,256]{1,0:T(8,128)(2,1)} async-done(((bf16[1024,256]{1,0:T(8,128)(2,1)}), bf16[128,256]{1,0:T(8,128)(2,1)}) %reduce-scatter.2.cloned.1.call-update) | async-done | bytes 65552 | tf_op jit(solution)/shard_map/reduce_scatter | solution.py:277
  139.8 2.2 %shard_map.96 = (bf16[128,768]{1,0:T(8,128)(2,1)}, bf16[128,384]{1,0:T(8,128)(2,1)}, bf16[128,384]{1,0:T(8,128)(2,1)}) custom-call(s32[2]{0:T(128)} %pad_add_fusion.place, bf16[8,128,512]{2,1,0:T(8,128)(2,1)} %copy-done.2, bf16[128,256]{1,0:T(8,128)(2,1)} %reduce-scatter.2.cloned.1.call-done.dkv_ref), custom_call_target="tpu_custom_call" | custom-call | tf_op jit(solution)/shard_map/pallas_call | solution.py:200
  142.0 5.4 %collective-permute-start.2 = (bf16[128,384]{1,0:T(8,128)(2,1)}, bf16[128,384]{1,0:T(8,128)(2,1)S(1)}, u32[]{:S(2)}, u32[]{:S(2)}) collective-permute-start(bf16[128,384]{1,0:T(8,128)(2,1)} %get-tuple-element.54), channel_id=1, source_target_pairs={{0,1},{1,0},{2,3},{3,2},{4,5},{5,4},{6,7},{7,6},{8,9},{9,8},{10,11... | collective-permute-start | bytes 294920 | tf_op jit(solution)/shard_map/ppermute | solution.py:34
  149.2 2.8 %shard_map.98 = bf16[1536,384]{1,0:T(8,128)(2,1)} custom-call(bf16[128,1536]{1,0:T(8,128)(2,1)} %bitcast.35, bf16[128,1536]{1,0:T(8,128)(2,1)} %copy-done.6, bf16[128,384]{1,0:T(8,128)(2,1)} %get-tuple-element.53.keep_ref, bf16[128,384]{1,0:T(8,128)(2,1)} %copy-done.7), custom_call_target="tpu_custom_call" | custom-call | tf_op jit(solution)/shard_map/pallas_call | solution.py:200
  152.0 3.9 %all-to-all-start.5 = ((bf16[4,384,384]{2,1,0:T(8,128)(2,1)}), bf16[4,384,384]{2,1,0:T(8,128)(2,1)S(1)}, u32[]{:S(2)}, u32[]{:S(2)}) async-start(bf16[4,384,384]{2,1,0:T(8,128)(2,1)} %bitcast.33), calls=%async_computation.6 | async-start | bytes 2359296 | tf_op jit(solution)/shard_map/all_to_all | solution.py:216
  156.2 2.9 %collective-permute-start.3 = (bf16[64,384]{1,0:T(8,128)(2,1)S(1)}, bf16[64,384]{1,0:T(8,128)(2,1)S(1)}, u32[]{:S(2)}, u32[]{:S(2)}) collective-permute-start(bf16[64,384]{1,0:T(8,128)(2,1)S(1)} %get-tuple-element.61), channel_id=1, source_target_pairs={{0,2},{2,0},{4,6},{6,4},{1,3},{3,1},{5,7},{7,5},{8,10},{10,8},{12,... | collective-permute-start | bytes 147464 | tf_op jit(solution)/shard_map/ppermute | solution.py:41
  160.0 3.3 %shard_map.97 = bf16[128,1536]{1,0:T(8,128)(2,1)} custom-call(bf16[128,768]{1,0:T(8,128)(2,1)} %get-tuple-element.51.both_ref, bf16[1536,512]{1,0:T(8,128)(2,1)} %w_query_ref.1, bf16[1536,256]{1,0:T(8,128)(2,1)} %w_keyval_ref.1), custom_call_target="tpu_custom_call" | custom-call | flops 300000000 | bytes 6000000 | tf_op jit(solution)/shard_map/pallas_call | solution.py:200
  163.8 8.1 %all-to-all-done.5 = bf16[4,384,384]{2,1,0:T(8,128)(2,1)S(1)} async-done(((bf16[4,384,384]{2,1,0:T(8,128)(2,1)}), bf16[4,384,384]{2,1,0:T(8,128)(2,1)S(1)}, u32[]{:S(2)}, u32[]{:S(2)}) %all-to-all-start.5) | async-done | bytes 1179680 | tf_op jit(solution)/shard_map/all_to_all | solution.py:216
  172.3 17.1 %all_to_all.36 = bf16[16,32,384]{2,1,0:T(8,128)(2,1)S(1)} all-to-all(bf16[16,32,384]{2,1,0:T(8,128)(2,1)S(1)} %pad_maximum_fusion), channel_id=1, replica_groups=mesh['x'=4,'z'=8,'yl'=2,'yh'=2,'core'=2] {'z','yl'}, dimensions={0} | all-to-all | bytes 786432 | tf_op jit(solution)/shard_map/all_to_all | solution.py:216
  189.5 2.6 %collective-permute-start.6 = (f32[32,384]{1,0:T(8,128)S(1)}, f32[32,384]{1,0:T(8,128)S(1)}, u32[]{:S(2)}, u32[]{:S(2)}) collective-permute-start(f32[32,384]{1,0:T(8,128)S(1)} %convert_reduce_fusion), channel_id=1, source_target_pairs={{0,2},{2,0},{1,3},{3,1},{4,6},{6,4},{5,7},{7,5},{8,10},{10,8},{9,1... | collective-permute-start | bytes 147464 | tf_op jit(solution)/shard_map/ppermute | solution.py:34
  194.0 4.7 %collective-permute-start.7 = (f32[40,384]{1,0:T(8,128)S(1)}, f32[40,384]{1,0:T(8,128)S(1)}, u32[]{:S(2)}, u32[]{:S(2)}) collective-permute-start(f32[40,384]{1,0:T(8,128)S(1)} %pad_maximum_fusion.2), channel_id=1, source_target_pairs={{0,1},{1,0},{2,3},{3,2},{4,5},{5,4},{6,7},{7,6},{8,9},{9,8},{10,11... | collective-permute-start | bytes 184328 | tf_op jit(solution)/shard_map/ppermute | solution.py:34
  (62 shorter events, 17.1 us)
Async XLA Ops:
  7.2 2.3 %copy-start.3 = (bf16[1,128,1536]{2,1,0:T(8,128)(2,1)S(1)}, bf16[1,128,1536]{2,1,0:T(8,128)(2,1)}, u32[]{:S(2)}) copy-start(bf16[1,128,1536]{2,1,0:T(8,128)(2,1)} %param.5) | copy-start | bytes 1179652
  7.2 2.3 %copy-start = (bf16[1536,512]{1,0:T(8,128)(2,1)S(1)}, bf16[1536,512]{1,0:T(8,128)(2,1)}, u32[]{:S(2)}) copy-start(bf16[1536,512]{1,0:T(8,128)(2,1)} %w_query_ref.1) | copy-start | bytes 4718596
  11.5 7.8 %copy-start.4 = (bf16[1536,256]{1,0:T(8,128)(2,1)S(1)}, bf16[1536,256]{1,0:T(8,128)(2,1)}, u32[]{:S(2)}) copy-start(bf16[1536,256]{1,0:T(8,128)(2,1)} %w_keyval_ref.1) | copy-start | bytes 2359300
  11.5 35.7 %all-to-all-start = ((bf16[8,128,1024]{2,1,0:T(8,128)(2,1)}), bf16[8,128,1024]{2,1,0:T(8,128)(2,1)}, u32[]{:S(2)}, u32[]{:S(2)}) async-start(bf16[8,128,1024]{2,1,0:T(8,128)(2,1)} %broadcast_in_dim.41), calls=%async_computation | async-start | bytes 4194304 | tf_op jit(solution)/shard_map/all_to_all | solution.py:216
  17.5 28.7 %collective-permute-start = (bf16[128,1536]{1,0:T(8,128)(2,1)S(1)}, bf16[128,1536]{1,0:T(8,128)(2,1)S(1)}, u32[]{:S(2)}, u32[]{:S(2)}) collective-permute-start(bf16[128,1536]{1,0:T(8,128)(2,1)S(1)} %bitcast.36), channel_id=1, source_target_pairs={{0,1},{1,0},{2,3},{3,2},{4,5},{5,4},{6,7},{7,6},{8,9},{9,8},{10,11... | collective-permute-start | bytes 1179656 | tf_op jit(solution)/shard_map/ppermute | solution.py:34
  46.2 10.8 %copy-start.6 = (bf16[128,1536]{1,0:T(8,128)(2,1)}, bf16[128,1536]{1,0:T(8,128)(2,1)S(1)}, u32[]{:S(2)}) copy-start(bf16[128,1536]{1,0:T(8,128)(2,1)S(1)} %collective-permute-done.other_ref) | copy-start | bytes 1179652
  66.8 17.2 %all-to-all-start.2 = ((bf16[8,128,512]{2,1,0:T(8,128)(2,1)}), bf16[8,128,512]{2,1,0:T(8,128)(2,1)S(1)}, u32[]{:S(2)}, u32[]{:S(2)}) async-start(bf16[8,128,512]{2,1,0:T(8,128)(2,1)} %get-tuple-element.40), calls=%async_computation.2 | async-start | bytes 2097152 | tf_op jit(solution)/shard_map/all_to_all | solution.py:216
  84.0 1.0 copy-start.1
  88.2 9.0 %collective-permute-start.1 = (bf16[512,768]{1,0:T(8,128)(2,1)}, bf16[512,768]{1,0:T(8,128)(2,1)S(1)}, u32[]{:S(2)}, u32[]{:S(2)}) collective-permute-start(bf16[512,768]{1,0:T(8,128)(2,1)} %get-tuple-element.43), channel_id=1, source_target_pairs={{0,1},{1,0},{2,3},{3,2},{4,5},{5,4},{6,7},{7,6},{8,9},{9,8},{10,11... | collective-permute-start | bytes 2359304 | tf_op jit(solution)/shard_map/ppermute | solution.py:34
  94.4 2.8 %copy-start.5 = (bf16[512,768]{1,0:T(8,128)(2,1)S(1)}, bf16[512,768]{1,0:T(8,128)(2,1)}, u32[]{:S(2)}) copy-start(bf16[512,768]{1,0:T(8,128)(2,1)} %get-tuple-element.42) | copy-start | bytes 2359300
  98.2 21.9 %all-to-all-start.3 = ((bf16[8,128,512]{2,1,0:T(8,128)(2,1)}), bf16[8,128,512]{2,1,0:T(8,128)(2,1)S(1)}, u32[]{:S(2)}, u32[]{:S(2)}) async-start(bf16[8,128,512]{2,1,0:T(8,128)(2,1)} %get-tuple-element.47), calls=%async_computation.3 | async-start | bytes 2097152 | tf_op jit(solution)/shard_map/all_to_all | solution.py:216
  103.6 36.2 %reduce-scatter.2.cloned.1.call-start = ((), (), s32[]{:S(2)}) async-start(), calls=%async_computation.8 | async-start | bytes 589824 | tf_op jit(solution)/shard_map/reduce_scatter | solution.py:277
  120.2 19.7 %copy-start.2 = (bf16[8,128,512]{2,1,0:T(8,128)(2,1)}, bf16[8,128,512]{2,1,0:T(8,128)(2,1)S(1)}, u32[]{:S(2)}) copy-start(bf16[8,128,512]{2,1,0:T(8,128)(2,1)S(1)} %all-to-all-done.3.dq_ref) | copy-start | bytes 3145732
  120.2 31.8 %all-to-all-start.4 = ((bf16[4,128,768]{2,1,0:T(8,128)(2,1)}), bf16[4,128,768]{2,1,0:T(8,128)(2,1)S(1)}, u32[]{:S(2)}, u32[]{:S(2)}) async-start(bf16[4,128,768]{2,1,0:T(8,128)(2,1)} %bitcast.5), calls=%async_computation.5 | async-start | bytes 1572864 | tf_op jit(solution)/shard_map/all_to_all | solution.py:216
  142.0 6.5 %collective-permute-start.2 = (bf16[128,384]{1,0:T(8,128)(2,1)}, bf16[128,384]{1,0:T(8,128)(2,1)S(1)}, u32[]{:S(2)}, u32[]{:S(2)}) collective-permute-start(bf16[128,384]{1,0:T(8,128)(2,1)} %get-tuple-element.54), channel_id=1, source_target_pairs={{0,1},{1,0},{2,3},{3,2},{4,5},{5,4},{6,7},{7,6},{8,9},{9,8},{10,11... | collective-permute-start | bytes 294920 | tf_op jit(solution)/shard_map/ppermute | solution.py:34
  148.6 0.6 copy-start.7
  152.0 19.9 %all-to-all-start.5 = ((bf16[4,384,384]{2,1,0:T(8,128)(2,1)}), bf16[4,384,384]{2,1,0:T(8,128)(2,1)S(1)}, u32[]{:S(2)}, u32[]{:S(2)}) async-start(bf16[4,384,384]{2,1,0:T(8,128)(2,1)} %bitcast.33), calls=%async_computation.6 | async-start | bytes 2359296 | tf_op jit(solution)/shard_map/all_to_all | solution.py:216
  156.2 7.1 %collective-permute-start.3 = (bf16[64,384]{1,0:T(8,128)(2,1)S(1)}, bf16[64,384]{1,0:T(8,128)(2,1)S(1)}, u32[]{:S(2)}, u32[]{:S(2)}) collective-permute-start(bf16[64,384]{1,0:T(8,128)(2,1)S(1)} %get-tuple-element.61), channel_id=1, source_target_pairs={{0,2},{2,0},{4,6},{6,4},{1,3},{3,1},{5,7},{7,5},{8,10},{10,8},{12,... | collective-permute-start | bytes 147464 | tf_op jit(solution)/shard_map/ppermute | solution.py:41
  159.0 4.3 %collective-permute-start.4 = (bf16[64,384]{1,0:T(8,128)(2,1)S(1)}, bf16[64,384]{1,0:T(8,128)(2,1)S(1)}, u32[]{:S(2)}, u32[]{:S(2)}) collective-permute-start(bf16[64,384]{1,0:T(8,128)(2,1)S(1)} %get-tuple-element.63), channel_id=1, source_target_pairs={{0,4},{2,6},{4,0},{6,2},{1,5},{3,7},{5,1},{7,3},{8,12},{10,14},{12... | collective-permute-start | bytes 147464 | tf_op jit(solution)/shard_map/ppermute | solution.py:41
  159.3 4.4 %collective-permute-start.5 = (bf16[64,384]{1,0:T(8,128)(2,1)S(1)}, bf16[64,384]{1,0:T(8,128)(2,1)S(1)}, u32[]{:S(2)}, u32[]{:S(2)}) collective-permute-start(bf16[64,384]{1,0:T(8,128)(2,1)S(1)} %get-tuple-element.62), channel_id=1, source_target_pairs={{0,6},{2,4},{4,2},{6,0},{1,7},{3,5},{5,3},{7,1},{8,14},{10,12},{12... | collective-permute-start | bytes 147464 | tf_op jit(solution)/shard_map/ppermute | solution.py:41
  189.5 4.5 %collective-permute-start.6 = (f32[32,384]{1,0:T(8,128)S(1)}, f32[32,384]{1,0:T(8,128)S(1)}, u32[]{:S(2)}, u32[]{:S(2)}) collective-permute-start(f32[32,384]{1,0:T(8,128)S(1)} %convert_reduce_fusion), channel_id=1, source_target_pairs={{0,2},{2,0},{1,3},{3,1},{4,6},{6,4},{5,7},{7,5},{8,10},{10,8},{9,1... | collective-permute-start | bytes 147464 | tf_op jit(solution)/shard_map/ppermute | solution.py:34
  194.0 5.6 %collective-permute-start.7 = (f32[40,384]{1,0:T(8,128)S(1)}, f32[40,384]{1,0:T(8,128)S(1)}, u32[]{:S(2)}, u32[]{:S(2)}) collective-permute-start(f32[40,384]{1,0:T(8,128)S(1)} %pad_maximum_fusion.2), channel_id=1, source_target_pairs={{0,1},{1,0},{2,3},{3,2},{4,5},{5,4},{6,7},{7,6},{8,9},{9,8},{10,11... | collective-permute-start | bytes 184328 | tf_op jit(solution)/shard_map/ppermute | solution.py:34
Sparse Core Ops, SparseCore 0:
  106.9 32.8 reduce-scatter.1

commit v10 on v8

--- a/solution.py
+++ b/solution.py
@@ -55,6 +55,14 @@
     return op(values.reshape(-1, 8, values.shape[1]), axis=0)
 
 
+def project_kernel(tokens_ref, upstream_ref, w_query_ref, w_out_ref, out_ref):
+    query = dot(tokens_ref[...], w_query_ref[...]).astype(BF16)
+    dmixed = dot(upstream_ref[...], w_out_ref[...], NT).astype(BF16)
+    for i in range(GROUP):
+        out_ref[i, :, :ROWS] = query
+        out_ref[i, :, ROWS:] = dmixed
+
+
 def forward_kernel(qd, kv, mixed, stats_out, vt, stats_ref, *scratch):
     vt[...] = kv[:, HEAD_DIM:].T
 
@@ -215,10 +223,6 @@
     return lax.all_to_all(blocks, axes, 0, 0)
 
 
-def share(array, axes, count):
-    return swap(jnp.broadcast_to(array[None], (count,) + array.shape), axes)
-
-
 def added(blocks):
     return jnp.sum(blocks.astype(F32), axis=0)
 
@@ -229,11 +233,17 @@
     core = lax.axis_index("core")
     group = lax.axis_index("x") * 2 + lax.axis_index("yl")
     place = jnp.stack([core, group]).astype(jnp.int32)
-    query = jnp.dot(local, w_query, preferred_element_type=F32).astype(BF16)
-    dmixed = jnp.dot(cotangent, w_out.T, preferred_element_type=F32).astype(BF16)
-    qd = jnp.concatenate([query, dmixed], axis=1)
-    qds = share(qd, ("x", "yl"), 8)
-    qd, early = lax.optimization_barrier((qd, local))
+    copies = call(
+        project_kernel,
+        [local, cotangent, w_query, w_out],
+        shape(8, POS, 2 * ROWS),
+        [VM] * 4,
+        VM,
+        [],
+        400_000_000,
+    )
+    qds = swap(copies, ("x", "yl"))
+    copies, early = lax.optimization_barrier((copies, local))
     keyval = jnp.dot(early, w_keyval, preferred_element_type=F32).astype(BF16)
     kvs = lax.all_gather(keyval, "z", axis=0, tiled=True)
     tokens_other = send(early, "core", 2, 1)

time: 194 us -> 194 us (level)
  Pallas kernels: 37.9 us -> 42.3 us
  matrix products: 2.95 us -> 0.27 us
    pallas_call x7 -> x8, Pallas kernels: 37.9 us -> 42.3 us  [call(): pl.pallas_call(kernel, out_shape=outs, in_specs=in_specs, out_specs=out_s...]
    dot_general x2 -> x0, matrix products: 2.68 us -> none  [the longest x1 2.3 us: body(): jnp.dot(cotangent, w_out.T, preferred_element_type=F32).astype(BF16)]
where the time goes in v10:
time: 194 us; the launch traced here: 193 us
  blocking collectives  73.3 us (38%)
  Pallas kernels  42.3 us (22%)
  starting transfers between devices  40.6 us (21%)
  waiting for transfers between devices  15.9 us (8%)
  between operations  14.2 us (7%)
  other arithmetic  4.17 us (2%)
  local copies, waits for them, and re-layouts  2.28 us (1%)
    all_to_all x3, blocking collectives, swap(): return lax.all_to_all(blocks, axes, 0, 0)  47.2 us
    pallas_call x8, Pallas kernels, call(): pl.pallas_call(kernel, out_shape=outs, in_specs=in_specs, out_specs=out_s...  42.3 us
    all_gather x1, blocking collectives, body(): kvs = lax.all_gather(keyval, 'z', axis=0, tiled=True)  26.1 us
    ppermute x5, starting transfers between devices, send(): lax.ppermute(array, axis, [(i, (i + step) % size) for i in range(size)])  19.7 us
    all_to_all x4, starting transfers between devices, swap(): return lax.all_to_all(blocks, axes, 0, 0)  17 us
    all_to_all x4, waiting for transfers between devices, swap(): return lax.all_to_all(blocks, axes, 0, 0)  8.93 us
    ppermute x5, waiting for transfers between devices, send(): lax.ppermute(array, axis, [(i, (i + step) % size) for i in range(size)])  4 us
  transfers between devices with their start and end apart: 13, of which 7 were waited for; matrix products, arithmetic and copies ran while one was open for 1% of the time, Pallas kernels for 15%

profile of v10, /device:TPU:1, one launch (start us, length us, event | category | flops | bytes accessed | tf_op | source)
XLA Modules:
  0.0 193.0 jit_solution(4352438382457539450)
XLA Ops:
  7.2 4.4 %shard_map.92 = bf16[8,128,1024]{2,1,0:T(8,128)(2,1)} custom-call(bf16[128,1536]{1,0:T(8,128)(2,1)} %bitcast.28, bf16[128,1536]{1,0:T(8,128)(2,1)} %bitcast.33, bf16[1536,512]{1,0:T(8,128)(2,1)} %w_query_ref.3, bf16[512,1536]{1,0:T(8,128)(2,1)} %w_out_ref.3), custom_call_target="tpu_custom_call" | custom-call | flops 400000000 | bytes 6000000 | tf_op jit(solution)/shard_map/pallas_call | solution.py:207
  11.6 6.0 %all-to-all-start = ((bf16[8,128,1024]{2,1,0:T(8,128)(2,1)}), bf16[8,128,1024]{2,1,0:T(8,128)(2,1)}, u32[]{:S(2)}, u32[]{:S(2)}) async-start(bf16[8,128,1024]{2,1,0:T(8,128)(2,1)} %shard_map.92), calls=%async_computation | async-start | bytes 4194304 | tf_op jit(solution)/shard_map/all_to_all | solution.py:223
  20.2 26.1 %all_gather.3.kv = bf16[1024,256]{1,0:T(8,128)(2,1)} all-gather(bf16[128,256]{1,0:T(8,128)(2,1)S(1)} %convolution_convert_fusion), channel_id=1, replica_groups=mesh['x'=4,'z'=8,'yl'=2,'yh'=2,'core'=2] {'z'}, dimensions={0}, use_global_device_ids=true | all-gather | bytes 589824 | tf_op jit(solution)/shard_map/all_gather | solution.py:248
  47.2 9.9 %shard_map.93 = (bf16[8,128,512]{2,1,0:T(8,128)(2,1)}, f32[8,16,512]{2,1,0:T(8,128)}) custom-call(bf16[8,128,1024]{2,1,0:T(8,128)(2,1)} %all-to-all-done.qd, bf16[1024,256]{1,0:T(8,128)(2,1)} %all_gather.3.kv), custom_call_target="tpu_custom_call" | custom-call | flops 10000000000 | bytes 6000000 | tf_op jit(solution)/shard_map/pallas_call | solution.py:207
  57.1 9.8 %all_to_all.35.stats_ref = f32[8,16,512]{2,1,0:T(8,128)} all-to-all(f32[8,16,512]{2,1,0:T(8,128)} %get-tuple-element.37), channel_id=1, replica_groups=mesh['x'=4,'z'=8,'yl'=2,'yh'=2,'core'=2] {'x','yl'}, dimensions={0} | all-to-all | bytes 524288 | tf_op jit(solution)/shard_map/all_to_all | solution.py:223
  66.9 3.6 %all-to-all-start.2 = ((bf16[8,128,512]{2,1,0:T(8,128)(2,1)}), bf16[8,128,512]{2,1,0:T(8,128)(2,1)S(1)}, u32[]{:S(2)}, u32[]{:S(2)}) async-start(bf16[8,128,512]{2,1,0:T(8,128)(2,1)} %get-tuple-element.40), calls=%async_computation.2 | async-start | bytes 2097152 | tf_op jit(solution)/shard_map/all_to_all | solution.py:223
  70.5 13.7 %shard_map.94 = (bf16[8,128,512]{2,1,0:T(8,128)(2,1)}, f32[1024,256]{1,0:T(8,128)}) custom-call(bf16[8,128,1024]{2,1,0:T(8,128)(2,1)} %all-to-all-done.qd, f32[8,16,512]{2,1,0:T(8,128)} %all_to_all.35.stats_ref, bf16[1024,256]{1,0:T(8,128)(2,1)} %all_gather.3.kv), custom_call_target="tpu_custom_call" | custom-call | flops 16000000000 | bytes 6000000 | tf_op jit(solution)/shard_map/pallas_call | solution.py:207
  85.3 3.2 %shard_map.95 = (bf16[128,512]{1,0:T(8,128)(2,1)}, bf16[512,768]{1,0:T(8,128)(2,1)}, bf16[512,768]{1,0:T(8,128)(2,1)}) custom-call(s32[2]{0:T(128)} %pad_add_fusion.place, bf16[8,128,512]{2,1,0:T(8,128)(2,1)} %copy-done, f32[8,16,512]{2,1,0:T(8,128)} %all_to_all.35.stats_ref, bf16[128,1536]{1,0:T(8,128)(2,1)} %bitcast.34), custom_call_target="tpu_custom_call" | custom-call | flops 400000000 | bytes 6000000 | tf_op jit(solution)/shard_map/pallas_call | solution.py:207
  88.5 6.2 %collective-permute-start.1 = (bf16[512,768]{1,0:T(8,128)(2,1)}, bf16[512,768]{1,0:T(8,128)(2,1)S(1)}, u32[]{:S(2)}, u32[]{:S(2)}) collective-permute-start(bf16[512,768]{1,0:T(8,128)(2,1)} %get-tuple-element.43), channel_id=1, source_target_pairs={{0,1},{1,0},{2,3},{3,2},{4,5},{5,4},{6,7},{7,6},{8,9},{9,8},{10,11... | collective-permute-start | bytes 2359304 | tf_op jit(solution)/shard_map/ppermute | solution.py:34
  94.7 2.8 %shard_map.96 = bf16[128,1536]{1,0:T(8,128)(2,1)} custom-call(bf16[128,1536]{1,0:T(8,128)(2,1)} %bitcast.29, bf16[128,512]{1,0:T(8,128)(2,1)} %get-tuple-element.44.mixed_ref, bf16[512,1536]{1,0:T(8,128)(2,1)} %w_out_ref.3), custom_call_target="tpu_custom_call" | custom-call | flops 20000000000 | bytes 6000000 | tf_op jit(solution)/shard_map/pallas_call | solution.py:207
  99.0 20.3 %all_to_all.36.dq_ref = bf16[8,128,512]{2,1,0:T(8,128)(2,1)} all-to-all(bf16[8,128,512]{2,1,0:T(8,128)(2,1)S(1)} %copy-done.3), channel_id=1, replica_groups=mesh['x'=4,'z'=8,'yl'=2,'yh'=2,'core'=2] {'x','yl'}, dimensions={0} | all-to-all | bytes 2097152 | tf_op jit(solution)/shard_map/all_to_all | solution.py:223
  119.3 3.5 %all-to-all-start.4 = ((bf16[4,128,768]{2,1,0:T(8,128)(2,1)}), bf16[4,128,768]{2,1,0:T(8,128)(2,1)S(1)}, u32[]{:S(2)}, u32[]{:S(2)}) async-start(bf16[4,128,768]{2,1,0:T(8,128)(2,1)} %bitcast.5), calls=%async_computation.5 | async-start | bytes 1572864 | tf_op jit(solution)/shard_map/all_to_all | solution.py:223
  122.8 2.6 %reduce-scatter.2.cloned.1.call-done.dkv_ref = f32[128,256]{1,0:T(8,128)} async-done(((f32[1024,256]{1,0:T(8,128)}), f32[128,256]{1,0:T(8,128)}) %reduce-scatter.2.cloned.1.call-update) | async-done | bytes 131088 | tf_op jit(solution)/shard_map/reduce_scatter | solution.py:285
  125.4 2.2 %shard_map.97 = (bf16[128,768]{1,0:T(8,128)(2,1)}, bf16[128,384]{1,0:T(8,128)(2,1)}, bf16[128,384]{1,0:T(8,128)(2,1)}) custom-call(s32[2]{0:T(128)} %pad_add_fusion.place, bf16[8,128,512]{2,1,0:T(8,128)(2,1)} %all_to_all.36.dq_ref, f32[128,256]{1,0:T(8,128)} %reduce-scatter.2.cloned.1.call-done.dkv_ref), custom_call_target="tpu_custom_call" | custom-call | tf_op jit(solution)/shard_map/pallas_call | solution.py:207
  127.6 4.4 %collective-permute-start.2 = (bf16[128,384]{1,0:T(8,128)(2,1)}, bf16[128,384]{1,0:T(8,128)(2,1)S(1)}, u32[]{:S(2)}, u32[]{:S(2)}) collective-permute-start(bf16[128,384]{1,0:T(8,128)(2,1)} %get-tuple-element.54), channel_id=1, source_target_pairs={{0,1},{1,0},{2,3},{3,2},{4,5},{5,4},{6,7},{7,6},{8,9},{9,8},{10,11... | collective-permute-start | bytes 294920 | tf_op jit(solution)/shard_map/ppermute | solution.py:34
  133.8 2.8 %shard_map.99 = bf16[1536,384]{1,0:T(8,128)(2,1)} custom-call(bf16[128,1536]{1,0:T(8,128)(2,1)} %bitcast.30, bf16[128,1536]{1,0:T(8,128)(2,1)} %copy-done.5, bf16[128,384]{1,0:T(8,128)(2,1)} %get-tuple-element.53.keep_ref, bf16[128,384]{1,0:T(8,128)(2,1)} %copy-done.6), custom_call_target="tpu_custom_call" | custom-call | tf_op jit(solution)/shard_map/pallas_call | solution.py:207
  136.6 3.9 %all-to-all-start.5 = ((bf16[4,384,384]{2,1,0:T(8,128)(2,1)}), bf16[4,384,384]{2,1,0:T(8,128)(2,1)S(1)}, u32[]{:S(2)}, u32[]{:S(2)}) async-start(bf16[4,384,384]{2,1,0:T(8,128)(2,1)} %bitcast.27), calls=%async_computation.6 | async-start | bytes 2359296 | tf_op jit(solution)/shard_map/all_to_all | solution.py:223
  140.8 3.0 %collective-permute-start.3 = (bf16[64,384]{1,0:T(8,128)(2,1)S(1)}, bf16[64,384]{1,0:T(8,128)(2,1)S(1)}, u32[]{:S(2)}, u32[]{:S(2)}) collective-permute-start(bf16[64,384]{1,0:T(8,128)(2,1)S(1)} %get-tuple-element.61), channel_id=1, source_target_pairs={{0,2},{2,0},{4,6},{6,4},{1,3},{3,1},{5,7},{7,5},{8,10},{10,8},{12,... | collective-permute-start | bytes 147464 | tf_op jit(solution)/shard_map/ppermute | solution.py:41
  144.7 3.3 %shard_map.98 = bf16[128,1536]{1,0:T(8,128)(2,1)} custom-call(bf16[128,768]{1,0:T(8,128)(2,1)} %get-tuple-element.51.both_ref, bf16[1536,512]{1,0:T(8,128)(2,1)} %w_query_ref.3, bf16[1536,256]{1,0:T(8,128)(2,1)} %w_keyval_ref.1), custom_call_target="tpu_custom_call" | custom-call | flops 300000000 | bytes 6000000 | tf_op jit(solution)/shard_map/pallas_call | solution.py:207
  148.4 8.1 %all-to-all-done.5 = bf16[4,384,384]{2,1,0:T(8,128)(2,1)S(1)} async-done(((bf16[4,384,384]{2,1,0:T(8,128)(2,1)}), bf16[4,384,384]{2,1,0:T(8,128)(2,1)S(1)}, u32[]{:S(2)}, u32[]{:S(2)}) %all-to-all-start.5) | async-done | bytes 1179680 | tf_op jit(solution)/shard_map/all_to_all | solution.py:223
  156.9 17.0 %all_to_all.37 = bf16[16,32,384]{2,1,0:T(8,128)(2,1)S(1)} all-to-all(bf16[16,32,384]{2,1,0:T(8,128)(2,1)S(1)} %pad_maximum_fusion), channel_id=1, replica_groups=mesh['x'=4,'z'=8,'yl'=2,'yh'=2,'core'=2] {'z','yl'}, dimensions={0} | all-to-all | bytes 786432 | tf_op jit(solution)/shard_map/all_to_all | solution.py:223
  174.0 2.6 %collective-permute-start.6 = (f32[32,384]{1,0:T(8,128)S(1)}, f32[32,384]{1,0:T(8,128)S(1)}, u32[]{:S(2)}, u32[]{:S(2)}) collective-permute-start(f32[32,384]{1,0:T(8,128)S(1)} %convert_reduce_fusion), channel_id=1, source_target_pairs={{0,2},{2,0},{1,3},{3,1},{4,6},{6,4},{5,7},{7,5},{8,10},{10,8},{9,1... | collective-permute-start | bytes 147464 | tf_op jit(solution)/shard_map/ppermute | solution.py:34
  176.6 1.9 %collective-permute-done.6 = f32[32,384]{1,0:T(8,128)S(1)} collective-permute-done((f32[32,384]{1,0:T(8,128)S(1)}, f32[32,384]{1,0:T(8,128)S(1)}, u32[]{:S(2)}, u32[]{:S(2)}) %collective-permute-start.6) | collective-permute-done | bytes 49184 | tf_op jit(solution)/shard_map/ppermute | solution.py:34
  178.6 4.7 %collective-permute-start.7 = (f32[40,384]{1,0:T(8,128)S(1)}, f32[40,384]{1,0:T(8,128)S(1)}, u32[]{:S(2)}, u32[]{:S(2)}) collective-permute-start(f32[40,384]{1,0:T(8,128)S(1)} %pad_maximum_fusion.1), channel_id=1, source_target_pairs={{0,1},{1,0},{2,3},{3,2},{4,5},{5,4},{6,7},{7,6},{8,9},{9,8},{10,11... | collective-permute-start | bytes 184328 | tf_op jit(solution)/shard_map/ppermute | solution.py:34
  (56 shorter events, 12.8 us)
Async XLA Ops:
  11.5 6.0 %copy-start.1 = (bf16[1,128,1536]{2,1,0:T(8,128)(2,1)S(1)}, bf16[1,128,1536]{2,1,0:T(8,128)(2,1)}, u32[]{:S(2)}) copy-start(bf16[1,128,1536]{2,1,0:T(8,128)(2,1)} %param.5) | copy-start | bytes 1179652
  11.5 7.8 %copy-start.2 = (bf16[1536,256]{1,0:T(8,128)(2,1)S(1)}, bf16[1536,256]{1,0:T(8,128)(2,1)}, u32[]{:S(2)}) copy-start(bf16[1536,256]{1,0:T(8,128)(2,1)} %w_keyval_ref.1) | copy-start | bytes 2359300
  11.6 35.6 %all-to-all-start = ((bf16[8,128,1024]{2,1,0:T(8,128)(2,1)}), bf16[8,128,1024]{2,1,0:T(8,128)(2,1)}, u32[]{:S(2)}, u32[]{:S(2)}) async-start(bf16[8,128,1024]{2,1,0:T(8,128)(2,1)} %shard_map.92), calls=%async_computation | async-start | bytes 4194304 | tf_op jit(solution)/shard_map/all_to_all | solution.py:223
  17.5 28.8 %collective-permute-start = (bf16[128,1536]{1,0:T(8,128)(2,1)S(1)}, bf16[128,1536]{1,0:T(8,128)(2,1)S(1)}, u32[]{:S(2)}, u32[]{:S(2)}) collective-permute-start(bf16[128,1536]{1,0:T(8,128)(2,1)S(1)} %bitcast.31), channel_id=1, source_target_pairs={{0,1},{1,0},{2,3},{3,2},{4,5},{5,4},{6,7},{7,6},{8,9},{9,8},{10,11... | collective-permute-start | bytes 1179656 | tf_op jit(solution)/shard_map/ppermute | solution.py:34
  46.3 10.7 %copy-start.5 = (bf16[128,1536]{1,0:T(8,128)(2,1)}, bf16[128,1536]{1,0:T(8,128)(2,1)S(1)}, u32[]{:S(2)}) copy-start(bf16[128,1536]{1,0:T(8,128)(2,1)S(1)} %collective-permute-done.other_ref) | copy-start | bytes 1179652
  66.9 17.4 %all-to-all-start.2 = ((bf16[8,128,512]{2,1,0:T(8,128)(2,1)}), bf16[8,128,512]{2,1,0:T(8,128)(2,1)S(1)}, u32[]{:S(2)}, u32[]{:S(2)}) async-start(bf16[8,128,512]{2,1,0:T(8,128)(2,1)} %get-tuple-element.40), calls=%async_computation.2 | async-start | bytes 2097152 | tf_op jit(solution)/shard_map/all_to_all | solution.py:223
  70.5 55.0 %reduce-scatter.2.cloned.1.call-start = ((), (), s32[]{:S(2)}) async-start(), calls=%async_computation.8 | async-start | bytes 1179648 | tf_op jit(solution)/shard_map/reduce_scatter | solution.py:285
  84.3 1.0 copy-start
  88.5 9.0 %collective-permute-start.1 = (bf16[512,768]{1,0:T(8,128)(2,1)}, bf16[512,768]{1,0:T(8,128)(2,1)S(1)}, u32[]{:S(2)}, u32[]{:S(2)}) collective-permute-start(bf16[512,768]{1,0:T(8,128)(2,1)} %get-tuple-element.43), channel_id=1, source_target_pairs={{0,1},{1,0},{2,3},{3,2},{4,5},{5,4},{6,7},{7,6},{8,9},{9,8},{10,11... | collective-permute-start | bytes 2359304 | tf_op jit(solution)/shard_map/ppermute | solution.py:34
  94.7 2.8 %copy-start.4 = (bf16[512,768]{1,0:T(8,128)(2,1)S(1)}, bf16[512,768]{1,0:T(8,128)(2,1)}, u32[]{:S(2)}) copy-start(bf16[512,768]{1,0:T(8,128)(2,1)} %get-tuple-element.42) | copy-start | bytes 2359300
  97.5 1.5 copy-start.3
  119.3 17.3 %all-to-all-start.4 = ((bf16[4,128,768]{2,1,0:T(8,128)(2,1)}), bf16[4,128,768]{2,1,0:T(8,128)(2,1)S(1)}, u32[]{:S(2)}, u32[]{:S(2)}) async-start(bf16[4,128,768]{2,1,0:T(8,128)(2,1)} %bitcast.5), calls=%async_computation.5 | async-start | bytes 1572864 | tf_op jit(solution)/shard_map/all_to_all | solution.py:223
  127.6 5.5 %collective-permute-start.2 = (bf16[128,384]{1,0:T(8,128)(2,1)}, bf16[128,384]{1,0:T(8,128)(2,1)S(1)}, u32[]{:S(2)}, u32[]{:S(2)}) collective-permute-start(bf16[128,384]{1,0:T(8,128)(2,1)} %get-tuple-element.54), channel_id=1, source_target_pairs={{0,1},{1,0},{2,3},{3,2},{4,5},{5,4},{6,7},{7,6},{8,9},{9,8},{10,11... | collective-permute-start | bytes 294920 | tf_op jit(solution)/shard_map/ppermute | solution.py:34
  133.2 0.6 copy-start.6
  136.6 19.9 %all-to-all-start.5 = ((bf16[4,384,384]{2,1,0:T(8,128)(2,1)}), bf16[4,384,384]{2,1,0:T(8,128)(2,1)S(1)}, u32[]{:S(2)}, u32[]{:S(2)}) async-start(bf16[4,384,384]{2,1,0:T(8,128)(2,1)} %bitcast.27), calls=%async_computation.6 | async-start | bytes 2359296 | tf_op jit(solution)/shard_map/all_to_all | solution.py:223
  140.8 7.2 %collective-permute-start.3 = (bf16[64,384]{1,0:T(8,128)(2,1)S(1)}, bf16[64,384]{1,0:T(8,128)(2,1)S(1)}, u32[]{:S(2)}, u32[]{:S(2)}) collective-permute-start(bf16[64,384]{1,0:T(8,128)(2,1)S(1)} %get-tuple-element.61), channel_id=1, source_target_pairs={{0,2},{2,0},{4,6},{6,4},{1,3},{3,1},{5,7},{7,5},{8,10},{10,8},{12,... | collective-permute-start | bytes 147464 | tf_op jit(solution)/shard_map/ppermute | solution.py:41
  143.7 4.3 %collective-permute-start.4 = (bf16[64,384]{1,0:T(8,128)(2,1)S(1)}, bf16[64,384]{1,0:T(8,128)(2,1)S(1)}, u32[]{:S(2)}, u32[]{:S(2)}) collective-permute-start(bf16[64,384]{1,0:T(8,128)(2,1)S(1)} %get-tuple-element.63), channel_id=1, source_target_pairs={{0,4},{2,6},{4,0},{6,2},{1,5},{3,7},{5,1},{7,3},{8,12},{10,14},{12... | collective-permute-start | bytes 147464 | tf_op jit(solution)/shard_map/ppermute | solution.py:41
  143.9 4.4 %collective-permute-start.5 = (bf16[64,384]{1,0:T(8,128)(2,1)S(1)}, bf16[64,384]{1,0:T(8,128)(2,1)S(1)}, u32[]{:S(2)}, u32[]{:S(2)}) collective-permute-start(bf16[64,384]{1,0:T(8,128)(2,1)S(1)} %get-tuple-element.62), channel_id=1, source_target_pairs={{0,6},{2,4},{4,2},{6,0},{1,7},{3,5},{5,3},{7,1},{8,14},{10,12},{12... | collective-permute-start | bytes 147464 | tf_op jit(solution)/shard_map/ppermute | solution.py:41
  174.0 4.5 %collective-permute-start.6 = (f32[32,384]{1,0:T(8,128)S(1)}, f32[32,384]{1,0:T(8,128)S(1)}, u32[]{:S(2)}, u32[]{:S(2)}) collective-permute-start(f32[32,384]{1,0:T(8,128)S(1)} %convert_reduce_fusion), channel_id=1, source_target_pairs={{0,2},{2,0},{1,3},{3,1},{4,6},{6,4},{5,7},{7,5},{8,10},{10,8},{9,1... | collective-permute-start | bytes 147464 | tf_op jit(solution)/shard_map/ppermute | solution.py:34
  178.6 5.6 %collective-permute-start.7 = (f32[40,384]{1,0:T(8,128)S(1)}, f32[40,384]{1,0:T(8,128)S(1)}, u32[]{:S(2)}, u32[]{:S(2)}) collective-permute-start(f32[40,384]{1,0:T(8,128)S(1)} %pad_maximum_fusion.1), channel_id=1, source_target_pairs={{0,1},{1,0},{2,3},{3,2},{4,5},{5,4},{6,7},{7,6},{8,9},{9,8},{10,11... | collective-permute-start | bytes 184328 | tf_op jit(solution)/shard_map/ppermute | solution.py:34
Sparse Core Ops, SparseCore 0:
  84.4 41.0 reduce-scatter.1
